TPU v7x, 32 devices: a whole 2x2x4 slice. The times are simulated.
32 devices in a mesh: dp: 8 (over z, x), tensor: 4 (over y, core).
Axes of the slice: x: 2, y: 2, z: 4, core: 2. Of those that a mesh axis runs over, the one named last changes fastest.
Arguments:
- tokens: bfloat16 [1, 4096, 1280], P(None, 'dp'), may hold values from -6 to 6
- cotangent: bfloat16 [1, 4096, 1280], P(None, 'dp'), may hold values from -6 to 6
- norm1_gain: float32 [1280], replicated, may hold values from 0.5 to 1.5
- norm1_shift: float32 [1280], replicated, may hold values from -3 to 3
- qkv_weight: bfloat16 [1280, 3, 1280], P(None, None, 'tensor'), may hold values from -0.15625 to 0.15625
- qv_bias: float32 [2, 1280], P(None, 'tensor'), may hold values from -0.24 to 0.24
- proj_weight: bfloat16 [1280, 1280], P('tensor'), may hold values from -4 to 4
- proj_bias: float32 [1280], replicated, may hold values from -3 to 3
- table_rows: bfloat16 [127, 80], replicated, may hold values from -0.59765625 to 0.59765625
- table_cols: bfloat16 [127, 80], replicated, may hold values from -0.59765625 to 0.59765625
- norm2_gain: float32 [1280], replicated, may hold values from 0.5 to 1.5
- norm2_shift: float32 [1280], replicated, may hold values from -3 to 3
- fc1_weight: bfloat16 [1280, 5120], P(None, 'tensor'), may hold values from -0.15625 to 0.15625
- fc1_bias: float32 [5120], P('tensor'), may hold values from -3 to 3
- fc2_weight: bfloat16 [5120, 1280], P('tensor'), may hold values from -0.125 to 0.125
- fc2_bias: float32 [1280], replicated, may hold values from -3 to 3
- threshold: float32 [1], replicated, may hold values from 0.5 to 3
Outputs:
- output: bfloat16 [1, 4096, 1280], P(None, 'dp')
- grad_tokens: bfloat16 [1, 4096, 1280], P(None, 'dp')
- grad_norm1_gain: float32 [1280], replicated
- grad_norm1_shift: float32 [1280], replicated
- grad_qkv: float32 [1280, 3, 1280], P('dp', None, 'tensor')
- grad_qv_bias: float32 [2, 1280], P(None, 'tensor')
- grad_proj: float32 [1280, 1280], P('tensor', 'dp')
- grad_proj_bias: float32 [1280], replicated
- grad_table_rows: float32 [127, 80], replicated
- grad_table_cols: float32 [127, 80], replicated
- grad_norm2_gain: float32 [1280], replicated
- grad_norm2_shift: float32 [1280], replicated
- grad_fc1: float32 [1280, 5120], P('dp', 'tensor')
- grad_fc1_bias: float32 [5120], P('tensor')
- grad_fc2: float32 [5120, 1280], P('tensor', 'dp')
- grad_fc2_bias: float32 [1280], replicated
- clipped_qk: bfloat16 [1280, 2, 1280], P(None, None, 'tensor')
- clipped_q_bias: float32 [1280], P('tensor')
- head_peaks: float32 [16], P('tensor')
- clip_factors: float32 [16], P('tensor')
All inputs are finite; a program needn't handle non-finite values.
Results may differ from a plain program's by a relative error of at most 0.02.
Values may be sent and summed in bfloat16 or wider, within the bound.
A program may use at most 192 MiB of HBM per device.

v0:
```python
import jax
import jax.numpy as jnp
from jax import lax
from jax.sharding import PartitionSpec as P

HEAD = 80
SIDE = 64


HIGHEST = lax.Precision.HIGHEST
EPSILON = 1e-06


def norm_forward(values, norm_gain, norm_shift):
    center = values - jnp.mean(values, axis=-1, keepdims=True)
    variance = jnp.mean(center * center, axis=-1, keepdims=True)
    inverse = lax.rsqrt(variance + EPSILON)
    scaled = center * inverse
    return (scaled * norm_gain + norm_shift, scaled, inverse)


def norm_backward(upstream, scaled, inverse, norm_gain):
    weighted = upstream * norm_gain
    centered_grad = weighted - jnp.mean(weighted, axis=-1, keepdims=True)
    centered_grad = centered_grad - scaled * jnp.mean(weighted * scaled, axis=-1, keepdims=True)
    return centered_grad * inverse


def gain_terms(upstream, scaled):
    return (jnp.sum(upstream * scaled, axis=0), jnp.sum(upstream, axis=0))


def rows_of(values, share_base, share_rows):
    return lax.dynamic_slice_in_dim(values, share_base, share_rows, 0)


def exact_gelu(values):
    return jax.nn.gelu(values, approximate=False)


def full_sum(values):
    return lax.psum(values.astype(jnp.bfloat16), "tensor").astype(jnp.float32)


def selections(row_count, row_base):
    image_rows = row_count // SIDE
    rel_index = jnp.arange(2 * SIDE - 1)[None, :, None]
    key_index = jnp.arange(SIDE)[None, None, :]
    query_rows = (jnp.arange(image_rows) + row_base)[:, None, None]
    query_cols = jnp.arange(SIDE)[:, None, None]
    pick_rows = (rel_index == query_rows - key_index + SIDE - 1).astype(jnp.float32)
    pick_cols = (rel_index == query_cols - key_index + SIDE - 1).astype(jnp.float32)
    local_keys = (jnp.arange(image_rows) + row_base)[None, None, :]
    pick_key_rows = (rel_index == query_cols - local_keys + SIDE - 1).astype(jnp.float32)
    return (pick_rows, pick_cols, pick_key_rows)


def head_scores(query_head, key_head, table_rows, table_cols, pick_rows, pick_cols):
    images = query_head.shape[0]
    row_count = query_head.shape[1]
    image_rows = row_count // SIDE
    logits = jnp.einsum(
        "iqc,ikc->iqk", query_head, key_head, preferred_element_type=jnp.float32
    ) * HEAD ** (-0.5)
    along_rows = jnp.einsum(
        "iqc,jc->iqj", query_head, table_rows, preferred_element_type=jnp.float32
    )
    along_cols = jnp.einsum(
        "iqc,jc->iqj", query_head, table_cols, preferred_element_type=jnp.float32
    )
    bias_rows = jnp.einsum(
        "irwj,rjk->irwk",
        along_rows.reshape(images, image_rows, SIDE, -1),
        pick_rows,
        precision=HIGHEST,
    )
    bias_cols = jnp.einsum(
        "irwj,wjk->irwk",
        along_cols.reshape(images, image_rows, SIDE, -1),
        pick_cols,
        precision=HIGHEST,
    )
    scores = (
        logits.reshape(images, image_rows, SIDE, SIDE, SIDE)
        + bias_rows[..., :, None]
        + bias_cols[..., None, :]
    )
    return (logits, scores.reshape(images, row_count, -1))


def on_device(
    tokens,
    cotangent,
    norm1_gain,
    norm1_shift,
    qkv_weight,
    qv_bias,
    proj_weight,
    proj_bias,
    table_rows,
    table_cols,
    norm2_gain,
    norm2_shift,
    fc1_weight,
    fc1_bias,
    fc2_weight,
    fc2_bias,
    threshold,
):
    images, row_count, model_width = tokens.shape
    token_count = images * row_count
    local_width = qkv_weight.shape[2]
    local_heads = local_width // HEAD
    image_rows = row_count // SIDE
    score_scale = HEAD ** (-0.5)
    groups = lax.axis_size("tensor")
    share_rows = token_count // groups
    share_base = lax.axis_index("tensor") * share_rows
    pick_rows, pick_cols, pick_key_rows = selections(row_count, lax.axis_index("dp") * image_rows)
    residual_in = tokens.reshape(token_count, model_width).astype(jnp.float32)
    normed1, scaled1, inverse1 = norm_forward(residual_in, norm1_gain, norm1_shift)
    normed1_low = normed1.astype(jnp.bfloat16)
    triple = jnp.einsum("nd,dtc->ntc", normed1_low, qkv_weight, preferred_element_type=jnp.float32)
    queries = (
        (triple[:, 0] + qv_bias[0]).astype(jnp.bfloat16).reshape(images, row_count, local_width)
    )
    key_rows = triple[:, 1].astype(jnp.bfloat16).reshape(images, row_count, local_width)
    value_rows = (
        (triple[:, 2] + qv_bias[1]).astype(jnp.bfloat16).reshape(images, row_count, local_width)
    )
    key_all, value_all = (
        lax.all_gather(key_rows, "dp", axis=1, tiled=True),
        lax.all_gather(value_rows, "dp", axis=1, tiled=True),
    )

    def head_slice(source, head_idx):
        return lax.dynamic_slice_in_dim(source, head_idx * HEAD, HEAD, 2)

    def forward_head(head_idx):
        logits, scores = head_scores(
            head_slice(queries, head_idx),
            head_slice(key_all, head_idx),
            table_rows,
            table_cols,
            pick_rows,
            pick_cols,
        )
        log_total = jax.nn.logsumexp(scores, axis=-1)
        weights = jnp.exp(scores - log_total[..., None]).astype(jnp.bfloat16)
        attended = jnp.einsum(
            "iqk,ikc->iqc",
            weights,
            head_slice(value_all, head_idx),
            preferred_element_type=jnp.float32,
        )
        return (attended.astype(jnp.bfloat16), log_total, jnp.max(logits))

    attended, log_totals, local_peaks = lax.map(forward_head, jnp.arange(local_heads))
    attended_flat = attended.transpose(1, 2, 0, 3).reshape(token_count, local_width)
    branch_part = jnp.dot(attended_flat, proj_weight, preferred_element_type=jnp.float32)
    middle_rows = residual_in + full_sum(branch_part) + proj_bias
    normed2, scaled2, inverse2 = norm_forward(middle_rows, norm2_gain, norm2_shift)
    normed2_low = normed2.astype(jnp.bfloat16)
    up_value = jnp.dot(normed2_low, fc1_weight, preferred_element_type=jnp.float32) + fc1_bias
    activated, gelu_pull = jax.vjp(exact_gelu, up_value)
    activated_low = activated.astype(jnp.bfloat16)
    mlp_part = jnp.dot(activated_low, fc2_weight, preferred_element_type=jnp.float32)
    output = (middle_rows + (full_sum(mlp_part) + fc2_bias)).astype(jnp.bfloat16)
    grad_out = cotangent.reshape(token_count, model_width)
    grad_out_f = grad_out.astype(jnp.float32)
    grad_fc2 = jnp.einsum("nf,nd->fd", activated_low, grad_out, preferred_element_type=jnp.float32)
    grad_fc2_bias = jnp.sum(grad_out_f, axis=0)
    grad_activated = jnp.einsum(
        "nd,fd->nf", grad_out, fc2_weight, preferred_element_type=jnp.float32
    )
    grad_up = gelu_pull(grad_activated)[0].astype(jnp.bfloat16)
    grad_fc1 = jnp.einsum("nd,nf->df", normed2_low, grad_up, preferred_element_type=jnp.float32)
    grad_fc1_bias = jnp.sum(grad_up.astype(jnp.float32), axis=0)
    normed2_part = jnp.einsum("nf,df->nd", grad_up, fc1_weight, preferred_element_type=jnp.float32)
    grad_normed2 = full_sum(normed2_part)
    grad_norm2_gain, grad_norm2_shift = gain_terms(
        rows_of(grad_normed2, share_base, share_rows), rows_of(scaled2, share_base, share_rows)
    )
    grad_middle = grad_out_f + norm_backward(grad_normed2, scaled2, inverse2, norm2_gain)
    grad_branch = grad_middle.astype(jnp.bfloat16)
    grad_proj = jnp.einsum(
        "nc,nd->cd", attended_flat, grad_branch, preferred_element_type=jnp.float32
    )
    grad_proj_bias = jnp.sum(grad_branch.astype(jnp.float32), axis=0)
    grad_attended = jnp.einsum(
        "nd,cd->nc", grad_branch, proj_weight, preferred_element_type=jnp.float32
    ).astype(jnp.bfloat16)
    grad_heads = grad_attended.reshape(images, row_count, local_heads, HEAD).transpose(2, 0, 1, 3)
    rows_table_f = table_rows.astype(jnp.float32)
    cols_table_f = table_cols.astype(jnp.float32)

    def make_backward():

        def backward_head(operands):
            head_idx, grad_head, log_total = operands
            query_head = head_slice(queries, head_idx)
            key_head = head_slice(key_all, head_idx)
            value_head = head_slice(value_all, head_idx)
            logits, scores = head_scores(
                query_head, key_head, table_rows, table_cols, pick_rows, pick_cols
            )
            probs = jnp.exp(scores - log_total[..., None])
            grad_probs = jnp.einsum(
                "iqc,ikc->iqk", grad_head, value_head, preferred_element_type=jnp.float32
            )
            row_dots = jnp.sum(probs * grad_probs, axis=-1, keepdims=True)
            grad_scores = (probs * (grad_probs - row_dots)).astype(jnp.bfloat16)
            grad_query = (
                jnp.einsum(
                    "iqk,ikc->iqc", grad_scores, key_head, preferred_element_type=jnp.float32
                )
                * score_scale
            )
            grid = grad_scores.astype(jnp.float32).reshape(images, image_rows, SIDE, SIDE, SIDE)
            grad_rows = jnp.einsum(
                "irwk,rjk->irwj", jnp.sum(grid, axis=4), pick_rows, precision=HIGHEST
            ).reshape(images, row_count, -1)
            grad_cols = jnp.einsum(
                "irwk,wjk->irwj", jnp.sum(grid, axis=3), pick_cols, precision=HIGHEST
            ).reshape(images, row_count, -1)
            grad_query = grad_query + jnp.einsum(
                "iqj,jc->iqc", grad_rows, rows_table_f, precision=HIGHEST
            )
            grad_query = grad_query + jnp.einsum(
                "iqj,jc->iqc", grad_cols, cols_table_f, precision=HIGHEST
            )
            query_f = query_head.astype(jnp.float32)
            grad_table_rows = jnp.einsum("iqj,iqc->jc", grad_rows, query_f, precision=HIGHEST)
            grad_table_cols = jnp.einsum("iqj,iqc->jc", grad_cols, query_f, precision=HIGHEST)
            grad_value = jnp.einsum(
                "iqk,iqc->ikc",
                probs.astype(jnp.bfloat16),
                grad_head,
                preferred_element_type=jnp.float32,
            )
            grad_key = (
                jnp.einsum(
                    "iqk,iqc->ikc", grad_scores, query_head, preferred_element_type=jnp.float32
                )
                * score_scale
            )
            return (grad_query, grad_key, grad_value, grad_table_rows, grad_table_cols)

        return backward_head

    grad_query, grad_key, grad_value, head_table_rows, head_table_cols = lax.map(
        make_backward(), (jnp.arange(local_heads), grad_heads, log_totals)
    )
    grad_key, grad_value = (
        lax.psum_scatter(
            grad_key.astype(jnp.bfloat16), "dp", scatter_dimension=2, tiled=True
        ).astype(jnp.float32),
        lax.psum_scatter(
            grad_value.astype(jnp.bfloat16), "dp", scatter_dimension=2, tiled=True
        ).astype(jnp.float32),
    )
    grad_triple = jnp.stack([grad_query, grad_key, grad_value]).astype(jnp.bfloat16)
    grad_triple = grad_triple.transpose(2, 3, 0, 1, 4).reshape(token_count, 3, local_width)
    grad_qkv = jnp.einsum(
        "nd,ntc->dtc", normed1_low, grad_triple, preferred_element_type=jnp.float32
    )
    grad_qv_bias = jnp.sum(grad_triple[:, 0::2].astype(jnp.float32), axis=0)
    normed1_part = jnp.einsum(
        "ntc,dtc->nd", grad_triple, qkv_weight, preferred_element_type=jnp.float32
    )
    grad_normed1 = full_sum(normed1_part)
    grad_norm1_gain, grad_norm1_shift = gain_terms(
        rows_of(grad_normed1, share_base, share_rows), rows_of(scaled1, share_base, share_rows)
    )
    from_norm1 = norm_backward(grad_normed1, scaled1, inverse1, norm1_gain)
    grad_tokens = (grad_middle + from_norm1).astype(jnp.bfloat16)
    grad_tokens = grad_tokens.reshape(images, row_count, model_width)
    grad_qkv, grad_proj, grad_fc1, grad_fc2 = (
        lax.psum_scatter(
            grad_qkv.astype(jnp.bfloat16), "dp", scatter_dimension=0, tiled=True
        ).astype(jnp.float32),
        lax.psum_scatter(
            grad_proj.astype(jnp.bfloat16), "dp", scatter_dimension=1, tiled=True
        ).astype(jnp.float32),
        lax.psum_scatter(
            grad_fc1.astype(jnp.bfloat16), "dp", scatter_dimension=0, tiled=True
        ).astype(jnp.float32),
        lax.psum_scatter(
            grad_fc2.astype(jnp.bfloat16), "dp", scatter_dimension=1, tiled=True
        ).astype(jnp.float32),
    )
    grad_proj_bias, grad_fc2_bias, grad_qv_bias, grad_fc1_bias = lax.psum(
        (grad_proj_bias, grad_fc2_bias, grad_qv_bias, grad_fc1_bias), "dp"
    )
    rows_term = jnp.sum(head_table_rows, axis=0)
    cols_term = jnp.sum(head_table_cols, axis=0)
    head_peaks = lax.pmax(local_peaks, "dp")
    (
        grad_table_rows,
        grad_table_cols,
        grad_norm1_gain,
        grad_norm1_shift,
        grad_norm2_gain,
        grad_norm2_shift,
    ) = lax.psum(
        (
            rows_term,
            cols_term,
            grad_norm1_gain,
            grad_norm1_shift,
            grad_norm2_gain,
            grad_norm2_shift,
        ),
        ("dp", "tensor"),
    )
    limit = threshold[0]
    clip_factors = jnp.sqrt(limit / jnp.maximum(head_peaks, limit))
    spread_factors = jnp.repeat(clip_factors, HEAD)
    clipped_qk = (qkv_weight[:, :2, :].astype(jnp.float32) * spread_factors).astype(jnp.bfloat16)
    clipped_q_bias = qv_bias[0] * spread_factors
    output = output.reshape(images, row_count, model_width)
    return (
        output,
        grad_tokens,
        grad_norm1_gain,
        grad_norm1_shift,
        grad_qkv,
        grad_qv_bias,
        grad_proj,
        grad_proj_bias,
        grad_table_rows,
        grad_table_cols,
        grad_norm2_gain,
        grad_norm2_shift,
        grad_fc1,
        grad_fc1_bias,
        grad_fc2,
        grad_fc2_bias,
        clipped_qk,
        clipped_q_bias,
        head_peaks,
        clip_factors,
    )


def solution(mesh):
    in_specs = (
        P(None, "dp", None),
        P(None, "dp", None),
        P(),
        P(),
        P(None, None, "tensor"),
        P(None, "tensor"),
        P("tensor", None),
        P(),
        P(),
        P(),
        P(),
        P(),
        P(None, "tensor"),
        P("tensor"),
        P("tensor", None),
        P(),
        P(),
    )
    out_specs = (
        P(None, "dp", None),
        P(None, "dp", None),
        P(),
        P(),
        P("dp", None, "tensor"),
        P(None, "tensor"),
        P("tensor", "dp"),
        P(),
        P(),
        P(),
        P(),
        P(),
        P("dp", "tensor"),
        P("tensor"),
        P("tensor", "dp"),
        P(),
        P(None, None, "tensor"),
        P("tensor"),
        P("tensor"),
        P("tensor"),
    )
    return jax.shard_map(
        on_device, mesh=mesh, in_specs=in_specs, out_specs=out_specs, check_vma=False
    )
```

profile of v0, /device:TPU:0, one launch (start us, length us, event | category | flops | bytes accessed | tf_op | source)
XLA Modules:
  0.0 1685.9 jit_solution(12993588428814126015)
XLA Ops:
  22.0 54.1 %all-gather.6.cloned.1.call-done = bf16[4096,1,320]{0,2,1:T(8,128)(2,1)} async-done(((bf16[512,1,320]{0,2,1:T(8,128)(2,1)}), bf16[4096,1,320]{0,2,1:T(8,128)(2,1)}) %all-gather.6.cloned.1.call-update) | async-done | bytes 2621456 | tf_op jit(solution)/shard_map/all_gather | solution.py:132
  80.5 53.2 %all-gather.4.cloned.1.call-done = bf16[1,4096,320]{1,2,0:T(8,128)(2,1)} async-done(((bf16[1,512,320]{1,2,0:T(8,128)(2,1)}), bf16[1,4096,320]{1,2,0:T(8,128)(2,1)}) %all-gather.4.cloned.1.call-update) | async-done | bytes 2621456 | tf_op jit(solution)/shard_map/all_gather | solution.py:133
  138.3 310.4 %while.35 = (s32[]{:T(128)}, bf16[4,1,512,80]{2,3,1,0:T(8,128)(2,1)}, f32[4,1,512]{2,1,0:T(1,128)S(1)}, f32[4]{0:T(128)}, s32[4]{0:T(128)S(1)}, /*index=5*/bf16[...) while((s32[]{:T(128)}, ...), condition=%wide.region_6.7_spmd.clone, body=%wide.region_2.6_spmd.clone.sunk | while | flops 811862528 | bytes 130380912 | solution.py:158
  154.5 14.8 add.482
  231.9 14.8 add.482
  309.3 14.8 add.482
  386.8 14.8 add.482
  451.9 37.2 %all-reduce.8.cloned.1.call-done = bf16[512,1280]{1,0:T(8,128)(2,1)} async-done(((bf16[512,1280]{1,0:T(8,128)(2,1)}), bf16[512,1280]{1,0:T(8,128)(2,1)}) %all-reduce.8.cloned.1.call-update) | async-done | bytes 1310736 | tf_op jit(solution)/shard_map/psum | solution.py:42
  511.7 35.9 %all-reduce.10.cloned.1.call-done = bf16[512,1280]{1,0:T(8,128)(2,1)} async-done(((bf16[512,1280]{1,0:T(8,128)(2,1)}), bf16[512,1280]{1,0:T(8,128)(2,1)}) %all-reduce.10.cloned.1.call-update) | async-done | bytes 1310736 | tf_op jit(solution)/shard_map/psum | solution.py:42
  556.9 476.7 %while.36 = (s32[]{:T(128)}, bf16[4,1,512,80]{2,3,1,0:T(8,128)(2,1)}, bf16[4,1,4096,80]{2,3,1,0:T(8,128)(2,1)}, bf16[4,1,4096,80]{2,3,1,0:T(8,128)(2,1)}, f32[4,...) while((s32[]{:T(128)}, ...), condition=%wide.region_18.19_spmd.clone.clone, body=%wide.region_14.18_spmd.clone.clone.sunk | while | flops 2175866368 | bytes 204020320 | solution.py:251
  602.4 14.7 add.492
  721.5 14.7 add.492
  840.6 14.7 add.492
  959.7 14.7 add.492
  1055.5 49.1 %reduce-scatter.7.cloned.1.call-done = bf16[4,1,512,80]{2,3,0,1:T(8,128)(2,1)} async-done(((bf16[4,1,4096,80]{2,3,0,1:T(8,128)(2,1)}), bf16[4,1,512,80]{2,3,0,1:T(8,128)(2,1)}) %reduce-scatter.7.cloned.1.call-update) | async-done | bytes 327696 | tf_op jit(solution)/shard_map/reduce_scatter | solution.py:255
  1104.6 73.3 %reduce-scatter.9.cloned.1.call-done = bf16[4,1,512,80]{2,3,1,0:T(8,128)(2,1)} async-done(((bf16[4,1,4096,80]{2,3,1,0:T(8,128)(2,1)}), bf16[4,1,512,80]{2,3,1,0:T(8,128)(2,1)}) %reduce-scatter.9.cloned.1.call-update) | async-done | bytes 327696 | tf_op jit(solution)/shard_map/reduce_scatter | solution.py:258
  1188.7 19.4 %pmax.7 = f32[4]{0:T(128)S(1)} all-reduce(f32[4]{0:T(128)S(1)} %copy-done.62), channel_id=1, replica_groups=mesh['dp'=8,'tensor'=4] {'dp'}, use_global_device_ids=true, to_apply=%region_48.49 | all-reduce | flops 4 | bytes 32 | tf_op jit(solution)/shard_map/pmax | solution.py:297
  1215.1 28.4 %reduce-scatter.13.cloned.1.call-done = bf16[320,160]{0,1:T(8,128)(2,1)} async-done(((bf16[320,1280]{0,1:T(8,128)(2,1)}), bf16[320,160]{0,1:T(8,128)(2,1)}) %reduce-scatter.13.cloned.1.call-update) | async-done | bytes 102416 | tf_op jit(solution)/shard_map/reduce_scatter | solution.py:282
  1246.4 37.2 %all-reduce.1 = (f32[2,320]{1,0:T(2,128)}, f32[1280]{0:T(1024)}, f32[1280]{0:T(1024)}, f32[1280]{0:T(1024)}) all-reduce(f32[2,320]{1,0:T(2,128)S(1)} %convert_reduce_fusion.4, f32[1280]{0:T(1024)S(1)} %copy-done.40, f32[1280]{0:T(1024)S(1)} %copy-done.48, f32[1280]{0:T(1024)S(1)} %copy-done.41), channel_id=1, replica_groups=mesh['dp'=8,'tensor'=4] {'dp'}, use_global_device_ids=true, to_apply=%region_30.31 | all-reduce | flops 4480 | bytes 35840 | tf_op jit(solution)/shard_map/psum | solution.py:292
  1283.6 39.5 %reduce-scatter.17.cloned.1.call-done = bf16[1280,160]{0,1:T(8,128)(2,1)} async-done(((bf16[1280,1280]{0,1:T(8,128)(2,1)}), bf16[1280,160]{0,1:T(8,128)(2,1)}) %reduce-scatter.17.cloned.1.call-update) | async-done | bytes 409616 | tf_op jit(solution)/shard_map/reduce_scatter | solution.py:288
  1325.0 76.7 %reduce-scatter.15.cloned.1.call-done = bf16[160,1280]{1,0:T(8,128)(2,1)} async-done(((bf16[1280,1280]{1,0:T(8,128)(2,1)}), bf16[160,1280]{1,0:T(8,128)(2,1)}) %reduce-scatter.15.cloned.1.call-update) | async-done | bytes 409616 | tf_op jit(solution)/shard_map/reduce_scatter | solution.py:285
  1403.7 60.2 %all-reduce.14.cloned.1.call-done = (bf16[512,1280]{1,0:T(8,128)(2,1)}, bf16[512,1280]{1,0:T(8,128)(2,1)}) async-done(((bf16[512,1280]{1,0:T(8,128)(2,1)}, bf16[512,1280]{1,0:T(8,128)(2,1)}), (bf16[512,1280]{1,0:T(8,128)(2,1)}, bf16[512,1280]{1,0:T(8,128)(2,1)})) %all-reduce.14.cloned.1.call-update) | async-done | bytes 2621456 | tf_op jit(solution)/shard_map/psum | solution.py:42
  1472.6 67.8 %reduce-scatter.11.cloned.1.call-done = bf16[160,3,320]{2,0,1:T(8,128)(2,1)} async-done(((bf16[1280,3,320]{2,0,1:T(8,128)(2,1)}), bf16[160,3,320]{2,0,1:T(8,128)(2,1)}) %reduce-scatter.11.cloned.1.call-update) | async-done | bytes 307216 | tf_op jit(solution)/shard_map/reduce_scatter | solution.py:279
  1542.3 128.3 %all-reduce.12.cloned.1.call-done = (f32[1280]{0:T(1024)}, f32[1280]{0:T(1024)}, f32[127,80]{0,1:T(8,128)}, f32[127,80]{0,1:T(8,128)}, f32[1280]{0:T(1024)}, /*index=5*/f32[1280]{0:T(1024)}) async-done(((f32[1280]{0:T(1024)}, f32[1280]{0:T(1024)}, f32[127,80]{0,1:T(8,128)}, f32[127,80]{0,1:T(8,128)}, f32[1280]{0:T(1024)}, /*index=5*/f32[1280]{0:T(1024)}), (f32[1280]{0:T(1024)}, f32[1280]{0:T(1024)}, ...) | async-done | bytes 101776 | tf_op jit(solution)/shard_map/psum | solution.py:305
  (480 shorter events, 784.4 us)
Async XLA Ops:
  7.2 485.8 %copy-start = (bf16[1280,1280]{1,0:T(8,128)(2,1)S(1)}, bf16[1280,1280]{1,0:T(8,128)(2,1)}, u32[]{:S(2)}) copy-start(bf16[1280,1280]{1,0:T(8,128)(2,1)} %param.33) | copy-start | bytes 9830404
  7.2 68.8 %all-gather.6.cloned.1.call-start = ((), (), s32[]{:S(2)}) async-start(), calls=%async_computation.15 | async-start | bytes 2949120 | tf_op jit(solution)/shard_map/all_gather | solution.py:132
  16.3 117.4 %all-gather.4.cloned.1.call-start = ((), (), s32[]{:S(2)}) async-start(), calls=%async_computation.6 | async-start | bytes 2949120 | tf_op jit(solution)/shard_map/all_gather | solution.py:133
  19.3 469.9 %all-reduce.8.cloned.1.call-start = ((), (), s32[]{:S(2)}) async-start(), calls=%async_computation.7 | async-start | bytes 2621440 | tf_op jit(solution)/shard_map/psum | solution.py:42
  192.3 12.9 copy-start.60
  448.7 40.5 %copy-start.32 = (f32[1280]{0:T(1024)S(1)}, f32[1280]{0:T(1024)}, u32[]{:S(2)}) copy-start(f32[1280]{0:T(1024)} %param.28) | copy-start | bytes 15364
  451.9 95.7 %all-reduce.10.cloned.1.call-start = ((), (), s32[]{:S(2)}) async-start(), calls=%async_computation.8 | async-start | bytes 2621440 | tf_op jit(solution)/shard_map/psum | solution.py:42
  508.5 42.0 %copy-start.11 = (f32[512,1280]{1,0:T(8,128)S(1)}, f32[512,1280]{1,0:T(8,128)}, u32[]{:S(2)}) copy-start(f32[512,1280]{1,0:T(8,128)} %copy-done.10) | copy-start | bytes 7864324
  508.5 596.1 %reduce-scatter.7.cloned.1.call-start = ((), (), s32[]{:S(2)}) async-start(), calls=%async_computation.9 | async-start | bytes 2949120 | tf_op jit(solution)/shard_map/reduce_scatter | solution.py:255
  1033.6 144.3 %reduce-scatter.9.cloned.1.call-start = ((), (), s32[]{:S(2)}) async-start(), calls=%async_computation.10 | async-start | bytes 2949120 | tf_op jit(solution)/shard_map/reduce_scatter | solution.py:258
  1034.2 209.3 %reduce-scatter.13.cloned.1.call-start = ((), (), s32[]{:S(2)}) async-start(), calls=%async_computation.12 | async-start | bytes 1105920 | tf_op jit(solution)/shard_map/reduce_scatter | solution.py:282
  1037.2 285.9 %reduce-scatter.17.cloned.1.call-start = ((), (), s32[]{:S(2)}) async-start(), calls=%async_computation.14 | async-start | bytes 3686400 | tf_op jit(solution)/shard_map/reduce_scatter | solution.py:288
  1042.6 359.1 %reduce-scatter.15.cloned.1.call-start = ((), (), s32[]{:S(2)}) async-start(), calls=%async_computation.13 | async-start | bytes 3686400 | tf_op jit(solution)/shard_map/reduce_scatter | solution.py:285
  1049.3 414.6 %all-reduce.14.cloned.1.call-start = ((), (), s32[]{:S(2)}) async-start(), calls=%async_computation.17 | async-start | bytes 5242880 | tf_op jit(solution)/shard_map/psum | solution.py:42
  1183.9 356.5 %reduce-scatter.11.cloned.1.call-start = ((), (), s32[]{:S(2)}) async-start(), calls=%async_computation.11 | async-start | bytes 3317760 | tf_op jit(solution)/shard_map/reduce_scatter | solution.py:279
  1187.8 20.4 %copy-start.46 = (f32[320]{0:T(512)S(1)}, f32[320]{0:T(512)}, u32[]{:S(2)}) copy-start(f32[320]{0:T(512)} %copy-done.45) | copy-start | bytes 3844
  1187.8 24.0 %copy-start.30 = (f32[4,127,80]{1,2,0:T(8,128)S(1)}, f32[4,127,80]{1,2,0:T(8,128)}, u32[]{:S(2)}) copy-start(f32[4,127,80]{1,2,0:T(8,128)} %get-tuple-element.189) | copy-start | bytes 487684
  1187.8 24.6 %copy-start.31 = (f32[4,127,80]{1,2,0:T(8,128)S(1)}, f32[4,127,80]{1,2,0:T(8,128)}, u32[]{:S(2)}) copy-start(f32[4,127,80]{1,2,0:T(8,128)} %get-tuple-element.188) | copy-start | bytes 487684
  1187.8 25.2 %copy-start.16 = (bf16[512,1280]{1,0:T(8,128)(2,1)S(1)}, bf16[512,1280]{1,0:T(8,128)(2,1)}, u32[]{:S(2)}) copy-start(bf16[512,1280]{1,0:T(8,128)(2,1)} %all-reduce.10.cloned.1.call-done) | copy-start | bytes 3932164
  1187.9 482.8 %all-reduce.12.cloned.1.call-start = ((), (), s32[]{:S(2)}) async-start(), calls=%async_computation.16 | async-start | bytes 229376 | tf_op jit(solution)/shard_map/psum | solution.py:305
  1213.1 33.3 %copy-start.40 = (f32[1280]{0:T(1024)S(1)}, f32[1280]{0:T(1024)}, u32[]{:S(2)}) copy-start(f32[1280]{0:T(1024)} %get-tuple-element.477) | copy-start | bytes 15364
  1213.1 33.3 %copy-start.41 = (f32[1280]{0:T(1024)S(1)}, f32[1280]{0:T(1024)}, u32[]{:S(2)}) copy-start(f32[1280]{0:T(1024)} %get-tuple-element.489) | copy-start | bytes 15364
  1213.1 33.3 %copy-start.48 = (f32[1280]{0:T(1024)S(1)}, f32[1280]{0:T(1024)}, u32[]{:S(2)}) copy-start(f32[1280]{0:T(1024)} %get-tuple-element.493) | copy-start | bytes 15364
  1467.2 211.4 %copy-start.1 = (bf16[1280,1280]{1,0:T(8,128)(2,1)S(1)}, bf16[1280,1280]{1,0:T(8,128)(2,1)}, u32[]{:S(2)}) copy-start(bf16[1280,1280]{1,0:T(8,128)(2,1)} %param.33) | copy-start | bytes 9830404
  (92 other events, 433.5 us)
Sparse Core Ops, SparseCore 0:
  16.4 59.5 all-gather.5
  78.7 55.0 all-gather.3
  452.0 37.1 all-reduce.7
  508.6 38.9 all-reduce.9
  1033.7 70.8 reduce-scatter.6
  1108.0 69.8 reduce-scatter.8
  1181.3 62.1 reduce-scatter.12
  1247.5 75.5 reduce-scatter.16
  1326.7 75.0 reduce-scatter.14
  1404.7 59.1 all-reduce.13
  1467.9 72.5 reduce-scatter.10
  1547.9 122.7 all-reduce.11
where the time goes:
time: 1700 us; the launch traced here: 1690 us
  waiting for transfers between devices  705 us (41%)
  local copies, waits for them, and re-layouts  465 us (27%)
  matrix products  302 us (18%)
  other arithmetic  134 us (8%)
  blocking collectives  56.5 us (3%)
    add x40, local copies, waits for them, and re-layouts, head_scores(): logits.reshape(images, image_rows, SIDE, SIDE, SIDE)  358 us
    psum x3, waiting for transfers between devices, full_sum(): return lax.psum(values.astype(jnp.bfloat16), 'tensor').astype(jnp.float32)  133 us
    psum x1, waiting for transfers between devices, on_device(): lax.psum((rows_term, cols_term, grad_norm1_gain, grad_norm1_shift, grad_n...  128 us
    dot_general x8, matrix products, head_scores(): jnp.einsum('iqc,ikc->iqk', query_head, key_head, preferred_element_type=j...  105 us
    reduce_scatter x1, waiting for transfers between devices, on_device(): lax.psum_scatter(grad_fc1.astype(jnp.bfloat16), 'dp', scatter_dimension=0...  76.7 us
    reduce_scatter x1, waiting for transfers between devices, on_device(): lax.psum_scatter(grad_value.astype(jnp.bfloat16), 'dp', scatter_dimension...  73.3 us
    reduce_scatter x1, waiting for transfers between devices, on_device(): lax.psum_scatter(grad_qkv.astype(jnp.bfloat16), 'dp', scatter_dimension=0...  67.8 us
    all_gather x1, waiting for transfers between devices, on_device(): lax.all_gather(key_rows, 'dp', axis=1, tiled=True)  54.1 us
  transfers between devices with their start and end apart: 12, of which 12 were waited for; matrix products, arithmetic and copies ran while one was open for 4% of the time, Pallas kernels for 0%

commit v1 on v0

v1 whole, which is shorter than its diff:
```python
import functools
import math

import jax
import jax.numpy as jnp
from jax import lax
from jax.experimental import pallas as pl
from jax.experimental.pallas import tpu as pltpu
from jax.sharding import PartitionSpec as P

HEAD = 80
SIDE = 64

MESH = pl.DeviceIdType.MESH
LOW = jnp.bfloat16
F32 = jnp.float32
EPSILON = 1e-06
SCALE = HEAD**-0.5
EXP2_SCALE = SCALE * math.log2(math.e)
COLS_AT = HEAD
ROWS_AT = COLS_AT + 2 * SIDE
LSE_AT = ROWS_AT + 16
AUG = LSE_AT + 16
VMEM_LIMIT = 60 * 2**20


def nn(a, b):
    return lax.dot_general(a, b, (((1,), (0,)), ((), ())), preferred_element_type=F32)


def tn(a, b):
    return lax.dot_general(a, b, (((0,), (0,)), ((), ())), preferred_element_type=F32)


def nt(a, b):
    return lax.dot_general(a, b, (((1,), (1,)), ((), ())), preferred_element_type=F32)


def parts_of(values, count):
    pieces = []
    for _ in range(count):
        piece = values.astype(LOW).astype(F32)
        pieces.append(piece)
        values = values - piece
    return pieces


def send_dp(src, dst, send_sem, recv_sem, dev):
    return pltpu.make_async_remote_copy(
        src_ref=src,
        dst_ref=dst,
        send_sem=send_sem,
        recv_sem=recv_sem,
        device_id={"dp": dev},
        device_id_type=MESH,
    )


def shifts(rows, dev):
    spot = lax.broadcasted_iota(jnp.int32, (2 * SIDE, rows), 1)
    by_row = SIDE - 1 - (dev * (rows // SIDE) + lax.shift_right_logical(spot, 6))
    by_col = SIDE - 1 - (spot & (SIDE - 1))
    return by_row, by_col


def skew(values, shift):
    for bit in (32, 16, 8, 4, 2, 1):
        moved = pltpu.roll(values, 2 * SIDE - bit, 0)
        values = jnp.where((shift & bit) != 0, moved, values)
    return values[:SIDE]


def unskew(values, shift):
    values = jnp.concatenate([values, jnp.zeros_like(values)], axis=0)
    for bit in (32, 16, 8, 4, 2, 1):
        moved = pltpu.roll(values, bit, 0)
        values = jnp.where((shift & bit) != 0, moved, values)
    return values


def greet(peers):
    barrier = pltpu.get_barrier_semaphore()
    for peer in peers:
        pl.semaphore_signal(barrier, inc=1, device_id={"dp": peer}, device_id_type=MESH)
    pl.semaphore_wait(barrier, len(peers))


def key_onehots(rows, dev):
    spot = lax.broadcasted_iota(jnp.int32, (2 * SIDE, rows), 1)
    index = lax.broadcasted_iota(jnp.int32, (2 * SIDE, rows), 0)
    cols = jnp.where((index & (SIDE - 1)) == (spot & (SIDE - 1)), 1.0, 0.0)
    spot, index = spot[:16], index[:16]
    offset = lax.rem(dev * (rows // SIDE), 8)
    in_group = jnp.where((index & 7) == offset + lax.shift_right_logical(spot, 6), 1.0, 0.0)
    return cols, in_group


class Shape:
    def __init__(self, heads, group, rows):
        self.heads, self.group, self.rows = heads, group, rows
        self.queries = heads * rows
        self.block = min(512, self.queries)


def forward_kernel(
    shape, qkv, tables, att, qaug, bias_rows, kv_out, o_out, lse_out, peak_out,
    rq, rkv, kaug_t, kaug, vaug, oacc, mrow, lpk, att_s, att_r,
    q_send, q_recv, k_send, k_recv, x_send, x_recv, r_send, r_recv, o_sem,
):
    heads, group, rows, block = shape.heads, shape.group, shape.rows, shape.block
    me = lax.axis_index("dp")
    z, g = me // group, lax.rem(me, group)
    column = [lax.rem(z + k, heads) for k in range(1, heads)]
    mates = [lax.rem(g + k, group) for k in range(1, group)]
    greet([h * group + g for h in column] + [z * group + o for o in mates])
    sends = []
    for h in column:
        sends.append(send_dp(qkv.at[h, 0], rq.at[z], q_send.at[h], q_recv.at[z], h * group + g))
    for h in column:
        sends.append(
            send_dp(
                qkv.at[h, pl.ds(1, 2)], rkv.at[z, g], k_send.at[h], k_recv.at[z], h * group + g
            )
        )
    for copy in sends:
        copy.start()
    rq[z] = qkv[z, 0]
    rkv[z, g] = qkv[z, pl.ds(1, 2)]
    qaug[pl.ds(LSE_AT, 16), :] = jnp.zeros((16, shape.queries), LOW)
    kaug_t[pl.ds(LSE_AT, 16), :] = jnp.zeros((16, rows), LOW)
    vaug[pl.ds(HEAD, 16), :] = jnp.where(
        lax.broadcasted_iota(jnp.int32, (16, rows), 0) == 0, 1.0, 0.0
    ).astype(LOW)
    oacc[...] = jnp.zeros_like(oacc)
    mrow[...] = jnp.full_like(mrow, -jnp.inf)
    lpk[...] = jnp.full_like(lpk, -jnp.inf)

    def prepare(k, carry):
        source = lax.rem(z - k + heads, heads)
        span = pl.ds(pl.multiple_of(source * rows, rows), rows)

        @pl.when(k > 0)
        def _():
            send_dp(rq.at[source], rq.at[source], q_send.at[source], q_recv.at[source], me).wait_recv()

        query = rq[source]
        by_row, by_col = shifts(rows, source * group + g)
        along_rows = skew(nn(tables[0], query) * (1.0 / SCALE), by_row)
        along_cols = skew(nn(tables[1], query) * (1.0 / SCALE), by_col)
        qaug[pl.ds(0, HEAD), span] = query
        cols = parts_of(along_cols, 2)
        qaug[pl.ds(COLS_AT, 2 * SIDE), span] = jnp.concatenate(cols, axis=0).astype(LOW)
        high, rest = parts_of(along_rows, 2)
        for at in range(SIDE // 8):
            pair = jnp.concatenate([high[8 * at : 8 * at + 8], rest[8 * at : 8 * at + 8]], axis=0)
            bias_rows[at, :, span] = pair.astype(LOW)
        return carry

    lax.fori_loop(0, heads, prepare, 0)

    def chunk(source, mate):
        dev = source * group + mate
        cols, in_group = key_onehots(rows, dev)
        kaug_t[pl.ds(0, HEAD), :] = rkv[source, mate, 0]
        kaug_t[pl.ds(COLS_AT, 2 * SIDE), :] = cols.astype(LOW)
        kaug_t[pl.ds(ROWS_AT, 16), :] = in_group.astype(LOW)
        kaug[...] = kaug_t[...].T
        vaug[pl.ds(0, HEAD), :] = rkv[source, mate, 1]
        qaug[pl.ds(ROWS_AT, 16), :] = bias_rows[(dev * (rows // SIDE)) // 8]

        def one(i, carry):
            span = pl.ds(pl.multiple_of(i * block, block), block)
            logits = nn(kaug[:, :HEAD], qaug[pl.ds(0, HEAD), span])
            lpk[...] = jnp.maximum(lpk[...], jnp.max(logits.reshape(rows // 8, 8, block), axis=0))
            scores = nn(kaug[...], qaug[:, span])
            before = mrow[:, span]
            top = jnp.maximum(before, jnp.max(scores, axis=0, keepdims=True))
            mrow[:, span] = top
            weights = jnp.exp2(scores * EXP2_SCALE - top * EXP2_SCALE).astype(LOW)
            keep = jnp.exp2((before - top) * EXP2_SCALE)
            oacc[:, span] = oacc[:, span] * keep + nn(vaug[...], weights)
            return carry

        lax.fori_loop(0, shape.queries // block, one, 0)

    def column_step(k, carry):
        source = lax.rem(z - k + heads, heads)

        @pl.when(k > 0)
        def _():
            send_dp(rkv.at[source, g], rkv.at[source, g], k_send.at[source], k_recv.at[source], me).wait_recv()

        for n, mate in enumerate(mates):
            send_dp(
                rkv.at[source, g], rkv.at[source, g], x_send.at[source, n], x_recv.at[source, g],
                z * group + mate,
            ).start()
        chunk(source, g)

        def mate_step(n, inner):
            mate = lax.rem(g + n, group)
            send_dp(
                rkv.at[source, mate], rkv.at[source, mate], x_send.at[source, 0], x_recv.at[source, mate], me
            ).wait_recv()
            chunk(source, mate)
            return inner

        lax.fori_loop(1, group, mate_step, 0)
        return carry

    lax.fori_loop(0, heads, column_step, 0)
    keep_kv = pltpu.make_async_copy(rkv, kv_out, o_sem)
    keep_kv.start()

    def finish(source, carry):
        span = pl.ds(pl.multiple_of(source * rows, rows), rows)
        total = oacc[pl.ds(HEAD, 1), span]
        attended = oacc[pl.ds(0, HEAD), span] / total
        o_out[:, span] = attended
        lse_out[:, span] = mrow[:, span] + jnp.log2(total) * (1.0 / EXP2_SCALE)
        att_s[source] = attended.astype(LOW)

        @pl.when(source != z)
        def _():
            send_dp(
                att_s.at[source], att_r.at[z], r_send.at[source], r_recv.at[z], source * group + g
            ).start()

        return carry

    lax.fori_loop(0, heads, finish, 0)
    att[z] = att_s[z]
    peak_out[...] = jnp.full(peak_out.shape, jnp.max(lpk[...]) * SCALE, F32)
    for h in column:
        send_dp(att_s.at[h], att_r.at[h], r_send.at[h], r_recv.at[h], h * group + g).wait()
        att[h] = att_r[h]
    for copy in sends:
        copy.wait_send()
    for source in range(heads):
        for n, mate in enumerate(mates):
            send_dp(
                rkv.at[source, g], rkv.at[source, g], x_send.at[source, n], x_recv.at[source, g],
                z * group + mate,
            ).wait_send()
    keep_kv.wait()


def attend(shape, qkv, tables):
    heads, group, rows, queries = shape.heads, shape.group, shape.rows, shape.queries
    vmem = pl.BlockSpec(memory_space=pltpu.VMEM)
    hbm = pl.BlockSpec(memory_space=pl.ANY)
    dma = pltpu.SemaphoreType.DMA
    return pl.pallas_call(
        functools.partial(forward_kernel, shape),
        out_shape=(
            jax.ShapeDtypeStruct((heads, HEAD, rows), LOW),
            jax.ShapeDtypeStruct((AUG, queries), LOW),
            jax.ShapeDtypeStruct((SIDE // 8, 16, queries), LOW),
            jax.ShapeDtypeStruct((heads, group, 2, HEAD, rows), LOW),
            jax.ShapeDtypeStruct((HEAD, queries), F32),
            jax.ShapeDtypeStruct((1, queries), F32),
            jax.ShapeDtypeStruct((8, 128), F32),
        ),
        in_specs=[vmem, vmem],
        out_specs=(vmem, vmem, vmem, hbm, vmem, vmem, vmem),
        scratch_shapes=[
            pltpu.VMEM((heads, HEAD, rows), LOW),
            pltpu.VMEM((heads, group, 2, HEAD, rows), LOW),
            pltpu.VMEM((AUG, rows), LOW),
            pltpu.VMEM((rows, AUG), LOW),
            pltpu.VMEM((HEAD + 16, rows), LOW),
            pltpu.VMEM((HEAD + 16, queries), F32),
            pltpu.VMEM((1, queries), F32),
            pltpu.VMEM((8, shape.block), F32),
            pltpu.VMEM((heads, HEAD, rows), LOW),
            pltpu.VMEM((heads, HEAD, rows), LOW),
            dma((heads,)), dma((heads,)), dma((heads,)), dma((heads,)),
            dma((heads, group)), dma((heads, group)), dma((heads,)), dma((heads,)),
            dma,
        ],
        compiler_params=pltpu.CompilerParams(
            collective_id=1, has_side_effects=True, vmem_limit_bytes=VMEM_LIMIT
        ),
        name="attend",
    )(qkv, tables)


def backward_kernel(
    shape, ga, tables, qaug_in, bias_rows, rkv, o_in, lse_in, grads, table_grads,
    rdo, qaug, q_tok, do_aug, do_tok, kaug_t, kaug, vaug_t, vaug, kacc, vacc, dq, drow, dcol,
    part, xr, summed, gq_s, gq_r, gkv_r,
    d_send, d_recv, x_send, x_recv, kv_send, kv_recv, q_send, q_recv,
):
    heads, group, rows, block = shape.heads, shape.group, shape.rows, shape.block
    queries = shape.queries
    me = lax.axis_index("dp")
    z, g = me // group, lax.rem(me, group)
    column = [lax.rem(z + k, heads) for k in range(1, heads)]
    mates = [lax.rem(g + k, group) for k in range(1, group)]
    greet([h * group + g for h in column] + [z * group + o for o in mates])
    sends = []
    for h in column:
        copy = send_dp(ga.at[h], rdo.at[z], d_send.at[h], d_recv.at[z], h * group + g)
        copy.start()
        sends.append(copy)
    rdo[z] = ga[z]
    qaug[...] = qaug_in[...]
    ones = jnp.where(lax.broadcasted_iota(jnp.int32, (16, rows), 0) < 3, 1.0, 0.0).astype(LOW)
    kaug_t[pl.ds(LSE_AT, 16), :] = ones
    vaug_t[pl.ds(HEAD, 16), :] = ones
    vaug_t[pl.ds(HEAD + 16, 32), :] = jnp.zeros((32, rows), LOW)
    low_lse = parts_of(-lse_in[...], 3)
    qaug[pl.ds(LSE_AT, 16), :] = jnp.concatenate(
        low_lse + [jnp.zeros((13, queries), F32)], axis=0
    ).astype(LOW)
    dq[...] = jnp.zeros_like(dq)
    dcol[...] = jnp.zeros_like(dcol)
    drow[...] = jnp.zeros_like(drow)

    def prepare(k, carry):
        source = lax.rem(z - k + heads, heads)
        span = pl.ds(pl.multiple_of(source * rows, rows), rows)

        @pl.when(k > 0)
        def _():
            send_dp(rdo.at[source], rdo.at[source], d_send.at[source], d_recv.at[source], me).wait_recv()

        upstream = rdo[source]
        dots = jnp.sum(upstream.astype(F32) * o_in[:, span], axis=0, keepdims=True)
        low_dots = parts_of(-dots, 3)
        do_aug[pl.ds(0, HEAD), span] = upstream
        do_aug[pl.ds(HEAD, 16), span] = jnp.concatenate(
            low_dots + [jnp.zeros((13, rows), F32)], axis=0
        ).astype(LOW)
        do_aug[pl.ds(HEAD + 16, 32), span] = jnp.zeros((32, rows), LOW)
        do_tok[span, :] = do_aug[:, span].T
        q_tok[span, :] = qaug[pl.ds(0, 128), span].T
        return carry

    lax.fori_loop(0, heads, prepare, 0)

    def chunk(source, mate):
        dev = source * group + mate
        at = (dev * (rows // SIDE)) // 8
        cols, in_group = key_onehots(rows, dev)
        kaug_t[pl.ds(0, HEAD), :] = rkv[source, mate, 0]
        kaug_t[pl.ds(COLS_AT, 2 * SIDE), :] = cols.astype(LOW)
        kaug_t[pl.ds(ROWS_AT, 16), :] = in_group.astype(LOW)
        kaug[...] = kaug_t[...].T
        vaug_t[pl.ds(0, HEAD), :] = rkv[source, mate, 1]
        vaug[...] = vaug_t[...].T
        qaug[pl.ds(ROWS_AT, 16), :] = bias_rows[at]
        kacc[...] = jnp.zeros_like(kacc)
        vacc[...] = jnp.zeros_like(vacc)
        back = jnp.concatenate(
            [kaug_t[pl.ds(0, COLS_AT + SIDE), :], kaug_t[pl.ds(ROWS_AT, 16), :]], axis=0
        )

        def one(i, carry):
            span = pl.ds(pl.multiple_of(i * block, block), block)
            probs = jnp.exp2(nn(kaug[...], qaug[:, span]) * EXP2_SCALE)
            pulled = nn(vaug[...], do_aug[:, span])
            low_grads = (probs * pulled).astype(LOW)
            vacc[...] += nn(probs.astype(LOW), do_tok[span, :])
            kacc[...] += nn(low_grads, q_tok[span, :])
            found = nn(back, low_grads)
            dq[:, span] += found[:HEAD]
            dcol[:, span] += found[COLS_AT : COLS_AT + SIDE]
            drow[at, :, span] += found[COLS_AT + SIDE : COLS_AT + SIDE + 8]
            return carry

        lax.fori_loop(0, queries // block, one, 0)

    def put(where, extra):
        key_part = (kacc[...] * SCALE).T[:HEAD]
        value_part = vacc[...].T[:HEAD]
        for other in extra:
            key_part = key_part + other[0].astype(F32)
            value_part = value_part + other[1].astype(F32)
        where[0] = key_part.astype(LOW)
        where[1] = value_part.astype(LOW)

    def mate_copy(source, mate):
        return send_dp(
            part.at[source, mate], xr.at[source, g], x_send.at[source, mate], x_recv.at[source, g],
            z * group + mate,
        )

    def mates_step(k, carry):
        source = lax.rem(z + k, heads)

        def mate_step(n, inner):
            mate = lax.rem(g + n, group)
            chunk(source, mate)
            put(part.at[source, mate], [])
            mate_copy(source, mate).start()
            return inner

        lax.fori_loop(1, group, mate_step, 0)
        return carry

    lax.fori_loop(1, heads + 1, mates_step, 0)

    def own_step(k, carry):
        source = lax.rem(z + k, heads)
        chunk(source, g)
        extra = []
        for mate in mates:
            send_dp(
                xr.at[source, mate], xr.at[source, mate], x_send.at[source, mate], x_recv.at[source, mate], me
            ).wait_recv()
            extra.append(xr.at[source, mate])
        put(summed.at[source], extra)

        @pl.when(source != z)
        def _():
            send_dp(
                summed.at[source], gkv_r.at[z], kv_send.at[source], kv_recv.at[z], source * group + g
            ).start()

        return carry

    lax.fori_loop(1, heads + 1, own_step, 0)
    table_grads[...] = jnp.zeros_like(table_grads)

    def finish(k, carry):
        source = lax.rem(z + k, heads)
        span = pl.ds(pl.multiple_of(source * rows, rows), rows)
        by_row, by_col = shifts(rows, source * group + g)
        total = dq[:, span] * SCALE
        for n, held in enumerate((drow[:, :, span].reshape(SIDE, rows), dcol[:, span])):
            spread = unskew(held, by_col if n else by_row)
            for piece in parts_of(spread, 2):
                low_piece = piece.astype(LOW)
                total = total + tn(tables[n], low_piece)
                table_grads[n] += nn(low_piece, q_tok[span, :])
        gq_s[source] = total.astype(LOW)

        @pl.when(source != z)
        def _():
            send_dp(
                gq_s.at[source], gq_r.at[z], q_send.at[source], q_recv.at[z], source * group + g
            ).start()

        return carry

    lax.fori_loop(1, heads + 1, finish, 0)
    grads[z, 0] = gq_s[z]
    grads[z, pl.ds(1, 2)] = summed[z]
    for h in column:
        send_dp(summed.at[h], gkv_r.at[h], kv_send.at[h], kv_recv.at[h], h * group + g).wait()
        grads[h, pl.ds(1, 2)] = gkv_r[h]
    for h in column:
        send_dp(gq_s.at[h], gq_r.at[h], q_send.at[h], q_recv.at[h], h * group + g).wait()
        grads[h, 0] = gq_r[h]
    for copy in sends:
        copy.wait_send()
    for source in range(heads):
        for mate in mates:
            mate_copy(source, mate).wait_send()


def attend_back(shape, ga, tables, qaug, bias_rows, kv, o_rows, lse):
    heads, group, rows, queries = shape.heads, shape.group, shape.rows, shape.queries
    vmem = pl.BlockSpec(memory_space=pltpu.VMEM)
    dma = pltpu.SemaphoreType.DMA
    return pl.pallas_call(
        functools.partial(backward_kernel, shape),
        out_shape=(
            jax.ShapeDtypeStruct((heads, 3, HEAD, rows), LOW),
            jax.ShapeDtypeStruct((2, 2 * SIDE, 128), F32),
        ),
        in_specs=[vmem] * 7,
        out_specs=(vmem, vmem),
        scratch_shapes=[
            pltpu.VMEM((heads, HEAD, rows), LOW),
            pltpu.VMEM((AUG, queries), LOW),
            pltpu.VMEM((queries, 128), LOW),
            pltpu.VMEM((128, queries), LOW),
            pltpu.VMEM((queries, 128), LOW),
            pltpu.VMEM((AUG, rows), LOW),
            pltpu.VMEM((rows, AUG), LOW),
            pltpu.VMEM((128, rows), LOW),
            pltpu.VMEM((rows, 128), LOW),
            pltpu.VMEM((rows, 128), F32),
            pltpu.VMEM((rows, 128), F32),
            pltpu.VMEM((HEAD, queries), F32),
            pltpu.VMEM((SIDE // 8, 8, queries), F32),
            pltpu.VMEM((SIDE, queries), F32),
            pltpu.VMEM((heads, group, 2, HEAD, rows), LOW),
            pltpu.VMEM((heads, group, 2, HEAD, rows), LOW),
            pltpu.VMEM((heads, 2, HEAD, rows), LOW),
            pltpu.VMEM((heads, HEAD, rows), LOW),
            pltpu.VMEM((heads, HEAD, rows), LOW),
            pltpu.VMEM((heads, 2, HEAD, rows), LOW),
            dma((heads,)), dma((heads,)), dma((heads, group)), dma((heads, group)),
            dma((heads,)), dma((heads,)), dma((heads,)), dma((heads,)),
        ],
        compiler_params=pltpu.CompilerParams(
            collective_id=2, has_side_effects=True, vmem_limit_bytes=VMEM_LIMIT
        ),
        name="attend_back",
    )(ga, tables, qaug, bias_rows, kv, o_rows, lse)


def norm_forward(values, norm_gain, norm_shift):
    center = values - jnp.mean(values, axis=-1, keepdims=True)
    variance = jnp.mean(center * center, axis=-1, keepdims=True)
    inverse = lax.rsqrt(variance + EPSILON)
    scaled = center * inverse
    return (scaled * norm_gain + norm_shift, scaled, inverse)


def norm_backward(upstream, scaled, inverse, norm_gain):
    weighted = upstream * norm_gain
    centered_grad = weighted - jnp.mean(weighted, axis=-1, keepdims=True)
    centered_grad = centered_grad - scaled * jnp.mean(weighted * scaled, axis=-1, keepdims=True)
    return centered_grad * inverse


def gain_terms(upstream, scaled):
    return (jnp.sum(upstream * scaled, axis=0), jnp.sum(upstream, axis=0))


def rows_of(values, share_base, share_rows):
    return lax.dynamic_slice_in_dim(values, share_base, share_rows, 0)


def exact_gelu(values):
    return jax.nn.gelu(values, approximate=False)


def full_sum(values):
    return lax.psum(values.astype(jnp.bfloat16), "tensor").astype(jnp.float32)


def on_device(
    tokens,
    cotangent,
    norm1_gain,
    norm1_shift,
    qkv_weight,
    qv_bias,
    proj_weight,
    proj_bias,
    table_rows,
    table_cols,
    norm2_gain,
    norm2_shift,
    fc1_weight,
    fc1_bias,
    fc2_weight,
    fc2_bias,
    threshold,
):
    images, row_count, model_width = tokens.shape
    token_count = images * row_count
    local_width = qkv_weight.shape[2]
    local_heads = local_width // HEAD
    groups = lax.axis_size("tensor")
    share_rows = token_count // groups
    share_base = lax.axis_index("tensor") * share_rows
    residual_in = tokens.reshape(token_count, model_width).astype(jnp.float32)
    normed1, scaled1, inverse1 = norm_forward(residual_in, norm1_gain, norm1_shift)
    normed1_low = normed1.astype(jnp.bfloat16)
    shape = Shape(local_heads, lax.axis_size("dp") // local_heads, row_count)
    flipped = jnp.stack([table_rows, table_cols])[:, ::-1]
    flipped = jnp.pad(flipped, ((0, 0), (0, 1), (0, 0)))
    triple = jnp.einsum("dtc,nd->tcn", qkv_weight, normed1_low, preferred_element_type=jnp.float32)
    bias = jnp.stack([qv_bias[0], jnp.zeros_like(qv_bias[0]), qv_bias[1]])
    triple = (triple + bias[:, :, None]).astype(jnp.bfloat16)
    qkv = triple.reshape(3, local_heads, HEAD, row_count).transpose(1, 0, 2, 3)
    attended, qaug, bias_rows, kv, o_rows, lse, peak = attend(shape, qkv, flipped)
    attended_flat = attended.reshape(local_width, token_count)
    branch_part = jnp.einsum(
        "cn,cd->nd", attended_flat, proj_weight, preferred_element_type=jnp.float32
    )
    middle_rows = residual_in + full_sum(branch_part) + proj_bias
    normed2, scaled2, inverse2 = norm_forward(middle_rows, norm2_gain, norm2_shift)
    normed2_low = normed2.astype(jnp.bfloat16)
    up_value = jnp.dot(normed2_low, fc1_weight, preferred_element_type=jnp.float32) + fc1_bias
    activated, gelu_pull = jax.vjp(exact_gelu, up_value)
    activated_low = activated.astype(jnp.bfloat16)
    mlp_part = jnp.dot(activated_low, fc2_weight, preferred_element_type=jnp.float32)
    output = (middle_rows + (full_sum(mlp_part) + fc2_bias)).astype(jnp.bfloat16)
    grad_out = cotangent.reshape(token_count, model_width)
    grad_out_f = grad_out.astype(jnp.float32)
    grad_fc2 = jnp.einsum("nf,nd->fd", activated_low, grad_out, preferred_element_type=jnp.float32)
    grad_fc2_bias = jnp.sum(grad_out_f, axis=0)
    grad_activated = jnp.einsum(
        "nd,fd->nf", grad_out, fc2_weight, preferred_element_type=jnp.float32
    )
    grad_up = gelu_pull(grad_activated)[0].astype(jnp.bfloat16)
    grad_fc1 = jnp.einsum("nd,nf->df", normed2_low, grad_up, preferred_element_type=jnp.float32)
    grad_fc1_bias = jnp.sum(grad_up.astype(jnp.float32), axis=0)
    normed2_part = jnp.einsum("nf,df->nd", grad_up, fc1_weight, preferred_element_type=jnp.float32)
    grad_normed2 = full_sum(normed2_part)
    grad_norm2_gain, grad_norm2_shift = gain_terms(
        rows_of(grad_normed2, share_base, share_rows), rows_of(scaled2, share_base, share_rows)
    )
    grad_middle = grad_out_f + norm_backward(grad_normed2, scaled2, inverse2, norm2_gain)
    grad_branch = grad_middle.astype(jnp.bfloat16)
    grad_proj = jnp.einsum(
        "cn,nd->cd", attended_flat, grad_branch, preferred_element_type=jnp.float32
    )
    grad_proj_bias = jnp.sum(grad_branch.astype(jnp.float32), axis=0)
    grad_attended = jnp.einsum(
        "cd,nd->cn", proj_weight, grad_branch, preferred_element_type=jnp.float32
    ).astype(jnp.bfloat16)
    grad_heads = grad_attended.reshape(local_heads, HEAD, row_count)
    grad_triple, table_terms = attend_back(
        shape, grad_heads, flipped, qaug, bias_rows, kv, o_rows, lse
    )
    grad_triple = grad_triple.transpose(1, 0, 2, 3).reshape(3, local_width, token_count)
    grad_qkv = jnp.einsum(
        "nd,tcn->dtc", normed1_low, grad_triple, preferred_element_type=jnp.float32
    )
    grad_qv_bias = jnp.sum(grad_triple[0::2].astype(jnp.float32), axis=2)
    normed1_part = jnp.einsum(
        "tcn,dtc->nd", grad_triple, qkv_weight, preferred_element_type=jnp.float32
    )
    grad_normed1 = full_sum(normed1_part)
    grad_norm1_gain, grad_norm1_shift = gain_terms(
        rows_of(grad_normed1, share_base, share_rows), rows_of(scaled1, share_base, share_rows)
    )
    from_norm1 = norm_backward(grad_normed1, scaled1, inverse1, norm1_gain)
    grad_tokens = (grad_middle + from_norm1).astype(jnp.bfloat16)
    grad_tokens = grad_tokens.reshape(images, row_count, model_width)
    grad_qkv, grad_proj, grad_fc1, grad_fc2 = (
        lax.psum_scatter(
            grad_qkv.astype(jnp.bfloat16), "dp", scatter_dimension=0, tiled=True
        ).astype(jnp.float32),
        lax.psum_scatter(
            grad_proj.astype(jnp.bfloat16), "dp", scatter_dimension=1, tiled=True
        ).astype(jnp.float32),
        lax.psum_scatter(
            grad_fc1.astype(jnp.bfloat16), "dp", scatter_dimension=0, tiled=True
        ).astype(jnp.float32),
        lax.psum_scatter(
            grad_fc2.astype(jnp.bfloat16), "dp", scatter_dimension=1, tiled=True
        ).astype(jnp.float32),
    )
    grad_proj_bias, grad_fc2_bias, grad_qv_bias, grad_fc1_bias = lax.psum(
        (grad_proj_bias, grad_fc2_bias, grad_qv_bias, grad_fc1_bias), "dp"
    )
    table_terms = table_terms[:, 2 * SIDE - 2 :: -1, :HEAD]
    rows_term, cols_term = table_terms[0], table_terms[1]
    own_head = jnp.arange(local_heads) == lax.axis_index("dp") // shape.group
    local_peaks = jnp.where(own_head, peak[0, 0], -jnp.inf)
    head_peaks = lax.pmax(local_peaks, "dp")
    (
        grad_table_rows,
        grad_table_cols,
        grad_norm1_gain,
        grad_norm1_shift,
        grad_norm2_gain,
        grad_norm2_shift,
    ) = lax.psum(
        (
            rows_term,
            cols_term,
            grad_norm1_gain,
            grad_norm1_shift,
            grad_norm2_gain,
            grad_norm2_shift,
        ),
        ("dp", "tensor"),
    )
    limit = threshold[0]
    clip_factors = jnp.sqrt(limit / jnp.maximum(head_peaks, limit))
    spread_factors = jnp.repeat(clip_factors, HEAD)
    clipped_qk = (qkv_weight[:, :2, :].astype(jnp.float32) * spread_factors).astype(jnp.bfloat16)
    clipped_q_bias = qv_bias[0] * spread_factors
    output = output.reshape(images, row_count, model_width)
    return (
        output,
        grad_tokens,
        grad_norm1_gain,
        grad_norm1_shift,
        grad_qkv,
        grad_qv_bias,
        grad_proj,
        grad_proj_bias,
        grad_table_rows,
        grad_table_cols,
        grad_norm2_gain,
        grad_norm2_shift,
        grad_fc1,
        grad_fc1_bias,
        grad_fc2,
        grad_fc2_bias,
        clipped_qk,
        clipped_q_bias,
        head_peaks,
        clip_factors,
    )


def solution(mesh):
    in_specs = (
        P(None, "dp", None),
        P(None, "dp", None),
        P(),
        P(),
        P(None, None, "tensor"),
        P(None, "tensor"),
        P("tensor", None),
        P(),
        P(),
        P(),
        P(),
        P(),
        P(None, "tensor"),
        P("tensor"),
        P("tensor", None),
        P(),
        P(),
    )
    out_specs = (
        P(None, "dp", None),
        P(None, "dp", None),
        P(),
        P(),
        P("dp", None, "tensor"),
        P(None, "tensor"),
        P("tensor", "dp"),
        P(),
        P(),
        P(),
        P(),
        P(),
        P("dp", "tensor"),
        P("tensor"),
        P("tensor", "dp"),
        P(),
        P(None, None, "tensor"),
        P("tensor"),
        P("tensor"),
        P("tensor"),
    )
    return jax.shard_map(
        on_device, mesh=mesh, in_specs=in_specs, out_specs=out_specs, check_vma=False
    )
```

time: 1700 us -> 752 us (0.44)
  local copies, waits for them, and re-layouts: 465 us -> 18.6 us
  matrix products: 302 us -> 47.7 us
  waiting for transfers between devices: 705 us -> 465 us
  Pallas kernels: 0 us -> 114 us
  other arithmetic: 134 us -> 34 us
    add x40 -> x0, local copies, waits for them, and re-layouts: 358 us -> none  [head_scores(): logits.reshape(images, image_rows, SIDE, SIDE, SIDE)]
    dot_general x90 -> x6, matrix products: 273 us -> 20.1 us  [the longest x1 4.34 us: on_device(): jnp.einsum('tcn,dtc->nd', grad_triple, qkv_weight, preferred_element_type...]
    reduce_scatter x2 -> x0, waiting for transfers between devices: 122 us -> none  [the longest x1 73.3 us: on_device(): lax.psum_scatter(grad_value.astype(jnp.bfloat16), 'dp', scatter_dimension...]
    pallas_call x0 -> x2, Pallas kernels: none -> 114 us  [the longest x1 59.9 us: attend(): pl.pallas_call(functools.partial(forward_kernel, shape), out_shape=(jax.S...]
    all_gather x2 -> x0, waiting for transfers between devices: 107 us -> none  [the longest x1 54.1 us: on_device(): lax.all_gather(key_rows, 'dp', axis=1, tiled=True)]
    psum x1, waiting for transfers between devices: 128 us -> 42.2 us  [on_device(): lax.psum((rows_term, cols_term, grad_norm1_gain, grad_norm1_shift, grad_n...]
    reduce_sum x11 -> x1, other arithmetic: 54.7 us -> 0.19 us  [on_device(): grad_qv_bias = jnp.sum(grad_triple[0::2].astype(jnp.float32), axis=2)]
    reshape x5 -> x1, local copies, waits for them, and re-layouts: 52.6 us -> 1.02 us  [on_device(): qkv = triple.reshape(3, local_heads, HEAD, row_count).transpose(1, 0, 2, 3)]
  transfers between devices with their start and end apart: 12 -> 8, of which waited for: 12 -> 8; matrix products, arithmetic and copies ran while one was open for 4% -> 6% of each run, Pallas kernels for 0% -> 0%
where the time goes in v1:
time: 752 us; the launch traced here: 751 us
  waiting for transfers between devices  465 us (62%)
  Pallas kernels  114 us (15%)
  blocking collectives  55.1 us (7%)
  matrix products  47.7 us (6%)
  other arithmetic  34 us (5%)
  local copies, waits for them, and re-layouts  18.6 us (2%)
  between operations  15.2 us (2%)
    psum x3, waiting for transfers between devices, full_sum(): return lax.psum(values.astype(jnp.bfloat16), 'tensor').astype(jnp.float32)  130 us
    reduce_scatter x1, waiting for transfers between devices, on_device(): lax.psum_scatter(grad_fc1.astype(jnp.bfloat16), 'dp', scatter_dimension=0...  77.2 us
    reduce_scatter x1, waiting for transfers between devices, on_device(): lax.psum_scatter(grad_fc2.astype(jnp.bfloat16), 'dp', scatter_dimension=1...  76.9 us
    reduce_scatter x1, waiting for transfers between devices, on_device(): lax.psum_scatter(grad_qkv.astype(jnp.bfloat16), 'dp', scatter_dimension=0...  73.8 us
    reduce_scatter x1, waiting for transfers between devices, on_device(): lax.psum_scatter(grad_proj.astype(jnp.bfloat16), 'dp', scatter_dimension=...  64.8 us
    pallas_call x1, Pallas kernels, attend(): pl.pallas_call(functools.partial(forward_kernel, shape), out_shape=(jax.S...  59.9 us
    pallas_call x1, Pallas kernels, attend_back(): pl.pallas_call(functools.partial(backward_kernel, shape), out_shape=(jax....  54.2 us
    psum x1, waiting for transfers between devices, on_device(): lax.psum((rows_term, cols_term, grad_norm1_gain, grad_norm1_shift, grad_n...  42.2 us
  transfers between devices with their start and end apart: 8, of which 8 were waited for; matrix products, arithmetic and copies ran while one was open for 6% of the time, Pallas kernels for 0%

profile of v1, /device:TPU:0, one launch (start us, length us, event | category | flops | bytes accessed | tf_op | source)
XLA Modules:
  0.0 751.1 jit_solution(10251721560294958716)
XLA Ops:
  12.1 3.7 add_convert_fusion.5
  17.5 59.9 %attend.1 = (bf16[4,80,512]{2,1,0:T(8,128)(2,1)}, bf16[240,2048]{1,0:T(8,128)(2,1)}, bf16[8,16,2048]{2,1,0:T(8,128)(2,1)}, bf16[4,2,2,80,512]{4,3,2,1,0:T(8,128)...) custom-call(bf16[4,3,80,512]{3,2,1,0:T(8,128)(2,1)} %bitcast.95, bf16[2,128,80]{2,1,0:T(8,128)(2,1)} %pad.4.tables), custom_call_target="tpu_custom_call" | custom-call | tf_op jit(solution)/shard_map/attend/pallas_call | solution.py:253
  77.4 2.9 convolution_convert_fusion.5
  80.6 40.0 %all-reduce.9.cloned.1.call-done = bf16[512,1280]{1,0:T(8,128)(2,1)} async-done(((bf16[512,1280]{1,0:T(8,128)(2,1)}), bf16[512,1280]{1,0:T(8,128)(2,1)}) %all-reduce.9.cloned.1.call-update) | async-done | bytes 1310736 | tf_op jit(solution)/shard_map/psum | solution.py:534
  124.5 8.2 %multiply_convert_fusion.1 = (bf16[512,1280]{1,0:T(8,128)(2,1)}, f32[512,1280]{1,0:T(8,128)S(1)}, f32[512,1280]{1,0:T(8,128)S(1)}) fusion(f32[1280]{0:T(1024)S(1)} %copy-done.36, bf16[1280,1280]{1,0:T(8,128)(2,1)S(1)} %copy-done, f32[512,1280]{1,0:T(8,128)S(1)} %subtract_multiply_fusion, f32[1280]{0:T(1024)S(1)} %copy-done.39, f32[1280]{0:T(1024)S(1)} %copy-done.24), kind=kOutput, calls=%fused_computation.35 | convolution fusion | flops 1722941440 | bytes 12467200 | tf_op jit(solution)/shard_map/dot_general | solution.py:581
  136.3 3.0 convolution_convert_fusion.3
  139.6 5.4 convolution_convert_fusion.4
  145.0 33.5 %all-reduce.11.cloned.1.call-done = bf16[512,1280]{1,0:T(8,128)(2,1)} async-done(((bf16[512,1280]{1,0:T(8,128)(2,1)}), bf16[512,1280]{1,0:T(8,128)(2,1)}) %all-reduce.11.cloned.1.call-update) | async-done | bytes 1310736 | tf_op jit(solution)/shard_map/psum | solution.py:534
  184.9 54.2 %attend_back.1 = (bf16[4,3,80,512]{3,2,1,0:T(8,128)(2,1)}, f32[2,128,128]{2,1,0:T(8,128)}) custom-call(bf16[4,80,512]{2,1,0:T(8,128)(2,1)} %bitcast.99, bf16[2,128,80]{2,1,0:T(8,128)(2,1)} %pad.4.tables, bf16[240,2048]{1,0:T(8,128)(2,1)} %get-tuple-element.30.qaug_in, bf16[8,16,2048]{2,1,0:T(8,128)(2,1)} %get-tuple-element.31.bias_rows, ...), custom_call_target="tpu_custom_call" | custom-call | tf_op jit(solution)/shard_map/attend_back/pallas_call | solution.py:467
  241.3 4.3 fusion.4
  249.2 56.8 %all-reduce.15.cloned.1.call-done = (bf16[512,1280]{1,0:T(8,128)(2,1)}, bf16[512,1280]{1,0:T(8,128)(2,1)}) async-done(((bf16[512,1280]{1,0:T(8,128)(2,1)}, bf16[512,1280]{1,0:T(8,128)(2,1)}), (bf16[512,1280]{1,0:T(8,128)(2,1)}, bf16[512,1280]{1,0:T(8,128)(2,1)})) %all-reduce.15.cloned.1.call-update) | async-done | bytes 2621456 | tf_op jit(solution)/shard_map/psum | solution.py:534
  309.4 3.7 convolution_convert_fusion.6
  313.4 3.8 convolution_convert_fusion.2
  319.0 3.6 convolution_convert_fusion
  324.3 5.0 convolution_convert_fusion.1
  331.2 21.4 %pmax.7 = f32[4]{0:T(128)S(1)} all-reduce(f32[4]{0:T(128)S(1)} %compare_select_fusion), channel_id=1, replica_groups=mesh['dp'=8,'tensor'=4] {'dp'}, use_global_device_ids=true, to_apply=%region_34.35 | all-reduce | flops 4 | bytes 32 | tf_op jit(solution)/shard_map/pmax | solution.py:650
  354.0 2.9 multiply_convert_fusion
  357.1 33.7 %all-reduce.2 = (f32[2,320]{1,0:T(2,128)}, f32[1280]{0:T(1024)}, f32[1280]{0:T(1024)}, f32[1280]{0:T(1024)}) all-reduce(f32[2,320]{1,0:T(2,128)S(1)} %convert_reduce_fusion.4, f32[1280]{0:T(1024)S(1)} %get-tuple-element.98, f32[1280]{0:T(1024)S(1)} %get-tuple-element.112, ...), channel_id=1, replica_groups=mesh['dp'=8,'tensor'=4] {'dp'}, use_global_device_ids=true, to_apply=%region_18.19 | all-reduce | flops 4480 | bytes 35840 | tf_op jit(solution)/shard_map/psum | solution.py:643
  390.9 5.3 fusion.21
  396.2 42.2 %all-reduce.13.cloned.1.call-done = (f32[1280]{0:T(1024)}, f32[1280]{0:T(1024)}, f32[127,80]{1,0:T(8,128)}, f32[127,80]{1,0:T(8,128)}, f32[1280]{0:T(1024)}, /*index=5*/f32[1280]{0:T(1024)}) async-done(((f32[1280]{0:T(1024)}, f32[1280]{0:T(1024)}, f32[127,80]{1,0:T(8,128)}, f32[127,80]{1,0:T(8,128)}, f32[1280]{0:T(1024)}, /*index=5*/f32[1280]{0:T(1024)}), (f32[1280]{0:T(1024)}, f32[1280]{0:T(1024)}, ...) | async-done | bytes 101776 | tf_op jit(solution)/shard_map/psum | solution.py:658
  441.6 64.8 %reduce-scatter.7.cloned.1.call-done = bf16[320,160]{0,1:T(8,128)(2,1)} async-done(((bf16[320,1280]{0,1:T(8,128)(2,1)}), bf16[320,160]{0,1:T(8,128)(2,1)}) %reduce-scatter.7.cloned.1.call-update) | async-done | bytes 102416 | tf_op jit(solution)/shard_map/reduce_scatter | solution.py:633
  508.0 73.8 %reduce-scatter.5.cloned.1.call-done = bf16[160,3,320]{2,0,1:T(8,128)(2,1)} async-done(((bf16[1280,3,320]{2,0,1:T(8,128)(2,1)}), bf16[160,3,320]{2,0,1:T(8,128)(2,1)}) %reduce-scatter.5.cloned.1.call-update) | async-done | bytes 307216 | tf_op jit(solution)/shard_map/reduce_scatter | solution.py:630
  583.8 76.9 %reduce-scatter.11.cloned.1.call-done = bf16[1280,160]{0,1:T(8,128)(2,1)} async-done(((bf16[1280,1280]{0,1:T(8,128)(2,1)}), bf16[1280,160]{0,1:T(8,128)(2,1)}) %reduce-scatter.11.cloned.1.call-update) | async-done | bytes 409616 | tf_op jit(solution)/shard_map/reduce_scatter | solution.py:639
  662.6 77.2 %reduce-scatter.9.cloned.1.call-done = bf16[160,1280]{1,0:T(8,128)(2,1)} async-done(((bf16[1280,1280]{1,0:T(8,128)(2,1)}), bf16[160,1280]{1,0:T(8,128)(2,1)}) %reduce-scatter.9.cloned.1.call-update) | async-done | bytes 409616 | tf_op jit(solution)/shard_map/reduce_scatter | solution.py:636
  (153 shorter events, 49.5 us)
Async XLA Ops:
  7.2 117.1 %copy-start = (bf16[1280,1280]{1,0:T(8,128)(2,1)S(1)}, bf16[1280,1280]{1,0:T(8,128)(2,1)}, u32[]{:S(2)}) copy-start(bf16[1280,1280]{1,0:T(8,128)(2,1)} %param.29) | copy-start | bytes 9830404
  7.3 113.3 %all-reduce.9.cloned.1.call-start = ((), (), s32[]{:S(2)}) async-start(), calls=%async_computation.4 | async-start | bytes 2621440 | tf_op jit(solution)/shard_map/psum | solution.py:534
  15.8 61.6 %copy-start.18 = (bf16[320,1280]{1,0:T(8,128)(2,1)S(1)}, bf16[320,1280]{1,0:T(8,128)(2,1)}, u32[]{:S(2)}) copy-start(bf16[320,1280]{1,0:T(8,128)(2,1)} %param.23) | copy-start | bytes 2457604
  16.9 103.7 %copy-start.22 = (f32[1280]{0:T(1024)S(1)}, f32[1280]{0:T(1024)}, u32[]{:S(2)}) copy-start(f32[1280]{0:T(1024)} %param.24) | copy-start | bytes 15364
  80.3 98.1 %all-reduce.11.cloned.1.call-start = ((), (), s32[]{:S(2)}) async-start(), calls=%async_computation.5 | async-start | bytes 2621440 | tf_op jit(solution)/shard_map/psum | solution.py:534
  124.5 8.2 %copy-start.35 = (bf16[1280,1280]{1,0:T(8,128)(2,1)S(1)}, bf16[1280,1280]{1,0:T(8,128)(2,1)}, u32[]{:S(2)}) copy-start(bf16[1280,1280]{1,0:T(8,128)(2,1)} %param.31) | copy-start | bytes 9830404
  139.3 166.7 %all-reduce.15.cloned.1.call-start = ((), (), s32[]{:S(2)}) async-start(), calls=%async_computation.11 | async-start | bytes 5242880 | tf_op jit(solution)/shard_map/psum | solution.py:534
  139.6 38.9 %copy-start.6 = (f32[512,1280]{1,0:T(8,128)S(1)}, f32[512,1280]{1,0:T(8,128)}, u32[]{:S(2)}) copy-start(f32[512,1280]{1,0:T(8,128)} %copy-done.5) | copy-start | bytes 7864324
  183.3 55.8 %copy-start.4 = (f32[512,1280]{1,0:T(8,128)}, f32[512,1280]{1,0:T(8,128)S(1)}, u32[]{:S(2)}) copy-start(f32[512,1280]{1,0:T(8,128)S(1)} %get-tuple-element.99) | copy-start | bytes 7864324
  245.7 192.8 %all-reduce.13.cloned.1.call-start = ((), (), s32[]{:S(2)}) async-start(), calls=%async_computation.10 | async-start | bytes 327680 | tf_op jit(solution)/shard_map/psum | solution.py:658
  247.3 60.4 %copy-start.3 = (bf16[1,512,1280]{2,1,0:T(8,128)(2,1)S(1)}, bf16[1,512,1280]{2,1,0:T(8,128)(2,1)}, u32[]{:S(2)}) copy-start(bf16[1,512,1280]{2,1,0:T(8,128)(2,1)} %param.17) | copy-start | bytes 3932164
  309.3 197.1 %reduce-scatter.7.cloned.1.call-start = ((), (), s32[]{:S(2)}) async-start(), calls=%async_computation.7 | async-start | bytes 1105920 | tf_op jit(solution)/shard_map/reduce_scatter | solution.py:633
  313.1 268.7 %reduce-scatter.5.cloned.1.call-start = ((), (), s32[]{:S(2)}) async-start(), calls=%async_computation.6 | async-start | bytes 3317760 | tf_op jit(solution)/shard_map/reduce_scatter | solution.py:630
  317.3 343.4 %reduce-scatter.11.cloned.1.call-start = ((), (), s32[]{:S(2)}) async-start(), calls=%async_computation.9 | async-start | bytes 3686400 | tf_op jit(solution)/shard_map/reduce_scatter | solution.py:639
  322.6 417.3 %reduce-scatter.9.cloned.1.call-start = ((), (), s32[]{:S(2)}) async-start(), calls=%async_computation.8 | async-start | bytes 3686400 | tf_op jit(solution)/shard_map/reduce_scatter | solution.py:636
  329.3 27.7 %copy-start.15 = (bf16[3,4,80,512]{3,2,1,0:T(8,128)(2,1)S(1)}, bf16[3,4,80,512]{3,2,1,0:T(8,128)(2,1)}, u32[]{:S(2)}) copy-start(bf16[3,4,80,512]{3,2,1,0:T(8,128)(2,1)} %copy-done.13) | copy-start | bytes 2949124
  329.3 61.6 %copy-start.28 = (f32[1280]{0:T(1024)S(1)}, f32[1280]{0:T(1024)}, u32[]{:S(2)}) copy-start(f32[1280]{0:T(1024)} %param.32) | copy-start | bytes 15364
  352.6 43.6 %copy-start.40 = (f32[4]{0:T(128)}, f32[4]{0:T(128)S(1)}, u32[]{:S(2)}) copy-start(f32[4]{0:T(128)S(1)} %pmax.7) | copy-start | bytes 52
  353.3 43.0 %copy-start.34 = (f32[4]{0:T(128)}, f32[4]{0:T(128)S(1)}, u32[]{:S(2)}) copy-start(f32[4]{0:T(128)S(1)} %divide_sqrt_fusion) | copy-start | bytes 52
  390.9 353.4 %copy-start.1 = (bf16[1280,1280]{1,0:T(8,128)(2,1)S(1)}, bf16[1280,1280]{1,0:T(8,128)(2,1)}, u32[]{:S(2)}) copy-start(bf16[1280,1280]{1,0:T(8,128)(2,1)} %param.29) | copy-start | bytes 9830404
  438.4 303.4 %copy-start.32 = (f32[1280]{0:T(1024)S(1)}, f32[1280]{0:T(1024)}, u32[]{:S(2)}) copy-start(f32[1280]{0:T(1024)} %get-tuple-element.118) | copy-start | bytes 15364
  438.4 304.0 %copy-start.31 = (f32[1280]{0:T(1024)S(1)}, f32[1280]{0:T(1024)}, u32[]{:S(2)}) copy-start(f32[1280]{0:T(1024)} %get-tuple-element.119) | copy-start | bytes 15364
  438.4 304.6 %copy-start.30 = (f32[1280]{0:T(1024)S(1)}, f32[1280]{0:T(1024)}, u32[]{:S(2)}) copy-start(f32[1280]{0:T(1024)} %get-tuple-element.126) | copy-start | bytes 15364
  438.4 305.2 %copy-start.29 = (f32[1280]{0:T(1024)S(1)}, f32[1280]{0:T(1024)}, u32[]{:S(2)}) copy-start(f32[1280]{0:T(1024)} %get-tuple-element.127) | copy-start | bytes 15364
  (27 other events, 80.1 us)
Sparse Core Ops, SparseCore 0:
  80.5 40.0 all-reduce.8
  139.4 38.9 all-reduce.10
  245.8 60.1 all-reduce.14
  313.4 124.9 all-reduce.12
  441.6 64.7 reduce-scatter.6
  510.3 71.5 reduce-scatter.4
  585.4 75.2 reduce-scatter.10
  664.7 75.1 reduce-scatter.8

commit v2 on v1

--- a/solution.py
+++ b/solution.py
@@ -503,35 +503,711 @@
     )(ga, tables, qaug, bias_rows, kv, o_rows, lse)
 
 
-def norm_forward(values, norm_gain, norm_shift):
+def send_tensor(src, dst, send_sem, recv_sem, dev):
+    return pltpu.make_async_remote_copy(
+        src_ref=src,
+        dst_ref=dst,
+        send_sem=send_sem,
+        recv_sem=recv_sem,
+        device_id={"tensor": dev},
+        device_id_type=MESH,
+    )
+
+
+def tensor_place():
+    me = lax.axis_index("tensor")
+    return lax.rem(me, 2), me // 2, lax.axis_size("tensor") // 2
+
+
+def tensor_peers():
+    core, line, lines = tensor_place()
+    far = [lax.rem(line + k, lines) * 2 + core for k in range(1, lines)]
+    return far + [line * 2 + 1 - core]
+
+
+def part_bufs(lines, share, width):
+    dma = pltpu.SemaphoreType.DMA
+    return [pltpu.VMEM((lines, share, width), LOW)] * 3 + [dma((lines,))] * 4
+
+
+class Reduce:
+    def __init__(self, part, mate_in, passed, line_in, m_send, m_recv, l_send, l_recv):
+        self.part, self.mate_in, self.passed, self.line_in = part, mate_in, passed, line_in
+        self.sems = m_send, m_recv, l_send, l_recv
+        self.core, self.line, self.lines = tensor_place()
+
+    def mate_copy(self, to):
+        m_send, m_recv, _, _ = self.sems
+        return send_tensor(
+            self.part.at[to * 2 + 1 - self.core], self.mate_in.at[to],
+            m_send.at[to], m_recv.at[to], self.line * 2 + 1 - self.core,
+        )
+
+    def line_copy(self, to, slot):
+        _, _, l_send, l_recv = self.sems
+        return send_tensor(
+            self.passed.at[to], self.line_in.at[slot], l_send.at[to], l_recv.at[slot],
+            to * 2 + self.core,
+        )
+
+    def give(self, to):
+        self.mate_copy(to).start()
+
+    def pass_on(self, to):
+        self.mate_copy(to).wait_recv()
+        both = self.part[to * 2 + self.core].astype(F32) + self.mate_in[to].astype(F32)
+        self.passed[to] = both.astype(LOW)
+        self.line_copy(to, self.line).start()
+
+    def others(self):
+        return [lax.rem(self.line + k, self.lines) for k in range(1, self.lines)]
+
+    def total(self):
+        self.mate_copy(self.line).wait_recv()
+        total = self.part[self.line * 2 + self.core].astype(F32) + self.mate_in[self.line].astype(F32)
+        for other in self.others():
+            self.line_copy(other, other).wait_recv()
+            total = total + self.line_in[other].astype(F32)
+        return total
+
+    def finish(self):
+        self.mate_copy(self.line).wait_send()
+        for other in self.others():
+            self.mate_copy(other).wait_send()
+            self.line_copy(other, self.line).wait_send()
+
+
+def gather_sems(lines):
+    dma = pltpu.SemaphoreType.DMA
+    return [dma((lines,)), dma((lines,)), dma((2 * lines,))]
+
+
+class Gather:
+    def __init__(self, whole, l_send, m_send, recv):
+        self.whole, self.sems = whole, (l_send, m_send, recv)
+        self.core, self.line, self.lines = tensor_place()
+
+    def line_copy(self, to):
+        l_send, _, recv = self.sems
+        own = self.line * 2 + self.core
+        return send_tensor(
+            self.whole.at[own], self.whole.at[own], l_send.at[to], recv.at[own], to * 2 + self.core
+        )
+
+    def mate_copy(self, at):
+        _, m_send, recv = self.sems
+        part = at * 2 + self.core
+        return send_tensor(
+            self.whole.at[part], self.whole.at[part], m_send.at[at], recv.at[part],
+            self.line * 2 + 1 - self.core,
+        )
+
+    def arrived(self, part):
+        l_send, _, recv = self.sems
+        send_tensor(
+            self.whole.at[part], self.whole.at[part], l_send.at[0], recv.at[part], part
+        ).wait_recv()
+
+    def others(self):
+        return [lax.rem(self.line + k, self.lines) for k in range(1, self.lines)]
+
+    def start(self):
+        for other in self.others():
+            self.line_copy(other).start()
+        self.mate_copy(self.line).start()
+
+    def forward(self, at):
+        self.arrived(at * 2 + self.core)
+        self.mate_copy(at).start()
+
+    def take(self, at):
+        self.arrived(at * 2 + 1 - self.core)
+
+    def finish(self):
+        self.mate_copy(self.line).wait_send()
+        for other in self.others():
+            self.mate_copy(other).wait_send()
+            self.line_copy(other).wait_send()
+
+
+def normed(values):
     center = values - jnp.mean(values, axis=-1, keepdims=True)
     variance = jnp.mean(center * center, axis=-1, keepdims=True)
     inverse = lax.rsqrt(variance + EPSILON)
-    scaled = center * inverse
-    return (scaled * norm_gain + norm_shift, scaled, inverse)
-
-
-def norm_backward(upstream, scaled, inverse, norm_gain):
-    weighted = upstream * norm_gain
-    centered_grad = weighted - jnp.mean(weighted, axis=-1, keepdims=True)
-    centered_grad = centered_grad - scaled * jnp.mean(weighted * scaled, axis=-1, keepdims=True)
-    return centered_grad * inverse
-
-
-def gain_terms(upstream, scaled):
-    return (jnp.sum(upstream * scaled, axis=0), jnp.sum(upstream, axis=0))
-
-
-def rows_of(values, share_base, share_rows):
-    return lax.dynamic_slice_in_dim(values, share_base, share_rows, 0)
-
-
-def exact_gelu(values):
-    return jax.nn.gelu(values, approximate=False)
-
-
-def full_sum(values):
-    return lax.psum(values.astype(jnp.bfloat16), "tensor").astype(jnp.float32)
+    return center * inverse, inverse
+
+
+def normed_back(upstream, scaled, inverse, gain):
+    weighted = upstream * gain
+    centered = weighted - jnp.mean(weighted, axis=-1, keepdims=True)
+    return (centered - scaled * jnp.mean(weighted * scaled, axis=-1, keepdims=True)) * inverse
+
+
+def tile_of(width):
+    return 256 if width % 256 == 0 else 128
+
+
+def middle_kernel(
+    att, proj_w, tokens, cot, fc1_hbm, fc2_hbm, fc1_bias, vectors,
+    output, branch_out, middle_out, fc1_out, fc2_out, proj_out, ga_out, fc1_bias_out, sums_out,
+    fc1, fc2, att_tok, branch, mlp, back, n2, act, gu, gb, outs, held, spread,
+    load1, load2, *rest,
+):
+    core, line, lines = tensor_place()
+    me = lax.axis_index("tensor")
+    _, share, width = tokens.shape
+    rows = tokens.shape[0] * share
+    hidden = fc1_hbm.shape[1]
+    step, dstep = tile_of(hidden), tile_of(width)
+    in_fc1 = pltpu.make_async_copy(fc1_hbm, fc1, load1)
+    in_fc2 = pltpu.make_async_copy(fc2_hbm, fc2, load2)
+    in_fc1.start()
+    in_fc2.start()
+    greet_tensor()
+    sum_branch = Reduce(branch, *rest[0:7])
+    sum_mlp = Reduce(mlp, *rest[7:14])
+    sum_back = Reduce(back, *rest[14:21])
+    all_n2 = Gather(n2, *rest[21:24])
+    all_gb = Gather(gb, *rest[24:27])
+    all_out = Gather(outs, *rest[27:30])
+    att_tok[...] = att[...].T.reshape(att_tok.shape)
+
+    def project(k, carry):
+        to = lax.rem(line + 1 + lax.rem(k, lines), lines)
+        part = to * 2 + jnp.where(k < lines, 1 - core, core)
+        branch[part] = nn(att_tok[part], proj_w[...]).astype(LOW)
+
+        @pl.when(k < lines)
+        def _():
+            sum_branch.give(to)
+
+        return carry
+
+    lax.fori_loop(0, 2 * lines, project, 0)
+    for other in sum_branch.others():
+        sum_branch.pass_on(other)
+    middle = tokens[me].astype(F32) + vectors[0:1]
+    middle = middle + sum_branch.total()
+    scaled, inverse = normed(middle)
+    n2[me] = (scaled * vectors[1:2] + vectors[2:3]).astype(LOW)
+    all_n2.start()
+    held[0] = middle
+    held[1] = scaled
+    spread[...] = jnp.broadcast_to(inverse, spread.shape)
+    fc1_bias_out[...] = jnp.zeros_like(fc1_bias_out)
+    in_fc1.wait()
+    in_fc2.wait()
+
+    def hidden_part(k, carry):
+        at = lax.rem(line + k, lines)
+
+        @pl.when(k > 0)
+        def _():
+            all_n2.forward(at)
+
+        all_n2.take(at)
+        pair = pl.ds(at * 2, 2)
+        inputs = n2[pair].reshape(2 * share, width)
+        pulls = cot[pair].reshape(2 * share, width)
+
+        def tile(n, inner):
+            span = pl.ds(pl.multiple_of(n * step, step), step)
+            up = nn(inputs, fc1[:, span]) + fc1_bias[:, span]
+            phi = 0.5 + 0.5 * lax.erf(up * math.sqrt(0.5))
+            slope = phi + up * (jnp.exp(-0.5 * up * up) * (2 * math.pi) ** -0.5)
+            act[pair, :, span] = (up * phi).astype(LOW).reshape(2, share, step)
+            grad_up = (nt(pulls, fc2[span, :]) * slope).astype(LOW)
+            gu[pair, :, span] = grad_up.reshape(2, share, step)
+            fc1_bias_out[:, span] += jnp.sum(grad_up.astype(F32), axis=0, keepdims=True)
+            return inner
+
+        lax.fori_loop(0, hidden // step, tile, 0)
+
+        def tile_back(n, inner):
+            span = pl.ds(pl.multiple_of(n * dstep, dstep), dstep)
+            found = nt(gu[pair].reshape(2 * share, hidden), fc1[span, :])
+            back[pair, :, span] = found.astype(LOW).reshape(2, share, dstep)
+            return inner
+
+        lax.fori_loop(0, width // dstep, tile_back, 0)
+        sum_back.give(at)
+
+        def tile_out(n, inner):
+            span = pl.ds(pl.multiple_of(n * dstep, dstep), dstep)
+            found = nn(act[pair].reshape(2 * share, hidden), fc2[:, span])
+            mlp[pair, :, span] = found.astype(LOW).reshape(2, share, dstep)
+            return inner
+
+        lax.fori_loop(0, width // dstep, tile_out, 0)
+        sum_mlp.give(at)
+        return carry
+
+    lax.fori_loop(0, lines, hidden_part, 0)
+    for other in sum_back.others():
+        sum_back.pass_on(other)
+    for other in sum_mlp.others():
+        sum_mlp.pass_on(other)
+
+    def weights2(n, carry):
+        span = pl.ds(pl.multiple_of(n * dstep, dstep), dstep)
+        found = tn(cot[:, :, span].reshape(rows, dstep), act[...].reshape(rows, hidden))
+        fc2_out[span, :] = found.astype(LOW)
+        return carry
+
+    lax.fori_loop(0, width // dstep, weights2, 0)
+    upstream = sum_back.total()
+    sums_out[0:1] = jnp.sum(upstream * held[1], axis=0, keepdims=True)
+    sums_out[1:2] = jnp.sum(upstream, axis=0, keepdims=True)
+    grad_middle = cot[me].astype(F32) + normed_back(
+        upstream, held[1], spread[:, :1], vectors[1:2]
+    )
+    middle_out[...] = grad_middle
+    gb[me] = grad_middle.astype(LOW)
+    all_gb.start()
+    outs[me] = (held[0] + sum_mlp.total() + vectors[3:4]).astype(LOW)
+    all_out.start()
+
+    def weights1(n, carry):
+        span = pl.ds(pl.multiple_of(n * dstep, dstep), dstep)
+        found = tn(n2[:, :, span].reshape(rows, dstep), gu[...].reshape(rows, hidden))
+        fc1_out[span, :] = found.astype(LOW)
+        return carry
+
+    lax.fori_loop(0, width // dstep, weights1, 0)
+    sums_out[2:3] = jnp.sum(cot[...].astype(F32).reshape(rows, width), axis=0, keepdims=True)
+    for other in all_gb.others():
+        all_gb.forward(other)
+    for other in all_out.others():
+        all_out.forward(other)
+    all_gb.take(line)
+    for other in all_gb.others():
+        all_gb.take(other)
+    whole = gb[...].reshape(rows, width)
+    sums_out[3:4] = jnp.sum(whole.astype(F32), axis=0, keepdims=True)
+    ga_out[...] = nt(proj_w[...], whole).astype(LOW)
+
+    def weights0(n, carry):
+        span = pl.ds(pl.multiple_of(n * dstep, dstep), dstep)
+        found = tn(gb[:, :, span].reshape(rows, dstep), att_tok[...].reshape(rows, -1))
+        proj_out[span, :] = found.astype(LOW)
+        return carry
+
+    lax.fori_loop(0, width // dstep, weights0, 0)
+    branch_out[...] = gb[...]
+    all_out.take(line)
+    for other in all_out.others():
+        all_out.take(other)
+    output[...] = outs[...]
+    for each in (sum_branch, sum_mlp, sum_back, all_n2, all_gb, all_out):
+        each.finish()
+
+
+def middle_block(att, proj_w, tokens, cot, fc1, fc2, fc1_bias, vectors):
+    count = lax.axis_size("tensor")
+    lines = count // 2
+    local, width = proj_w.shape
+    rows = tokens.shape[0]
+    share = rows // count
+    hidden = fc1.shape[1]
+    vmem = pl.BlockSpec(memory_space=pltpu.VMEM)
+    hbm = pl.BlockSpec(memory_space=pl.ANY)
+    dma = pltpu.SemaphoreType.DMA
+    whole = (count, share, width)
+    scratch = [
+        pltpu.VMEM((width, hidden), LOW),
+        pltpu.VMEM((hidden, width), LOW),
+        pltpu.VMEM((count, share, local), LOW),
+        pltpu.VMEM(whole, LOW),
+        pltpu.VMEM(whole, LOW),
+        pltpu.VMEM(whole, LOW),
+        pltpu.VMEM(whole, LOW),
+        pltpu.VMEM((count, share, hidden), LOW),
+        pltpu.VMEM((count, share, hidden), LOW),
+        pltpu.VMEM(whole, LOW),
+        pltpu.VMEM(whole, LOW),
+        pltpu.VMEM((2, share, width), F32),
+        pltpu.VMEM((share, 128), F32),
+        dma,
+        dma,
+    ]
+    scratch += part_bufs(lines, share, width) * 3 + gather_sems(lines) * 3
+    return pl.pallas_call(
+        middle_kernel,
+        out_shape=(
+            jax.ShapeDtypeStruct(whole, LOW),
+            jax.ShapeDtypeStruct(whole, LOW),
+            jax.ShapeDtypeStruct((share, width), F32),
+            jax.ShapeDtypeStruct((width, hidden), LOW),
+            jax.ShapeDtypeStruct((width, hidden), LOW),
+            jax.ShapeDtypeStruct((width, local), LOW),
+            jax.ShapeDtypeStruct((local, rows), LOW),
+            jax.ShapeDtypeStruct((1, hidden), F32),
+            jax.ShapeDtypeStruct((8, width), F32),
+        ),
+        in_specs=[vmem] * 4 + [hbm] * 2 + [vmem] * 2,
+        out_specs=(vmem,) * 9,
+        scratch_shapes=scratch,
+        compiler_params=pltpu.CompilerParams(
+            collective_id=3, has_side_effects=True, vmem_limit_bytes=VMEM_LIMIT
+        ),
+        name="middle",
+    )(
+        att, proj_w, tokens.reshape(whole), cot.reshape(whole), fc1, fc2,
+        fc1_bias.reshape(1, hidden), vectors,
+    )
+
+
+def greet_tensor():
+    peers = tensor_peers()
+    barrier = pltpu.get_barrier_semaphore()
+    for peer in peers:
+        pl.semaphore_signal(barrier, inc=1, device_id={"tensor": peer}, device_id_type=MESH)
+    pl.semaphore_wait(barrier, len(peers))
+
+
+class Ring:
+    def __init__(self, heads):
+        self.heads, self.group = heads, lax.axis_size("dp") // heads
+        me = lax.axis_index("dp")
+        self.z, self.g = me // self.group, lax.rem(me, self.group)
+
+    def column(self):
+        return [lax.rem(self.z + k, self.heads) for k in range(1, self.heads)]
+
+    def mates(self):
+        return [lax.rem(self.g + k, self.group) for k in range(1, self.group)]
+
+    def peers(self):
+        far = [h * self.group + self.g for h in self.column()]
+        return far + [self.z * self.group + o for o in self.mates()]
+
+
+def greet_all(ring):
+    barrier = pltpu.get_barrier_semaphore()
+    near, far = tensor_peers(), ring.peers()
+    for peer in near:
+        pl.semaphore_signal(barrier, inc=1, device_id={"tensor": peer}, device_id_type=MESH)
+    for peer in far:
+        pl.semaphore_signal(barrier, inc=1, device_id={"dp": peer}, device_id_type=MESH)
+    pl.semaphore_wait(barrier, len(near) + len(far))
+
+
+def scatter_bufs(heads, share, width):
+    group = lax.axis_size("dp") // heads
+    dma = pltpu.SemaphoreType.DMA
+    block = (heads, share, width)
+    return [
+        pltpu.VMEM(block, LOW), pltpu.VMEM((group,) + block, LOW), pltpu.VMEM(block, LOW),
+        pltpu.VMEM(block, LOW), dma((heads, group)), dma((heads, group)),
+        dma((heads,)), dma((heads,)), dma((heads,)),
+    ]
+
+
+SCATTER_BUFS = 9
+
+
+class Scatter:
+    def __init__(self, ring, source, mine, mate_in, passed, far_in, m_send, m_recv, f_send, f_recv, load):
+        self.ring, self.source, self.mine = ring, source, mine
+        self.mate_in, self.passed, self.far_in = mate_in, passed, far_in
+        self.sems = m_send, m_recv, f_send, f_recv, load
+
+    def load_copy(self, at):
+        ring = self.ring
+        return pltpu.make_async_copy(
+            self.source.at[at * ring.group + ring.g], self.mine.at[at], self.sems[4].at[at]
+        )
+
+    def mate_copy(self, at, mate, slot):
+        ring = self.ring
+        return send_dp(
+            self.source.at[at * ring.group + mate], self.mate_in.at[slot, at],
+            self.sems[0].at[at, mate], self.sems[1].at[at, slot], ring.z * ring.group + mate,
+        )
+
+    def far_copy(self, at, slot):
+        ring = self.ring
+        return send_dp(
+            self.passed.at[at], self.far_in.at[slot], self.sems[2].at[at], self.sems[3].at[slot],
+            at * ring.group + ring.g,
+        )
+
+    def give(self, at):
+        self.load_copy(at).start()
+        for mate in self.ring.mates():
+            self.mate_copy(at, mate, self.ring.g).start()
+
+    def give_all(self):
+        for at in self.ring.column() + [self.ring.z]:
+            self.give(at)
+
+    def near_sum(self, at):
+        self.load_copy(at).wait()
+        total = self.mine[at].astype(F32)
+        for mate in self.ring.mates():
+            self.mate_copy(at, mate, mate).wait_recv()
+            total = total + self.mate_in[mate, at].astype(F32)
+        return total
+
+    def pass_on(self, at):
+        self.passed[at] = self.near_sum(at).astype(LOW)
+        self.far_copy(at, self.ring.z).start()
+
+    def pass_all(self):
+        def step(k, carry):
+            self.pass_on(lax.rem(self.ring.z + k, self.ring.heads))
+            return carry
+
+        lax.fori_loop(1, self.ring.heads, step, 0)
+
+    def total(self):
+        total = self.near_sum(self.ring.z)
+        for other in self.ring.column():
+            self.far_copy(other, other).wait_recv()
+            total = total + self.far_in[other].astype(F32)
+        return total
+
+    def finish(self):
+        for at in self.ring.column() + [self.ring.z]:
+            for mate in self.ring.mates():
+                self.mate_copy(at, mate, self.ring.g).wait_send()
+        for other in self.ring.column():
+            self.far_copy(other, self.ring.z).wait_send()
+
+
+def small_bufs(heads, stages, shape):
+    group, lines = lax.axis_size("dp") // heads, lax.axis_size("tensor") // 2
+    dma = pltpu.SemaphoreType.DMA
+    found = []
+    for stage in stages:
+        count = {"core": 2, "line": lines, "mate": group, "far": heads}[stage]
+        found += [
+            pltpu.VMEM(shape, F32), pltpu.VMEM((count,) + shape, F32), dma((count,)), dma((count,))
+        ]
+    return found
+
+
+class Small:
+    def __init__(self, ring, stages, merge, *bufs):
+        self.ring, self.stages, self.merge = ring, stages, merge
+        self.bufs = [bufs[4 * n : 4 * n + 4] for n in range(len(stages))]
+        core, line, lines = tensor_place()
+        self.peers = {
+            "core": (core, [(1 - core, line * 2 + 1 - core)]),
+            "line": (line, [(o, o * 2 + core) for o in [lax.rem(line + k, lines) for k in range(1, lines)]]),
+            "mate": (ring.g, [(o, ring.z * ring.group + o) for o in ring.mates()]),
+            "far": (ring.z, [(o, o * ring.group + ring.g) for o in ring.column()]),
+        }
+
+    def copy(self, n, slot, other, dev):
+        value, held, send, recv = self.bufs[n]
+        call = send_tensor if self.stages[n] in ("core", "line") else send_dp
+        return call(value, held.at[slot], send.at[other], recv.at[slot], dev)
+
+    def start(self, n, value):
+        own, peers = self.peers[self.stages[n]]
+        self.bufs[n][0][...] = value
+        for other, dev in peers:
+            self.copy(n, own, other, dev).start()
+
+    def take(self, n):
+        _, peers = self.peers[self.stages[n]]
+        total = self.bufs[n][0][...]
+        for other, dev in peers:
+            self.copy(n, other, other, dev).wait_recv()
+            total = self.merge(total, self.bufs[n][1][other])
+        return total
+
+    def run(self, upto=None):
+        for n in range(len(self.stages)):
+            value = self.take(n)
+            if n + 1 < len(self.stages):
+                self.start(n + 1, value)
+        return value
+
+    def finish(self):
+        for n in range(len(self.stages)):
+            own, peers = self.peers[self.stages[n]]
+            for other, dev in peers:
+                self.copy(n, own, other, dev).wait_send()
+
+
+EVERY = ("core", "line", "mate", "far")
+OVER_DP = ("mate", "far")
+
+
+def add_peaks(a, b):
+    row = lax.broadcasted_iota(jnp.int32, a.shape, 0)
+    return jnp.where(row == 2, jnp.maximum(a, b), a + b)
+
+
+def widen(row, width):
+    if row.shape[1] == width:
+        return row
+    return jnp.concatenate([row, jnp.zeros((1, width - row.shape[1]), F32)], axis=1)
+
+
+def tail_kernel(
+    heads, grads, qkv_w, n1_t, tokens, grad_middle, vectors, tables, sums, fc1_bias, peak,
+    fc1, fc2, proj,
+    tokens_out, fc1_out, fc2_out, proj_out, qkv_out, tables_out, sums_out, late_out, dp_out,
+    g_all, g_tok, part, gt, gq, *rest,
+):
+    ring = Ring(heads)
+    core, line, lines = tensor_place()
+    me = lax.axis_index("tensor")
+    count, share, width = tokens.shape
+    rows = count * share
+    local = heads * HEAD
+    dstep = tile_of(width)
+    rest = list(rest)
+
+    def taken(number):
+        found, rest[:] = rest[:number], rest[number:]
+        return found
+
+    greet_all(ring)
+    moved2 = Scatter(ring, fc2, *taken(SCATTER_BUFS))
+    moved1 = Scatter(ring, fc1, *taken(SCATTER_BUFS))
+    moved0 = Scatter(ring, proj, *taken(SCATTER_BUFS))
+    moved3 = Scatter(ring, gq, *taken(SCATTER_BUFS))
+    sum_part = Reduce(part, *taken(7))
+    all_gt = Gather(gt, *taken(3))
+    small_tables = Small(ring, EVERY, lax.add, *taken(16))
+    small_sums = Small(ring, EVERY, lax.add, *taken(16))
+    small_late = Small(ring, EVERY, lax.add, *taken(16))
+    small_dp = Small(ring, OVER_DP, add_peaks, *taken(8))
+    moved2.give_all()
+    moved1.give_all()
+    moved0.give_all()
+    small_tables.start(0, tables[...].reshape(4 * SIDE, 128))
+    small_sums.start(0, sums[...])
+    for t in range(3):
+        for h in range(heads):
+            g_all[pl.ds(t * local + h * HEAD, HEAD), :] = grads[h, t]
+    g_tok[...] = g_all[...].T.reshape(g_tok.shape)
+    whole = g_tok[...].reshape(rows, 3 * local)
+    lane = lax.broadcasted_iota(jnp.int32, (1, width), 1)
+    peaks = jnp.where(lane == ring.z, peak[0:1, 0:1], -jnp.inf)
+    bias_sums = jnp.sum(whole.astype(F32), axis=0, keepdims=True)
+    dp_rows = [widen(fc1_bias[...], width), widen(bias_sums, width), peaks]
+    small_dp.start(0, jnp.concatenate(dp_rows + [jnp.zeros((5, width), F32)], axis=0))
+
+    def norm_part(k, carry):
+        at = lax.rem(line + 1 + k, lines)
+        pair = pl.ds(at * 2, 2)
+
+        def tile(n, inner):
+            span = pl.ds(pl.multiple_of(n * dstep, dstep), dstep)
+            found = nt(g_tok[pair].reshape(2 * share, 3 * local), qkv_w[span, :])
+            part[pair, :, span] = found.astype(LOW).reshape(2, share, dstep)
+            return inner
+
+        lax.fori_loop(0, width // dstep, tile, 0)
+        sum_part.give(at)
+        return carry
+
+    lax.fori_loop(0, lines, norm_part, 0)
+    for other in sum_part.others():
+        sum_part.pass_on(other)
+
+    def weight_part(k, carry):
+        at = lax.rem(ring.z + 1 + k // ring.group, heads)
+        dev = at * ring.group + lax.rem(ring.g + 1 + lax.rem(k, ring.group), ring.group)
+        gq[dev] = nn(n1_t[dev], g_tok[...].reshape(rows, 3 * local)).astype(LOW)
+
+        @pl.when(lax.rem(k, ring.group) == ring.group - 1)
+        def _():
+            moved3.give(at)
+
+        return carry
+
+    lax.fori_loop(0, heads * ring.group, weight_part, 0)
+    scaled, inverse = normed(tokens[me].astype(F32))
+    upstream = sum_part.total()
+    late = [
+        jnp.sum(upstream * scaled, axis=0, keepdims=True),
+        jnp.sum(upstream, axis=0, keepdims=True),
+        jnp.zeros((6, width), F32),
+    ]
+    small_late.start(0, jnp.concatenate(late, axis=0))
+    found = grad_middle[...] + normed_back(upstream, scaled, inverse, vectors[0:1])
+    gt[me] = found.astype(LOW)
+    all_gt.start()
+    moved2.pass_all()
+    for other in all_gt.others():
+        all_gt.forward(other)
+    dp_out[...] = small_dp.run()
+    sums_out[...] = small_sums.run()
+    moved1.pass_all()
+    tables_out[...] = small_tables.run()
+    moved0.pass_all()
+    all_gt.take(line)
+    for other in all_gt.others():
+        all_gt.take(other)
+    tokens_out[...] = gt[...]
+    late_out[...] = small_late.run()
+    moved3.pass_all()
+    fc2_out[...] = moved2.total().T
+    fc1_out[...] = moved1.total()
+    proj_out[...] = moved0.total().T
+    qkv_out[...] = moved3.total()
+    for each in (
+        moved0, moved1, moved2, moved3, sum_part, all_gt,
+        small_tables, small_sums, small_late, small_dp,
+    ):
+        each.finish()
+
+
+def tail(heads, grads, qkv_w, n1_t, tokens, grad_middle, vectors, tables, sums, fc1_bias, peak, fc1, fc2, proj):
+    count = lax.axis_size("tensor")
+    lines = count // 2
+    local = heads * HEAD
+    devices, owned, rows = n1_t.shape
+    width = devices * owned
+    share = rows // count
+    hidden = fc1.shape[1]
+    vmem = pl.BlockSpec(memory_space=pltpu.VMEM)
+    hbm = pl.BlockSpec(memory_space=pl.ANY)
+    whole = (count, share, width)
+    scratch = [
+        pltpu.VMEM((3 * local, rows), LOW),
+        pltpu.VMEM((count, share, 3 * local), LOW),
+        pltpu.VMEM(whole, LOW),
+        pltpu.VMEM(whole, LOW),
+        pltpu.VMEM((devices, owned, 3 * local), LOW),
+    ]
+    for columns in (hidden, hidden, local, 3 * local):
+        scratch += scatter_bufs(heads, owned, columns)
+    scratch += part_bufs(lines, share, width) + gather_sems(lines)
+    scratch += small_bufs(heads, EVERY, (4 * SIDE, 128))
+    scratch += small_bufs(heads, EVERY, (8, width)) * 2
+    scratch += small_bufs(heads, OVER_DP, (8, width))
+    return pl.pallas_call(
+        functools.partial(tail_kernel, heads),
+        out_shape=(
+            jax.ShapeDtypeStruct(whole, LOW),
+            jax.ShapeDtypeStruct((owned, hidden), F32),
+            jax.ShapeDtypeStruct((hidden, owned), F32),
+            jax.ShapeDtypeStruct((local, owned), F32),
+            jax.ShapeDtypeStruct((owned, 3 * local), F32),
+            jax.ShapeDtypeStruct((4 * SIDE, 128), F32),
+            jax.ShapeDtypeStruct((8, width), F32),
+            jax.ShapeDtypeStruct((8, width), F32),
+            jax.ShapeDtypeStruct((8, width), F32),
+        ),
+        in_specs=[vmem] * 10 + [hbm] * 3,
+        out_specs=(vmem,) * 9,
+        scratch_shapes=scratch,
+        compiler_params=pltpu.CompilerParams(
+            collective_id=4, has_side_effects=True, vmem_limit_bytes=VMEM_LIMIT
+        ),
+        name="tail",
+    )(
+        grads, qkv_w, n1_t, tokens.reshape(whole), grad_middle, vectors, tables, sums, fc1_bias, peak,
+        fc1.reshape(devices, owned, hidden), fc2.reshape(devices, owned, hidden),
+        proj.reshape(devices, owned, local),
+    )
 
 
 def on_device(
@@ -558,11 +1234,9 @@
     local_width = qkv_weight.shape[2]
     local_heads = local_width // HEAD
     groups = lax.axis_size("tensor")
-    share_rows = token_count // groups
-    share_base = lax.axis_index("tensor") * share_rows
     residual_in = tokens.reshape(token_count, model_width).astype(jnp.float32)
-    normed1, scaled1, inverse1 = norm_forward(residual_in, norm1_gain, norm1_shift)
-    normed1_low = normed1.astype(jnp.bfloat16)
+    scaled1, _ = normed(residual_in)
+    normed1_low = (scaled1 * norm1_gain + norm1_shift).astype(jnp.bfloat16)
     shape = Shape(local_heads, lax.axis_size("dp") // local_heads, row_count)
     flipped = jnp.stack([table_rows, table_cols])[:, ::-1]
     flipped = jnp.pad(flipped, ((0, 0), (0, 1), (0, 0)))
@@ -571,101 +1245,71 @@
     triple = (triple + bias[:, :, None]).astype(jnp.bfloat16)
     qkv = triple.reshape(3, local_heads, HEAD, row_count).transpose(1, 0, 2, 3)
     attended, qaug, bias_rows, kv, o_rows, lse, peak = attend(shape, qkv, flipped)
-    attended_flat = attended.reshape(local_width, token_count)
-    branch_part = jnp.einsum(
-        "cn,cd->nd", attended_flat, proj_weight, preferred_element_type=jnp.float32
+    grad_out = cotangent.reshape(token_count, model_width)
+    vectors = jnp.stack([proj_bias, norm2_gain, norm2_shift, fc2_bias])
+    vectors = jnp.pad(vectors, ((0, 4), (0, 0)))
+    (
+        output,
+        grad_branch,
+        grad_middle,
+        grad_fc1,
+        grad_fc2,
+        grad_proj,
+        grad_attended,
+        grad_fc1_bias,
+        sums,
+    ) = middle_block(
+        attended.reshape(local_width, token_count),
+        proj_weight,
+        tokens.reshape(token_count, model_width),
+        grad_out,
+        fc1_weight,
+        fc2_weight,
+        fc1_bias,
+        vectors,
     )
-    middle_rows = residual_in + full_sum(branch_part) + proj_bias
-    normed2, scaled2, inverse2 = norm_forward(middle_rows, norm2_gain, norm2_shift)
-    normed2_low = normed2.astype(jnp.bfloat16)
-    up_value = jnp.dot(normed2_low, fc1_weight, preferred_element_type=jnp.float32) + fc1_bias
-    activated, gelu_pull = jax.vjp(exact_gelu, up_value)
-    activated_low = activated.astype(jnp.bfloat16)
-    mlp_part = jnp.dot(activated_low, fc2_weight, preferred_element_type=jnp.float32)
-    output = (middle_rows + (full_sum(mlp_part) + fc2_bias)).astype(jnp.bfloat16)
-    grad_out = cotangent.reshape(token_count, model_width)
-    grad_out_f = grad_out.astype(jnp.float32)
-    grad_fc2 = jnp.einsum("nf,nd->fd", activated_low, grad_out, preferred_element_type=jnp.float32)
-    grad_fc2_bias = jnp.sum(grad_out_f, axis=0)
-    grad_activated = jnp.einsum(
-        "nd,fd->nf", grad_out, fc2_weight, preferred_element_type=jnp.float32
-    )
-    grad_up = gelu_pull(grad_activated)[0].astype(jnp.bfloat16)
-    grad_fc1 = jnp.einsum("nd,nf->df", normed2_low, grad_up, preferred_element_type=jnp.float32)
-    grad_fc1_bias = jnp.sum(grad_up.astype(jnp.float32), axis=0)
-    normed2_part = jnp.einsum("nf,df->nd", grad_up, fc1_weight, preferred_element_type=jnp.float32)
-    grad_normed2 = full_sum(normed2_part)
-    grad_norm2_gain, grad_norm2_shift = gain_terms(
-        rows_of(grad_normed2, share_base, share_rows), rows_of(scaled2, share_base, share_rows)
-    )
-    grad_middle = grad_out_f + norm_backward(grad_normed2, scaled2, inverse2, norm2_gain)
-    grad_branch = grad_middle.astype(jnp.bfloat16)
-    grad_proj = jnp.einsum(
-        "cn,nd->cd", attended_flat, grad_branch, preferred_element_type=jnp.float32
-    )
-    grad_proj_bias = jnp.sum(grad_branch.astype(jnp.float32), axis=0)
-    grad_attended = jnp.einsum(
-        "cd,nd->cn", proj_weight, grad_branch, preferred_element_type=jnp.float32
-    ).astype(jnp.bfloat16)
     grad_heads = grad_attended.reshape(local_heads, HEAD, row_count)
     grad_triple, table_terms = attend_back(
         shape, grad_heads, flipped, qaug, bias_rows, kv, o_rows, lse
     )
-    grad_triple = grad_triple.transpose(1, 0, 2, 3).reshape(3, local_width, token_count)
-    grad_qkv = jnp.einsum(
-        "nd,tcn->dtc", normed1_low, grad_triple, preferred_element_type=jnp.float32
+    devices = lax.axis_size("dp")
+    tail_vectors = jnp.pad(norm1_gain[None], ((0, 7), (0, 0)))
+    (
+        grad_tokens,
+        grad_fc1,
+        grad_fc2,
+        grad_proj,
+        grad_qkv,
+        table_sums,
+        sums,
+        late,
+        dp_sums,
+    ) = tail(
+        local_heads,
+        grad_triple,
+        qkv_weight.reshape(model_width, 3 * local_width),
+        normed1_low.T.reshape(devices, model_width // devices, token_count),
+        tokens.reshape(token_count, model_width),
+        grad_middle,
+        tail_vectors,
+        table_terms,
+        sums,
+        grad_fc1_bias,
+        peak,
+        grad_fc1,
+        grad_fc2,
+        grad_proj,
     )
-    grad_qv_bias = jnp.sum(grad_triple[0::2].astype(jnp.float32), axis=2)
-    normed1_part = jnp.einsum(
-        "tcn,dtc->nd", grad_triple, qkv_weight, preferred_element_type=jnp.float32
-    )
-    grad_normed1 = full_sum(normed1_part)
-    grad_norm1_gain, grad_norm1_shift = gain_terms(
-        rows_of(grad_normed1, share_base, share_rows), rows_of(scaled1, share_base, share_rows)
-    )
-    from_norm1 = norm_backward(grad_normed1, scaled1, inverse1, norm1_gain)
-    grad_tokens = (grad_middle + from_norm1).astype(jnp.bfloat16)
     grad_tokens = grad_tokens.reshape(images, row_count, model_width)
-    grad_qkv, grad_proj, grad_fc1, grad_fc2 = (
-        lax.psum_scatter(
-            grad_qkv.astype(jnp.bfloat16), "dp", scatter_dimension=0, tiled=True
-        ).astype(jnp.float32),
-        lax.psum_scatter(
-            grad_proj.astype(jnp.bfloat16), "dp", scatter_dimension=1, tiled=True
-        ).astype(jnp.float32),
-        lax.psum_scatter(
-            grad_fc1.astype(jnp.bfloat16), "dp", scatter_dimension=0, tiled=True
-        ).astype(jnp.float32),
-        lax.psum_scatter(
-            grad_fc2.astype(jnp.bfloat16), "dp", scatter_dimension=1, tiled=True
-        ).astype(jnp.float32),
-    )
-    grad_proj_bias, grad_fc2_bias, grad_qv_bias, grad_fc1_bias = lax.psum(
-        (grad_proj_bias, grad_fc2_bias, grad_qv_bias, grad_fc1_bias), "dp"
-    )
-    table_terms = table_terms[:, 2 * SIDE - 2 :: -1, :HEAD]
-    rows_term, cols_term = table_terms[0], table_terms[1]
-    own_head = jnp.arange(local_heads) == lax.axis_index("dp") // shape.group
-    local_peaks = jnp.where(own_head, peak[0, 0], -jnp.inf)
-    head_peaks = lax.pmax(local_peaks, "dp")
-    (
-        grad_table_rows,
-        grad_table_cols,
-        grad_norm1_gain,
-        grad_norm1_shift,
-        grad_norm2_gain,
-        grad_norm2_shift,
-    ) = lax.psum(
-        (
-            rows_term,
-            cols_term,
-            grad_norm1_gain,
-            grad_norm1_shift,
-            grad_norm2_gain,
-            grad_norm2_shift,
-        ),
-        ("dp", "tensor"),
-    )
+    grad_qkv = grad_qkv.reshape(model_width // devices, 3, local_width)
+    table_sums = table_sums.reshape(2, 2 * SIDE, 128)[:, 2 * SIDE - 2 :: -1, :HEAD]
+    grad_table_rows, grad_table_cols = table_sums[0], table_sums[1]
+    grad_norm2_gain, grad_norm2_shift = sums[0], sums[1]
+    grad_fc2_bias, grad_proj_bias = sums[2] / groups, sums[3] / groups
+    grad_norm1_gain, grad_norm1_shift = late[0], late[1]
+    grad_fc1_bias = dp_sums[0, : fc1_bias.shape[0]]
+    grad_qv_bias = dp_sums[1, : 3 * local_width].reshape(3, local_width)[0::2]
+    head_peaks = dp_sums[2, :local_heads]
     limit = threshold[0]
     clip_factors = jnp.sqrt(limit / jnp.maximum(head_peaks, limit))
     spread_factors = jnp.repeat(clip_factors, HEAD)

time: 752 us -> 438 us (0.58)
  waiting for transfers between devices: 465 us -> 0 us
  Pallas kernels: 114 us -> 394 us
  blocking collectives: 55.1 us -> 0 us
  matrix products: 47.7 us -> 3.35 us
  other arithmetic: 34 us -> 9.4 us
  between operations: 15.2 us -> 1.61 us
    reduce_scatter x4 -> x0, waiting for transfers between devices: 293 us -> none  [the longest x1 77.2 us: on_device(): lax.psum_scatter(grad_fc1.astype(jnp.bfloat16), 'dp', scatter_dimension=0...]
    pallas_call x0 -> x2, Pallas kernels: none -> 280 us  [the longest x1 212 us: tail(): pl.pallas_call(functools.partial(tail_kernel, heads), out_shape=(jax.Shap...]
    psum x4 -> x0, waiting for transfers between devices: 173 us -> none  [the longest x3 130 us: full_sum(): return lax.psum(values.astype(jnp.bfloat16), 'tensor').astype(jnp.float32)]
    dot_general x11 -> x0, matrix products: 43.9 us -> none  [the longest x1 8.19 us: on_device(): jnp.dot(normed2_low, fc1_weight, preferred_element_type=jnp.float32)]
    psum x1 -> x0, blocking collectives: 33.7 us -> none  [on_device(): lax.psum((grad_proj_bias, grad_fc2_bias, grad_qv_bias, grad_fc1_bias), 'dp')]
    pmax x1 -> x0, blocking collectives: 21.4 us -> none  [on_device(): head_peaks = lax.pmax(local_peaks, 'dp')]
    reduce_sum x10 -> x2, other arithmetic: 14.6 us -> 3.36 us  [the longest x1 1.8 us: normed(): variance = jnp.mean(center * center, axis=-1, keepdims=True)]
    convert_element_type x6 -> x0, other arithmetic: 9.18 us -> none  [the longest x4 7.4 us: on_device(): grad_qkv, grad_proj, grad_fc1, grad_fc2 = (lax.psum_scatter(grad_qkv.asty...]
  transfers between devices with their start and end apart: 8 -> 0, of which waited for: 8 -> 0; matrix products, arithmetic and copies ran while one was open for 6% -> 0% of each run, Pallas kernels for 0% -> 0%
where the time goes in v2:
time: 438 us; the launch traced here: 435 us
  Pallas kernels  394 us (90%)
  local copies, waits for them, and re-layouts  26 us (6%)
  other arithmetic  9.4 us (2%)
    pallas_call x1, Pallas kernels, tail(): pl.pallas_call(functools.partial(tail_kernel, heads), out_shape=(jax.Shap...  212 us
    pallas_call x1, Pallas kernels, middle_block(): pl.pallas_call(middle_kernel, out_shape=(jax.ShapeDtypeStruct(whole, LOW)...  68.9 us
    pallas_call x1, Pallas kernels, attend(): pl.pallas_call(functools.partial(forward_kernel, shape), out_shape=(jax.S...  59.7 us
    pallas_call x1, Pallas kernels, attend_back(): pl.pallas_call(functools.partial(backward_kernel, shape), out_shape=(jax....  54.1 us
    unnamed x44, local copies, waits for them, and re-layouts  8.8 us

profile of v2, /device:TPU:0, one launch (start us, length us, event | category | flops | bytes accessed | tf_op | source)
XLA Modules:
  0.0 434.6 jit_solution(12302839363229805174)
XLA Ops:
  0.7 0.8 slice_reduce_fusion.6
  1.7 1.6 convert_reduce_fusion
  3.2 1.8 fusion.3
  5.1 3.3 add_convert_fusion
  8.5 1.0 copy.59
  10.8 59.7 %attend.1 = (bf16[4,80,512]{2,1,0:T(8,128)(2,1)}, bf16[240,2048]{1,0:T(8,128)(2,1)}, bf16[8,16,2048]{2,1,0:T(8,128)(2,1)}, bf16[4,2,2,80,512]{4,3,2,1,0:T(8,128)...) custom-call(bf16[4,3,80,512]{3,2,1,0:T(8,128)(2,1)} %bitcast.59, bf16[2,128,80]{2,1,0:T(8,128)(2,1)} %pad.12.tables), custom_call_target="tpu_custom_call" | custom-call | tf_op jit(solution)/shard_map/attend/pallas_call | solution.py:253
  71.9 68.9 %middle.1 = (bf16[4,128,1280]{2,1,0:T(8,128)(2,1)}, bf16[4,128,1280]{2,1,0:T(8,128)(2,1)}, f32[128,1280]{1,0:T(8,128)}, bf16[1280,1280]{1,0:T(8,128)(2,1)}, bf16...) custom-call(bf16[320,512]{1,0:T(8,128)(2,1)} %bitcast.67, ...), custom_call_target="tpu_custom_call" | custom-call | tf_op jit(solution)/shard_map/middle/pallas_call | solution.py:834
  140.8 54.1 %attend_back.1 = (bf16[4,3,80,512]{3,2,1,0:T(8,128)(2,1)}, f32[2,128,128]{2,1,0:T(8,128)}) custom-call(bf16[4,80,512]{2,1,0:T(8,128)(2,1)} %bitcast.68, bf16[2,128,80]{2,1,0:T(8,128)(2,1)} %pad.12.tables, bf16[240,2048]{1,0:T(8,128)(2,1)} %get-tuple-element.49.qaug_in, bf16[8,16,2048]{2,1,0:T(8,128)(2,1)} %get-tuple-element.50.bias_rows, ...), custom_call_target="tpu_custom_call" | custom-call | tf_op jit(solution)/shard_map/attend_back/pallas_call | solution.py:467
  194.9 4.6 %copy.50.qkv_w = bf16[1280,960]{1,0:T(8,128)(2,1)} copy(bf16[1280,960]{0,1:T(8,128)(2,1)} %bitcast.57) | data formatting | bytes 4915200 | tf_op jit(solution)/shard_map/reshape | solution.py:1290
  200.0 1.5 copy.49
  202.1 211.5 %tail.1 = (bf16[4,128,1280]{2,1,0:T(8,128)(2,1)}, f32[160,1280]{1,0:T(8,128)}, f32[1280,160]{1,0:T(8,128)}, f32[320,160]{1,0:T(8,128)}, f32[160,960]{1,0:T(8,128...) custom-call(bf16[4,3,80,512]{3,2,1,0:T(8,128)(2,1)} %get-tuple-element.54.grads, ...), custom_call_target="tpu_custom_call" | custom-call | tf_op jit(solution)/shard_map/tail/pallas_call | solution.py:1186
  413.7 1.5 slice_reduce_fusion.3
  415.2 1.5 reshape.113
  416.7 0.9 copy.53
  417.6 0.9 slice_reduce_fusion.5
  419.2 1.8 copy.54
  421.0 1.5 multiply_reduce_fusion
  422.4 0.9 fusion.10
  424.9 2.6 copy.55
  428.1 1.2 divide_sqrt_fusion
  429.5 1.5 multiply_convert_fusion
  431.6 1.1 copy.64
  432.6 1.1 copy.65
  433.7 0.9 copy.66
  (61 shorter events, 6.9 us)
Async XLA Ops:
  0.7 4.4 %copy-start = (bf16[1,512,1280]{2,1,0:T(8,128)(2,1)S(1)}, bf16[1,512,1280]{2,1,0:T(8,128)(2,1)}, u32[]{:S(2)}) copy-start(bf16[1,512,1280]{2,1,0:T(8,128)(2,1)} %param.17) | copy-start | bytes 3932164
  0.7 4.4 %copy-start.10 = (f32[1280]{0:T(1024)S(1)}, f32[1280]{0:T(1024)}, u32[]{:S(2)}) copy-start(f32[1280]{0:T(1024)} %param.20) | copy-start | bytes 15364
  0.7 4.4 %copy-start.6 = (f32[1280]{0:T(1024)S(1)}, f32[1280]{0:T(1024)}, u32[]{:S(2)}) copy-start(f32[1280]{0:T(1024)} %param.19) | copy-start | bytes 15364
  5.1 4.5 %copy-start.7 = (bf16[127,80]{0,1:T(8,128)(2,1)S(1)}, bf16[127,80]{0,1:T(8,128)(2,1)}, u32[]{:S(2)}) copy-start(bf16[127,80]{0,1:T(8,128)(2,1)} %param.26) | copy-start | bytes 60964
  5.1 4.6 %copy-start.8 = (bf16[127,80]{0,1:T(8,128)(2,1)S(1)}, bf16[127,80]{0,1:T(8,128)(2,1)}, u32[]{:S(2)}) copy-start(bf16[127,80]{0,1:T(8,128)(2,1)} %param.25) | copy-start | bytes 60964
  8.4 62.1 %copy-start.11 = (f32[1280]{0:T(1024)S(1)}, f32[1280]{0:T(1024)}, u32[]{:S(2)}) copy-start(f32[1280]{0:T(1024)} %param.30) | copy-start | bytes 15364
  8.5 62.7 %copy-start.12 = (f32[1280]{0:T(1024)S(1)}, f32[1280]{0:T(1024)}, u32[]{:S(2)}) copy-start(f32[1280]{0:T(1024)} %param.32) | copy-start | bytes 15364
  8.5 62.7 %copy-start.13 = (f32[1280]{0:T(1024)S(1)}, f32[1280]{0:T(1024)}, u32[]{:S(2)}) copy-start(f32[1280]{0:T(1024)} %param.28) | copy-start | bytes 15364
  8.5 62.7 %copy-start.14 = (f32[1280]{0:T(1024)S(1)}, f32[1280]{0:T(1024)}, u32[]{:S(2)}) copy-start(f32[1280]{0:T(1024)} %param.27) | copy-start | bytes 15364
  8.5 62.7 %copy-start.15 = (f32[1280]{0:T(1024)S(1)}, f32[1280]{0:T(1024)}, u32[]{:S(2)}) copy-start(f32[1280]{0:T(1024)} %param.24) | copy-start | bytes 15364
  194.8 4.6 %copy-start.1 = (bf16[1,512,1280]{2,1,0:T(8,128)(2,1)S(1)}, bf16[1,512,1280]{2,1,0:T(8,128)(2,1)}, u32[]{:S(2)}) copy-start(bf16[1,512,1280]{2,1,0:T(8,128)(2,1)} %param.17) | copy-start | bytes 3932164
  413.7 7.3 %copy-start.9 = (f32[8,1280]{1,0:T(8,128)S(1)}, f32[8,1280]{1,0:T(8,128)}, u32[]{:S(2)}) copy-start(f32[8,1280]{1,0:T(8,128)} %get-tuple-element.68) | copy-start | bytes 122884
  416.7 12.8 %copy-start.2 = (bf16[1280,3,320]{0,2,1:T(8,128)(2,1)S(1)}, bf16[1280,3,320]{0,2,1:T(8,128)(2,1)}, u32[]{:S(2)}) copy-start(bf16[1280,3,320]{0,2,1:T(8,128)(2,1)} %param.21) | copy-start | bytes 7372804
  429.3 3.3 copy-start.16
  429.5 2.1 copy-start.3
  429.5 3.1 copy-start.4
  431.6 2.1 copy-start.5

commit v3 on v2

--- a/solution.py
+++ b/solution.py
@@ -99,7 +99,7 @@
     def __init__(self, heads, group, rows):
         self.heads, self.group, self.rows = heads, group, rows
         self.queries = heads * rows
-        self.block = min(512, self.queries)
+        self.block = min(1024, self.queries)
 
 
 def forward_kernel(
@@ -286,11 +286,25 @@
 
 
 def backward_kernel(
-    shape, ga, tables, qaug_in, bias_rows, rkv, o_in, lse_in, grads, table_grads,
+    shape, ga, tables, qaug_in, bias_rows, rkv, o_in, lse_in, fc2_state, fc1, fc2,
+    grads, table_grads, fc1_out, fc2_out,
     rdo, qaug, q_tok, do_aug, do_tok, kaug_t, kaug, vaug_t, vaug, kacc, vacc, dq, drow, dcol,
     part, xr, summed, gq_s, gq_r, gkv_r,
-    d_send, d_recv, x_send, x_recv, kv_send, kv_recv, q_send, q_recv,
+    d_send, d_recv, x_send, x_recv, kv_send, kv_recv, q_send, q_recv, *rest,
 ):
+    chunks = fc1.shape[1]
+    rest = list(rest)
+
+    def taken(number):
+        found, rest[:] = rest[:number], rest[number:]
+        return found
+
+    whole_bufs = 2 + 3 * halve_bits()
+    moved2 = [Halve(near_first(), fc2_state, taken(3 * (halve_bits() - 1)), first=1)]
+    moved1 = [Halve(near_first(), fc1.at[:, 0], taken(whole_bufs), own=True)]
+    if chunks > 1:
+        moved2 += [Halve(near_first(), fc2.at[:, 1], taken(whole_bufs), own=True)]
+        moved1 += [Halve(far_first(shape.group), fc1.at[:, 1], taken(whole_bufs), own=True)]
     heads, group, rows, block = shape.heads, shape.group, shape.rows, shape.block
     queries = shape.queries
     me = lax.axis_index("dp")
@@ -303,6 +317,11 @@
         copy = send_dp(ga.at[h], rdo.at[z], d_send.at[h], d_recv.at[z], h * group + g)
         copy.start()
         sends.append(copy)
+    if chunks > 1:
+        moved2[1].start()
+        moved2[1].load()
+        moved1[1].load()
+    moved1[0].load()
     rdo[z] = ga[z]
     qaug[...] = qaug_in[...]
     ones = jnp.where(lax.broadcasted_iota(jnp.int32, (16, rows), 0) < 3, 1.0, 0.0).astype(LOW)
@@ -338,6 +357,9 @@
         return carry
 
     lax.fori_loop(0, heads, prepare, 0)
+    moved2[0].start()
+    if chunks > 1:
+        moved1[1].start()
 
     def chunk(source, mate):
         dev = source * group + mate
@@ -397,9 +419,18 @@
             return inner
 
         lax.fori_loop(1, group, mate_step, 0)
+
+        @pl.when(k == 2)
+        def _():
+            moved2[0].run(1)
+
         return carry
 
     lax.fori_loop(1, heads + 1, mates_step, 0)
+    moved1[0].start()
+    if chunks > 1:
+        moved2[1].loaded()
+        moved2[1].run(0)
 
     def own_step(k, carry):
         source = lax.rem(z + k, heads)
@@ -418,9 +449,22 @@
                 summed.at[source], gkv_r.at[z], kv_send.at[source], kv_recv.at[z], source * group + g
             ).start()
 
+        @pl.when(k == 1)
+        def _():
+            if chunks > 1:
+                moved1[1].loaded()
+                moved1[1].run(0)
+
+        @pl.when(k == 2)
+        def _():
+            if chunks > 1:
+                moved2[1].run(1)
+
         return carry
 
     lax.fori_loop(1, heads + 1, own_step, 0)
+    moved1[0].loaded()
+    moved1[0].run(0)
     table_grads[...] = jnp.zeros_like(table_grads)
 
     def finish(k, carry):
@@ -445,6 +489,20 @@
         return carry
 
     lax.fori_loop(1, heads + 1, finish, 0)
+    if chunks > 1:
+        moved1[1].run(1)
+    for other in range(2, halve_bits() - 1):
+        for each in moved2:
+            each.run(other)
+    found = [each.total() for each in moved2]
+    fc2_out[...] = (jnp.concatenate(found, axis=0) if chunks > 1 else found[0]).T
+    for other in range(1, halve_bits() - 1):
+        moved1[0].run(other)
+        if chunks > 1 and other > 1:
+            moved1[1].run(other)
+    owned = fc1_out.shape[0] // chunks
+    for n, each in enumerate(moved1):
+        fc1_out[pl.ds(n * owned, owned), :] = each.total()
     grads[z, 0] = gq_s[z]
     grads[z, pl.ds(1, 2)] = summed[z]
     for h in column:
@@ -458,9 +516,15 @@
     for source in range(heads):
         for mate in mates:
             mate_copy(source, mate).wait_send()
-
-
-def attend_back(shape, ga, tables, qaug, bias_rows, kv, o_rows, lse):
+    for each in moved1 + moved2:
+        each.finish()
+
+
+def attend_back(shape, ga, tables, qaug, bias_rows, kv, o_rows, lse, fc2_state, fc1, fc2):
+    devices, chunks, owned, hidden = fc1.shape
+    hbm = pl.BlockSpec(memory_space=pl.ANY)
+    moving = halve_bufs(owned, hidden, first=1)
+    moving += halve_bufs(owned, hidden, own=True) * (3 if chunks > 1 else 1)
     heads, group, rows, queries = shape.heads, shape.group, shape.rows, shape.queries
     vmem = pl.BlockSpec(memory_space=pltpu.VMEM)
     dma = pltpu.SemaphoreType.DMA
@@ -469,9 +533,11 @@
         out_shape=(
             jax.ShapeDtypeStruct((heads, 3, HEAD, rows), LOW),
             jax.ShapeDtypeStruct((2, 2 * SIDE, 128), F32),
+            jax.ShapeDtypeStruct((chunks * owned, hidden), F32),
+            jax.ShapeDtypeStruct((hidden, chunks * owned), F32),
         ),
-        in_specs=[vmem] * 7,
-        out_specs=(vmem, vmem),
+        in_specs=[vmem] * 8 + [hbm] * 2,
+        out_specs=(vmem,) * 4,
         scratch_shapes=[
             pltpu.VMEM((heads, HEAD, rows), LOW),
             pltpu.VMEM((AUG, queries), LOW),
@@ -495,12 +561,12 @@
             pltpu.VMEM((heads, 2, HEAD, rows), LOW),
             dma((heads,)), dma((heads,)), dma((heads, group)), dma((heads, group)),
             dma((heads,)), dma((heads,)), dma((heads,)), dma((heads,)),
-        ],
+        ] + moving,
         compiler_params=pltpu.CompilerParams(
             collective_id=2, has_side_effects=True, vmem_limit_bytes=VMEM_LIMIT
         ),
         name="attend_back",
-    )(ga, tables, qaug, bias_rows, kv, o_rows, lse)
+    )(ga, tables, qaug, bias_rows, kv, o_rows, lse, fc2_state, fc1, fc2)
 
 
 def send_tensor(src, dst, send_sem, recv_sem, dev):
@@ -647,29 +713,165 @@
     return 256 if width % 256 == 0 else 128
 
 
+class Ring:
+    def __init__(self, heads):
+        self.heads, self.group = heads, lax.axis_size("dp") // heads
+        me = lax.axis_index("dp")
+        self.z, self.g = me // self.group, lax.rem(me, self.group)
+
+    def column(self):
+        return [lax.rem(self.z + k, self.heads) for k in range(1, self.heads)]
+
+    def mates(self):
+        return [lax.rem(self.g + k, self.group) for k in range(1, self.group)]
+
+    def peers(self):
+        far = [h * self.group + self.g for h in self.column()]
+        return far + [self.z * self.group + o for o in self.mates()]
+
+
+def greet_all(ring):
+    barrier = pltpu.get_barrier_semaphore()
+    near, far = tensor_peers(), ring.peers()
+    for peer in near:
+        pl.semaphore_signal(barrier, inc=1, device_id={"tensor": peer}, device_id_type=MESH)
+    for peer in far:
+        pl.semaphore_signal(barrier, inc=1, device_id={"dp": peer}, device_id_type=MESH)
+    pl.semaphore_wait(barrier, len(near) + len(far))
+
+
+def halve_bits():
+    return (lax.axis_size("dp") - 1).bit_length()
+
+
+def near_first():
+    return tuple(range(halve_bits()))
+
+
+def far_first(group):
+    first = group.bit_length() - 1
+    return (first,) + tuple(bit for bit in range(halve_bits()) if bit != first)
+
+
+def halve_bufs(share, width, first=0, last=None, own=False):
+    bits = halve_bits()
+    last = bits - 1 if last is None else last
+    dma = pltpu.SemaphoreType.DMA
+    found = []
+    if own:
+        found += [pltpu.VMEM((1 << (bits - 1), share, width), LOW), dma]
+    for stage in range(first, last + 1):
+        count = 1 << (bits - 1 - stage)
+        found += [pltpu.VMEM((count, share, width), LOW), dma((count,)), dma((count,))]
+    return found
+
+
+class Halve:
+    def __init__(self, order, source, bufs, first=0, last=None, own=False):
+        self.order, self.source, self.first = order, source, first
+        self.last = len(order) - 1 if last is None else last
+        bufs = list(bufs)
+        self.own = bufs[0:2] if own else None
+        bufs = bufs[2:] if own else bufs
+        self.stages = {first + n: bufs[3 * n : 3 * n + 3] for n in range(len(bufs) // 3)}
+        self.me = lax.axis_index("dp")
+
+    def bit(self, stage):
+        return lax.rem(self.me // (1 << self.order[stage]), 2)
+
+    def count(self, stage):
+        return 1 << (len(self.order) - 1 - stage)
+
+    def index(self, stage, at, bit):
+        if stage > 0:
+            return at * 2 + bit
+        place = bit * (1 << self.order[0])
+        for n, other in enumerate(self.order[1:]):
+            place = place + lax.rem(at // (1 << n), 2) * (1 << other)
+        return place
+
+    def held(self, stage):
+        return self.source if stage == self.first else self.stages[stage - 1][0]
+
+    def copy(self, stage, at):
+        bit = self.bit(stage)
+        into, send, recv = self.stages[stage]
+        return send_dp(
+            self.held(stage).at[self.index(stage, at, 1 - bit)], into.at[at],
+            send.at[at], recv.at[at], self.me + (1 - 2 * bit) * (1 << self.order[stage]),
+        )
+
+    def spots(self, stage):
+        if stage == len(self.order) - 1:
+            return [0]
+        bit, half = self.bit(stage + 1), self.count(stage) // 2
+        return [n * 2 + 1 - bit for n in range(half)] + [n * 2 + bit for n in range(half)]
+
+    def load(self):
+        for at in range(self.count(0)):
+            pltpu.make_async_copy(
+                self.source.at[self.index(0, at, self.bit(0))], self.own[0].at[at], self.own[1]
+            ).start()
+
+    def loaded(self):
+        pltpu.make_async_copy(
+            self.source.at[pl.ds(0, self.count(0))], self.own[0], self.own[1]
+        ).wait()
+
+    def start(self):
+        for at in self.spots(self.first):
+            self.copy(self.first, at).start()
+
+    def kept(self, stage, at):
+        if stage == self.first and self.own is not None:
+            return self.own[0][at].astype(F32)
+        return self.held(stage)[self.index(stage, at, self.bit(stage))].astype(F32)
+
+    def sum_at(self, stage, at):
+        self.copy(stage, at).wait_recv()
+        return self.kept(stage, at) + self.stages[stage][0][at].astype(F32)
+
+    def run(self, stage):
+        for n, at in enumerate(self.spots(stage)):
+            self.stages[stage][0][at] = self.sum_at(stage, at).astype(LOW)
+            if stage < self.last and n < self.count(stage) // 2:
+                self.copy(stage + 1, n).start()
+
+    def total(self):
+        return self.sum_at(self.last, 0)
+
+    def finish(self):
+        for stage in self.stages:
+            for at in range(self.count(stage)):
+                self.copy(stage, at).wait_send()
+
+
 def middle_kernel(
-    att, proj_w, tokens, cot, fc1_hbm, fc2_hbm, fc1_bias, vectors,
-    output, branch_out, middle_out, fc1_out, fc2_out, proj_out, ga_out, fc1_bias_out, sums_out,
+    heads, att, proj_w, tokens, cot, fc1_hbm, fc2_hbm, fc1_bias, vectors,
+    output, middle_out, fc1_out, fc2_out, proj_out, ga_out, fc1_bias_out, sums_out, fc2_state,
     fc1, fc2, att_tok, branch, mlp, back, n2, act, gu, gb, outs, held, spread,
-    load1, load2, *rest,
+    wide, load1, load2, *rest,
 ):
     core, line, lines = tensor_place()
     me = lax.axis_index("tensor")
     _, share, width = tokens.shape
     rows = tokens.shape[0] * share
-    hidden = fc1_hbm.shape[1]
+    local, hidden = proj_w.shape[0], fc1_hbm.shape[1]
     step, dstep = tile_of(hidden), tile_of(width)
     in_fc1 = pltpu.make_async_copy(fc1_hbm, fc1, load1)
     in_fc2 = pltpu.make_async_copy(fc2_hbm, fc2, load2)
     in_fc1.start()
     in_fc2.start()
-    greet_tensor()
+    greet_all(Ring(heads))
     sum_branch = Reduce(branch, *rest[0:7])
     sum_mlp = Reduce(mlp, *rest[7:14])
     sum_back = Reduce(back, *rest[14:21])
     all_n2 = Gather(n2, *rest[21:24])
     all_gb = Gather(gb, *rest[24:27])
     all_out = Gather(outs, *rest[27:30])
+    devices, chunks, owned, _ = fc2_out.shape
+    blocks = rest[30]
+    moved = Halve(near_first(), blocks, rest[31:], last=0)
     att_tok[...] = att[...].T.reshape(att_tok.shape)
 
     def project(k, carry):
@@ -745,16 +947,22 @@
     lax.fori_loop(0, lines, hidden_part, 0)
     for other in sum_back.others():
         sum_back.pass_on(other)
-    for other in sum_mlp.others():
-        sum_mlp.pass_on(other)
 
     def weights2(n, carry):
         span = pl.ds(pl.multiple_of(n * dstep, dstep), dstep)
         found = tn(cot[:, :, span].reshape(rows, dstep), act[...].reshape(rows, hidden))
-        fc2_out[span, :] = found.astype(LOW)
+        wide[span, :] = found.astype(LOW)
         return carry
 
     lax.fori_loop(0, width // dstep, weights2, 0)
+    for dev in range(devices):
+        for chunk in range(chunks):
+            at = (dev * chunks + chunk) * owned
+            fc2_out[dev, chunk] = wide[pl.ds(at, owned), :]
+        blocks[dev] = wide[pl.ds(dev * chunks * owned, owned), :]
+    moved.start()
+    for other in sum_mlp.others():
+        sum_mlp.pass_on(other)
     upstream = sum_back.total()
     sums_out[0:1] = jnp.sum(upstream * held[1], axis=0, keepdims=True)
     sums_out[1:2] = jnp.sum(upstream, axis=0, keepdims=True)
@@ -770,10 +978,14 @@
     def weights1(n, carry):
         span = pl.ds(pl.multiple_of(n * dstep, dstep), dstep)
         found = tn(n2[:, :, span].reshape(rows, dstep), gu[...].reshape(rows, hidden))
-        fc1_out[span, :] = found.astype(LOW)
+        wide[span, :] = found.astype(LOW)
         return carry
 
     lax.fori_loop(0, width // dstep, weights1, 0)
+    for dev in range(devices):
+        for chunk in range(chunks):
+            at = (dev * chunks + chunk) * owned
+            fc1_out[dev, chunk] = wide[pl.ds(at, owned), :]
     sums_out[2:3] = jnp.sum(cot[...].astype(F32).reshape(rows, width), axis=0, keepdims=True)
     for other in all_gb.others():
         all_gb.forward(other)
@@ -789,20 +1001,23 @@
     def weights0(n, carry):
         span = pl.ds(pl.multiple_of(n * dstep, dstep), dstep)
         found = tn(gb[:, :, span].reshape(rows, dstep), att_tok[...].reshape(rows, -1))
-        proj_out[span, :] = found.astype(LOW)
+        wide[span, :local] = found.astype(LOW)
         return carry
 
     lax.fori_loop(0, width // dstep, weights0, 0)
-    branch_out[...] = gb[...]
+    for dev in range(devices):
+        proj_out[dev] = wide[pl.ds(dev * chunks * owned, chunks * owned), :local]
     all_out.take(line)
     for other in all_out.others():
         all_out.take(other)
     output[...] = outs[...]
-    for each in (sum_branch, sum_mlp, sum_back, all_n2, all_gb, all_out):
+    moved.run(0)
+    fc2_state[...] = moved.stages[0][0][...]
+    for each in (sum_branch, sum_mlp, sum_back, all_n2, all_gb, all_out, moved):
         each.finish()
 
 
-def middle_block(att, proj_w, tokens, cot, fc1, fc2, fc1_bias, vectors):
+def middle_block(heads, att, proj_w, tokens, cot, fc1, fc2, fc1_bias, vectors):
     count = lax.axis_size("tensor")
     lines = count // 2
     local, width = proj_w.shape
@@ -813,6 +1028,10 @@
     hbm = pl.BlockSpec(memory_space=pl.ANY)
     dma = pltpu.SemaphoreType.DMA
     whole = (count, share, width)
+    devices = lax.axis_size("dp")
+    owned = width // devices
+    chunks = 2 if owned % 32 == 0 else 1
+    weights = (devices, chunks, owned // chunks, hidden)
     scratch = [
         pltpu.VMEM((width, hidden), LOW),
         pltpu.VMEM((hidden, width), LOW),
@@ -827,22 +1046,25 @@
         pltpu.VMEM(whole, LOW),
         pltpu.VMEM((2, share, width), F32),
         pltpu.VMEM((share, 128), F32),
+        pltpu.VMEM((width, hidden), LOW),
         dma,
         dma,
     ]
     scratch += part_bufs(lines, share, width) * 3 + gather_sems(lines) * 3
+    scratch += [pltpu.VMEM((devices, owned // chunks, hidden), LOW)]
+    scratch += halve_bufs(owned // chunks, hidden, last=0)
     return pl.pallas_call(
-        middle_kernel,
+        functools.partial(middle_kernel, heads),
         out_shape=(
             jax.ShapeDtypeStruct(whole, LOW),
-            jax.ShapeDtypeStruct(whole, LOW),
             jax.ShapeDtypeStruct((share, width), F32),
-            jax.ShapeDtypeStruct((width, hidden), LOW),
-            jax.ShapeDtypeStruct((width, hidden), LOW),
-            jax.ShapeDtypeStruct((width, local), LOW),
+            jax.ShapeDtypeStruct(weights, LOW),
+            jax.ShapeDtypeStruct(weights, LOW),
+            jax.ShapeDtypeStruct((devices, owned, local), LOW),
             jax.ShapeDtypeStruct((local, rows), LOW),
             jax.ShapeDtypeStruct((1, hidden), F32),
             jax.ShapeDtypeStruct((8, width), F32),
+            jax.ShapeDtypeStruct((devices // 2, owned // chunks, hidden), LOW),
         ),
         in_specs=[vmem] * 4 + [hbm] * 2 + [vmem] * 2,
         out_specs=(vmem,) * 9,
@@ -857,124 +1079,6 @@
     )
 
 
-def greet_tensor():
-    peers = tensor_peers()
-    barrier = pltpu.get_barrier_semaphore()
-    for peer in peers:
-        pl.semaphore_signal(barrier, inc=1, device_id={"tensor": peer}, device_id_type=MESH)
-    pl.semaphore_wait(barrier, len(peers))
-
-
-class Ring:
-    def __init__(self, heads):
-        self.heads, self.group = heads, lax.axis_size("dp") // heads
-        me = lax.axis_index("dp")
-        self.z, self.g = me // self.group, lax.rem(me, self.group)
-
-    def column(self):
-        return [lax.rem(self.z + k, self.heads) for k in range(1, self.heads)]
-
-    def mates(self):
-        return [lax.rem(self.g + k, self.group) for k in range(1, self.group)]
-
-    def peers(self):
-        far = [h * self.group + self.g for h in self.column()]
-        return far + [self.z * self.group + o for o in self.mates()]
-
-
-def greet_all(ring):
-    barrier = pltpu.get_barrier_semaphore()
-    near, far = tensor_peers(), ring.peers()
-    for peer in near:
-        pl.semaphore_signal(barrier, inc=1, device_id={"tensor": peer}, device_id_type=MESH)
-    for peer in far:
-        pl.semaphore_signal(barrier, inc=1, device_id={"dp": peer}, device_id_type=MESH)
-    pl.semaphore_wait(barrier, len(near) + len(far))
-
-
-def scatter_bufs(heads, share, width):
-    group = lax.axis_size("dp") // heads
-    dma = pltpu.SemaphoreType.DMA
-    block = (heads, share, width)
-    return [
-        pltpu.VMEM(block, LOW), pltpu.VMEM((group,) + block, LOW), pltpu.VMEM(block, LOW),
-        pltpu.VMEM(block, LOW), dma((heads, group)), dma((heads, group)),
-        dma((heads,)), dma((heads,)), dma((heads,)),
-    ]
-
-
-SCATTER_BUFS = 9
-
-
-class Scatter:
-    def __init__(self, ring, source, mine, mate_in, passed, far_in, m_send, m_recv, f_send, f_recv, load):
-        self.ring, self.source, self.mine = ring, source, mine
-        self.mate_in, self.passed, self.far_in = mate_in, passed, far_in
-        self.sems = m_send, m_recv, f_send, f_recv, load
-
-    def load_copy(self, at):
-        ring = self.ring
-        return pltpu.make_async_copy(
-            self.source.at[at * ring.group + ring.g], self.mine.at[at], self.sems[4].at[at]
-        )
-
-    def mate_copy(self, at, mate, slot):
-        ring = self.ring
-        return send_dp(
-            self.source.at[at * ring.group + mate], self.mate_in.at[slot, at],
-            self.sems[0].at[at, mate], self.sems[1].at[at, slot], ring.z * ring.group + mate,
-        )
-
-    def far_copy(self, at, slot):
-        ring = self.ring
-        return send_dp(
-            self.passed.at[at], self.far_in.at[slot], self.sems[2].at[at], self.sems[3].at[slot],
-            at * ring.group + ring.g,
-        )
-
-    def give(self, at):
-        self.load_copy(at).start()
-        for mate in self.ring.mates():
-            self.mate_copy(at, mate, self.ring.g).start()
-
-    def give_all(self):
-        for at in self.ring.column() + [self.ring.z]:
-            self.give(at)
-
-    def near_sum(self, at):
-        self.load_copy(at).wait()
-        total = self.mine[at].astype(F32)
-        for mate in self.ring.mates():
-            self.mate_copy(at, mate, mate).wait_recv()
-            total = total + self.mate_in[mate, at].astype(F32)
-        return total
-
-    def pass_on(self, at):
-        self.passed[at] = self.near_sum(at).astype(LOW)
-        self.far_copy(at, self.ring.z).start()
-
-    def pass_all(self):
-        def step(k, carry):
-            self.pass_on(lax.rem(self.ring.z + k, self.ring.heads))
-            return carry
-
-        lax.fori_loop(1, self.ring.heads, step, 0)
-
-    def total(self):
-        total = self.near_sum(self.ring.z)
-        for other in self.ring.column():
-            self.far_copy(other, other).wait_recv()
-            total = total + self.far_in[other].astype(F32)
-        return total
-
-    def finish(self):
-        for at in self.ring.column() + [self.ring.z]:
-            for mate in self.ring.mates():
-                self.mate_copy(at, mate, self.ring.g).wait_send()
-        for other in self.ring.column():
-            self.far_copy(other, self.ring.z).wait_send()
-
-
 def small_bufs(heads, stages, shape):
     group, lines = lax.axis_size("dp") // heads, lax.axis_size("tensor") // 2
     dma = pltpu.SemaphoreType.DMA
@@ -1018,12 +1122,8 @@
             total = self.merge(total, self.bufs[n][1][other])
         return total
 
-    def run(self, upto=None):
-        for n in range(len(self.stages)):
-            value = self.take(n)
-            if n + 1 < len(self.stages):
-                self.start(n + 1, value)
-        return value
+    def step(self, n):
+        self.start(n + 1, self.take(n))
 
     def finish(self):
         for n in range(len(self.stages)):
@@ -1048,10 +1148,9 @@
 
 
 def tail_kernel(
-    heads, grads, qkv_w, n1_t, tokens, grad_middle, vectors, tables, sums, fc1_bias, peak,
-    fc1, fc2, proj,
-    tokens_out, fc1_out, fc2_out, proj_out, qkv_out, tables_out, sums_out, late_out, dp_out,
-    g_all, g_tok, part, gt, gq, *rest,
+    heads, grads, qkv_w, n1_t, tokens, grad_middle, vectors, tables, sums, fc1_bias, peak, proj,
+    tokens_out, proj_out, qkv_out, tables_out, sums_out, late_out, dp_out,
+    g_all, g_tok, part, gt, *rest,
 ):
     ring = Ring(heads)
     core, line, lines = tensor_place()
@@ -1060,6 +1159,7 @@
     rows = count * share
     local = heads * HEAD
     dstep = tile_of(width)
+    devices, chunks, _, _ = n1_t.shape
     rest = list(rest)
 
     def taken(number):
@@ -1067,21 +1167,19 @@
         return found
 
     greet_all(ring)
-    moved2 = Scatter(ring, fc2, *taken(SCATTER_BUFS))
-    moved1 = Scatter(ring, fc1, *taken(SCATTER_BUFS))
-    moved0 = Scatter(ring, proj, *taken(SCATTER_BUFS))
-    moved3 = Scatter(ring, gq, *taken(SCATTER_BUFS))
+    blocks = [taken(1)[0] for _ in range(chunks)]
+    orders = [near_first(), far_first(ring.group)]
+    moved3 = [Halve(orders[n], blocks[n], taken(3 * halve_bits())) for n in range(chunks)]
+    moved0 = Halve(near_first(), proj, taken(3 * halve_bits()))
     sum_part = Reduce(part, *taken(7))
     all_gt = Gather(gt, *taken(3))
     small_tables = Small(ring, EVERY, lax.add, *taken(16))
     small_sums = Small(ring, EVERY, lax.add, *taken(16))
     small_late = Small(ring, EVERY, lax.add, *taken(16))
     small_dp = Small(ring, OVER_DP, add_peaks, *taken(8))
-    moved2.give_all()
-    moved1.give_all()
-    moved0.give_all()
     small_tables.start(0, tables[...].reshape(4 * SIDE, 128))
     small_sums.start(0, sums[...])
+    moved0.start()
     for t in range(3):
         for h in range(heads):
             g_all[pl.ds(t * local + h * HEAD, HEAD), :] = grads[h, t]
@@ -1111,18 +1209,17 @@
     for other in sum_part.others():
         sum_part.pass_on(other)
 
-    def weight_part(k, carry):
-        at = lax.rem(ring.z + 1 + k // ring.group, heads)
-        dev = at * ring.group + lax.rem(ring.g + 1 + lax.rem(k, ring.group), ring.group)
-        gq[dev] = nn(n1_t[dev], g_tok[...].reshape(rows, 3 * local)).astype(LOW)
-
-        @pl.when(lax.rem(k, ring.group) == ring.group - 1)
-        def _():
-            moved3.give(at)
-
-        return carry
-
-    lax.fori_loop(0, heads * ring.group, weight_part, 0)
+    for n in range(chunks):
+
+        def weight_part(dev, carry):
+            found = nn(n1_t[dev, n], g_tok[...].reshape(rows, 3 * local))
+            blocks[n][dev] = found.astype(LOW)
+            return carry
+
+        lax.fori_loop(0, devices, weight_part, 0)
+        moved3[n].start()
+    small_tables.step(0)
+    small_sums.step(0)
     scaled, inverse = normed(tokens[me].astype(F32))
     upstream = sum_part.total()
     late = [
@@ -1134,51 +1231,56 @@
     found = grad_middle[...] + normed_back(upstream, scaled, inverse, vectors[0:1])
     gt[me] = found.astype(LOW)
     all_gt.start()
-    moved2.pass_all()
+    small_tables.step(1)
+    small_sums.step(1)
+    small_late.step(0)
+    small_dp.step(0)
+    moved0.run(0)
+    small_late.step(1)
     for other in all_gt.others():
         all_gt.forward(other)
-    dp_out[...] = small_dp.run()
-    sums_out[...] = small_sums.run()
-    moved1.pass_all()
-    tables_out[...] = small_tables.run()
-    moved0.pass_all()
+    for each in moved3:
+        each.run(0)
+    small_tables.step(2)
+    small_sums.step(2)
+    small_late.step(2)
+    for stage in range(1, halve_bits() - 1):
+        moved0.run(stage)
+        for each in moved3:
+            each.run(stage)
     all_gt.take(line)
     for other in all_gt.others():
         all_gt.take(other)
     tokens_out[...] = gt[...]
-    late_out[...] = small_late.run()
-    moved3.pass_all()
-    fc2_out[...] = moved2.total().T
-    fc1_out[...] = moved1.total()
+    dp_out[...] = small_dp.take(1)
+    tables_out[...] = small_tables.take(3)
+    sums_out[...] = small_sums.take(3)
+    late_out[...] = small_late.take(3)
     proj_out[...] = moved0.total().T
-    qkv_out[...] = moved3.total()
-    for each in (
-        moved0, moved1, moved2, moved3, sum_part, all_gt,
-        small_tables, small_sums, small_late, small_dp,
-    ):
+    for n, each in enumerate(moved3):
+        qkv_out[n] = each.total()
+    for each in [moved0, sum_part, all_gt, small_tables, small_sums, small_late, small_dp] + moved3:
         each.finish()
 
 
-def tail(heads, grads, qkv_w, n1_t, tokens, grad_middle, vectors, tables, sums, fc1_bias, peak, fc1, fc2, proj):
+def tail(heads, grads, qkv_w, n1_t, tokens, grad_middle, vectors, tables, sums, fc1_bias, peak, proj):
     count = lax.axis_size("tensor")
     lines = count // 2
     local = heads * HEAD
-    devices, owned, rows = n1_t.shape
-    width = devices * owned
+    devices, chunks, owned, rows = n1_t.shape
+    width = devices * chunks * owned
     share = rows // count
-    hidden = fc1.shape[1]
     vmem = pl.BlockSpec(memory_space=pltpu.VMEM)
-    hbm = pl.BlockSpec(memory_space=pl.ANY)
     whole = (count, share, width)
     scratch = [
         pltpu.VMEM((3 * local, rows), LOW),
         pltpu.VMEM((count, share, 3 * local), LOW),
         pltpu.VMEM(whole, LOW),
         pltpu.VMEM(whole, LOW),
-        pltpu.VMEM((devices, owned, 3 * local), LOW),
     ]
-    for columns in (hidden, hidden, local, 3 * local):
-        scratch += scatter_bufs(heads, owned, columns)
+    scratch += [pltpu.VMEM((devices, owned, 3 * local), LOW)] * chunks
+    scratch += halve_bufs(owned, 3 * local) * chunks
+    scratch += halve_bufs(chunks * owned, local)
     scratch += part_bufs(lines, share, width) + gather_sems(lines)
     scratch += small_bufs(heads, EVERY, (4 * SIDE, 128))
     scratch += small_bufs(heads, EVERY, (8, width)) * 2
@@ -1187,26 +1289,23 @@
         functools.partial(tail_kernel, heads),
         out_shape=(
             jax.ShapeDtypeStruct(whole, LOW),
-            jax.ShapeDtypeStruct((owned, hidden), F32),
-            jax.ShapeDtypeStruct((hidden, owned), F32),
-            jax.ShapeDtypeStruct((local, owned), F32),
-            jax.ShapeDtypeStruct((owned, 3 * local), F32),
+            jax.ShapeDtypeStruct((local, chunks * owned), F32),
+            jax.ShapeDtypeStruct((chunks, owned, 3 * local), F32),
             jax.ShapeDtypeStruct((4 * SIDE, 128), F32),
             jax.ShapeDtypeStruct((8, width), F32),
             jax.ShapeDtypeStruct((8, width), F32),
             jax.ShapeDtypeStruct((8, width), F32),
         ),
-        in_specs=[vmem] * 10 + [hbm] * 3,
-        out_specs=(vmem,) * 9,
+        in_specs=[vmem] * 11,
+        out_specs=(vmem,) * 7,
         scratch_shapes=scratch,
         compiler_params=pltpu.CompilerParams(
             collective_id=4, has_side_effects=True, vmem_limit_bytes=VMEM_LIMIT
         ),
         name="tail",
     )(
-        grads, qkv_w, n1_t, tokens.reshape(whole), grad_middle, vectors, tables, sums, fc1_bias, peak,
-        fc1.reshape(devices, owned, hidden), fc2.reshape(devices, owned, hidden),
-        proj.reshape(devices, owned, local),
+        grads, qkv_w, n1_t, tokens.reshape(whole), grad_middle, vectors, tables, sums, fc1_bias,
+        peak, proj,
     )
 
 
@@ -1250,7 +1349,6 @@
     vectors = jnp.pad(vectors, ((0, 4), (0, 0)))
     (
         output,
-        grad_branch,
         grad_middle,
         grad_fc1,
         grad_fc2,
@@ -1258,7 +1356,9 @@
         grad_attended,
         grad_fc1_bias,
         sums,
+        fc2_state,
     ) = middle_block(
+        local_heads,
         attended.reshape(local_width, token_count),
         proj_weight,
         tokens.reshape(token_count, model_width),
@@ -1269,15 +1369,13 @@
         vectors,
     )
     grad_heads = grad_attended.reshape(local_heads, HEAD, row_count)
-    grad_triple, table_terms = attend_back(
-        shape, grad_heads, flipped, qaug, bias_rows, kv, o_rows, lse
+    devices, chunks, owned, _ = grad_fc1.shape
+    grad_triple, table_terms, grad_fc1, grad_fc2 = attend_back(
+        shape, grad_heads, flipped, qaug, bias_rows, kv, o_rows, lse, fc2_state, grad_fc1, grad_fc2
     )
-    devices = lax.axis_size("dp")
     tail_vectors = jnp.pad(norm1_gain[None], ((0, 7), (0, 0)))
     (
         grad_tokens,
-        grad_fc1,
-        grad_fc2,
         grad_proj,
         grad_qkv,
         table_sums,
@@ -1288,7 +1386,7 @@
         local_heads,
         grad_triple,
         qkv_weight.reshape(model_width, 3 * local_width),
-        normed1_low.T.reshape(devices, model_width // devices, token_count),
+        normed1_low.T.reshape(devices, chunks, owned, token_count),
         tokens.reshape(token_count, model_width),
         grad_middle,
         tail_vectors,
@@ -1296,8 +1394,6 @@
         sums,
         grad_fc1_bias,
         peak,
-        grad_fc1,
-        grad_fc2,
         grad_proj,
     )
     grad_tokens = grad_tokens.reshape(images, row_count, model_width)

time: 438 us -> 345 us (0.79)
  Pallas kernels: 394 us -> 304 us
    pallas_call x1, Pallas kernels: 212 us -> 76.9 us  [tail(): pl.pallas_call(functools.partial(tail_kernel, heads), out_shape=(jax.Shap...]
    pallas_call x1, Pallas kernels: 54.1 us -> 97.4 us  [attend_back(): pl.pallas_call(functools.partial(backward_kernel, shape), out_shape=(jax....]
    unnamed x44 -> x46, local copies, waits for them, and re-layouts: 8.8 us -> 7.83 us
where the time goes in v3:
time: 345 us; the launch traced here: 344 us
  Pallas kernels  304 us (88%)
  local copies, waits for them, and re-layouts  24.2 us (7%)
  other arithmetic  10.6 us (3%)
    pallas_call x1, Pallas kernels, attend_back(): pl.pallas_call(functools.partial(backward_kernel, shape), out_shape=(jax....  97.4 us
    pallas_call x1, Pallas kernels, tail(): pl.pallas_call(functools.partial(tail_kernel, heads), out_shape=(jax.Shap...  76.9 us
    pallas_call x1, Pallas kernels, middle_block(): pl.pallas_call(functools.partial(middle_kernel, heads), out_shape=(jax.Sh...  72.8 us
    pallas_call x1, Pallas kernels, attend(): pl.pallas_call(functools.partial(forward_kernel, shape), out_shape=(jax.S...  57.2 us
    unnamed x46, local copies, waits for them, and re-layouts  7.83 us

profile of v3, /device:TPU:0, one launch (start us, length us, event | category | flops | bytes accessed | tf_op | source)
XLA Modules:
  0.0 344.2 jit_solution(15867415046182247652)
XLA Ops:
  0.7 0.8 slice_reduce_fusion.6
  1.7 1.6 convert_reduce_fusion
  3.2 1.8 fusion.3
  5.1 3.4 add_convert_fusion
  8.5 1.0 copy.59
  10.8 57.2 %attend.1 = (bf16[4,80,512]{2,1,0:T(8,128)(2,1)}, bf16[240,2048]{1,0:T(8,128)(2,1)}, bf16[8,16,2048]{2,1,0:T(8,128)(2,1)}, bf16[4,2,2,80,512]{4,3,2,1,0:T(8,128)...) custom-call(bf16[4,3,80,512]{3,2,1,0:T(8,128)(2,1)} %bitcast.56, bf16[2,128,80]{2,1,0:T(8,128)(2,1)} %pad.12.tables), custom_call_target="tpu_custom_call" | custom-call | tf_op jit(solution)/shard_map/attend/pallas_call | solution.py:253
  69.4 72.8 %middle.1 = (bf16[4,128,1280]{2,1,0:T(8,128)(2,1)}, f32[128,1280]{1,0:T(8,128)}, bf16[8,2,80,1280]{3,2,1,0:T(8,128)(2,1)}, bf16[8,2,80,1280]{3,2,1,0:T(8,128)(2,...) custom-call(bf16[320,512]{1,0:T(8,128)(2,1)} %bitcast.61, ...), custom_call_target="tpu_custom_call" | custom-call | tf_op jit(solution)/shard_map/middle/pallas_call | solution.py:1056
  142.2 97.4 %attend_back.1 = (bf16[4,3,80,512]{3,2,1,0:T(8,128)(2,1)}, f32[2,128,128]{2,1,0:T(8,128)}, f32[160,1280]{1,0:T(8,128)}, f32[1280,160]{1,0:T(8,128)}) custom-call(bf16[4,80,512]{2,1,0:T(8,128)(2,1)} %bitcast.62, bf16[2,128,80]{2,1,0:T(8,128)(2,1)} %pad.12.tables, bf16[240,2048]{1,0:T(8,128)(2,1)} %get-tuple-element.50.qaug_in, ...), custom_call_target="tpu_custom_call" | custom-call | tf_op jit(solution)/shard_map/attend_back/pallas_call | solution.py:531
  239.7 1.6 fusion.8
  241.3 2.6 copy.49
  243.8 3.6 %copy.50.qkv_w = bf16[1280,960]{1,0:T(8,128)(2,1)} copy(bf16[1280,960]{0,1:T(8,128)(2,1)S(1)} %bitcast.54) | data formatting | bytes 4915200 | tf_op jit(solution)/shard_map/reshape | solution.py:1388
  248.1 76.9 %tail.1 = (bf16[4,128,1280]{2,1,0:T(8,128)(2,1)}, f32[320,160]{1,0:T(8,128)}, f32[2,80,960]{2,1,0:T(8,128)}, f32[256,128]{1,0:T(8,128)}, f32[8,1280]{1,0:T(8,128...) custom-call(bf16[4,3,80,512]{3,2,1,0:T(8,128)(2,1)} %get-tuple-element.58.grads, bf16[1280,960]{1,0:T(8,128)(2,1)} %copy.50.qkv_w, ...), custom_call_target="tpu_custom_call" | custom-call | tf_op jit(solution)/shard_map/tail/pallas_call | solution.py:1288
  325.0 1.6 multiply_reduce_fusion
  326.6 1.5 reshape.101
  328.2 0.9 copy.53
  329.8 1.2 divide_sqrt_fusion
  331.2 1.5 multiply_convert_fusion
  332.7 0.8 copy.54
  335.1 1.5 slice_reduce_fusion.3
  336.6 0.8 slice_reduce_fusion.5
  338.6 2.6 copy.55
  341.2 1.1 copy.64
  342.3 1.1 copy.65
  343.3 0.9 copy.66
  (63 shorter events, 6.4 us)
Async XLA Ops:
  0.7 4.4 %copy-start = (bf16[1,512,1280]{2,1,0:T(8,128)(2,1)S(1)}, bf16[1,512,1280]{2,1,0:T(8,128)(2,1)}, u32[]{:S(2)}) copy-start(bf16[1,512,1280]{2,1,0:T(8,128)(2,1)} %param.17) | copy-start | bytes 3932164
  0.7 4.4 %copy-start.8 = (f32[1280]{0:T(1024)S(1)}, f32[1280]{0:T(1024)}, u32[]{:S(2)}) copy-start(f32[1280]{0:T(1024)} %param.19) | copy-start | bytes 15364
  0.7 4.4 %copy-start.11 = (f32[1280]{0:T(1024)S(1)}, f32[1280]{0:T(1024)}, u32[]{:S(2)}) copy-start(f32[1280]{0:T(1024)} %param.20) | copy-start | bytes 15364
  5.1 4.5 %copy-start.9 = (bf16[127,80]{0,1:T(8,128)(2,1)S(1)}, bf16[127,80]{0,1:T(8,128)(2,1)}, u32[]{:S(2)}) copy-start(bf16[127,80]{0,1:T(8,128)(2,1)} %param.25) | copy-start | bytes 60964
  5.1 4.6 %copy-start.10 = (bf16[127,80]{0,1:T(8,128)(2,1)S(1)}, bf16[127,80]{0,1:T(8,128)(2,1)}, u32[]{:S(2)}) copy-start(bf16[127,80]{0,1:T(8,128)(2,1)} %param.26) | copy-start | bytes 60964
  8.5 59.6 %copy-start.12 = (f32[1280]{0:T(1024)S(1)}, f32[1280]{0:T(1024)}, u32[]{:S(2)}) copy-start(f32[1280]{0:T(1024)} %param.24) | copy-start | bytes 15364
  8.5 59.6 %copy-start.13 = (f32[1280]{0:T(1024)S(1)}, f32[1280]{0:T(1024)}, u32[]{:S(2)}) copy-start(f32[1280]{0:T(1024)} %param.27) | copy-start | bytes 15364
  8.5 59.6 %copy-start.14 = (f32[1280]{0:T(1024)S(1)}, f32[1280]{0:T(1024)}, u32[]{:S(2)}) copy-start(f32[1280]{0:T(1024)} %param.28) | copy-start | bytes 15364
  8.5 59.6 %copy-start.15 = (f32[1280]{0:T(1024)S(1)}, f32[1280]{0:T(1024)}, u32[]{:S(2)}) copy-start(f32[1280]{0:T(1024)} %param.32) | copy-start | bytes 15364
  8.5 60.3 %copy-start.16 = (f32[1280]{0:T(1024)S(1)}, f32[1280]{0:T(1024)}, u32[]{:S(2)}) copy-start(f32[1280]{0:T(1024)} %param.30) | copy-start | bytes 15364
  142.2 97.4 %copy-start.1 = (bf16[1,512,1280]{2,1,0:T(8,128)(2,1)S(1)}, bf16[1,512,1280]{2,1,0:T(8,128)(2,1)}, u32[]{:S(2)}) copy-start(bf16[1,512,1280]{2,1,0:T(8,128)(2,1)} %param.17) | copy-start | bytes 3932164
  241.3 2.6 copy-start.2
  329.1 3.6 %copy-start.6 = (f32[320,160]{1,0:T(8,128)S(1)}, f32[320,160]{1,0:T(8,128)}, u32[]{:S(2)}) copy-start(f32[320,160]{1,0:T(8,128)} %get-tuple-element.100) | copy-start | bytes 614404
  329.1 4.4 %copy-start.7 = (f32[256,128]{1,0:T(8,128)S(1)}, f32[256,128]{1,0:T(8,128)}, u32[]{:S(2)}) copy-start(f32[256,128]{1,0:T(8,128)} %get-tuple-element.71) | copy-start | bytes 393220
  331.0 10.2 %copy-start.17 = (f32[4]{0:T(128)}, f32[4]{0:T(128)S(1)}, u32[]{:S(2)}) copy-start(f32[4]{0:T(128)S(1)} %get-tuple-element.167) | copy-start | bytes 52
  332.7 8.6 %copy-start.3 = (bf16[4,128,1280]{2,1,0:T(8,128)(2,1)S(1)}, bf16[4,128,1280]{2,1,0:T(8,128)(2,1)}, u32[]{:S(2)}) copy-start(bf16[4,128,1280]{2,1,0:T(8,128)(2,1)} %get-tuple-element.48) | copy-start | bytes 3932164
  333.5 8.8 %copy-start.4 = (bf16[4,128,1280]{2,1,0:T(8,128)(2,1)S(1)}, bf16[4,128,1280]{2,1,0:T(8,128)(2,1)}, u32[]{:S(2)}) copy-start(bf16[4,128,1280]{2,1,0:T(8,128)(2,1)} %get-tuple-element.65) | copy-start | bytes 3932164
  341.2 2.1 copy-start.5

commit v4 on v3

--- a/solution.py
+++ b/solution.py
@@ -21,7 +21,13 @@
 ROWS_AT = COLS_AT + 2 * SIDE
 LSE_AT = ROWS_AT + 16
 AUG = LSE_AT + 16
-VMEM_LIMIT = 60 * 2**20
+VMEM_LIMIT = {
+    "attend": 60 * 2**20,
+    "middle": 40 * 2**20,
+    "attend_back": 24 * 2**20,
+    "tail": 24 * 2**20,
+    "finish": 12 * 2**20,
+}
 
 
 def nn(a, b):
@@ -56,6 +62,20 @@
     )
 
 
+def paired(place, k, count):
+    found, bit = 0, 1
+    while bit < count:
+        found = found + bit * lax.rem(place // bit + k // bit, 2)
+        bit *= 2
+    return found
+
+
+def turned(count):
+    row = lax.broadcasted_iota(jnp.int32, (count, count), 0)
+    column = lax.broadcasted_iota(jnp.int32, (count, count), 1)
+    return jnp.where(row + column == count - 2, 1.0, 0.0).astype(LOW)
+
+
 def shifts(rows, dev):
     spot = lax.broadcasted_iota(jnp.int32, (2 * SIDE, rows), 1)
     by_row = SIDE - 1 - (dev * (rows // SIDE) + lax.shift_right_logical(spot, 6))
@@ -102,30 +122,82 @@
         self.block = min(1024, self.queries)
 
 
-def forward_kernel(
-    shape, qkv, tables, att, qaug, bias_rows, kv_out, o_out, lse_out, peak_out,
-    rq, rkv, kaug_t, kaug, vaug, oacc, mrow, lpk, att_s, att_r,
+def forward_kernel(shape, count, outs, *refs):
+    held = refs[count + outs : 2 * count + outs]
+    load = refs[2 * count + outs]
+    copies = [
+        pltpu.make_async_copy(a, b, load.at[n]) for n, (a, b) in enumerate(zip(refs[:count], held))
+    ]
+    for copy in copies[2:] + copies[:2]:
+        copy.start()
+    forward_body(
+        shape, copies, *held, *refs[count : count + outs], *refs[2 * count + outs + 1 :]
+    )
+
+
+def forward_body(
+    shape, copies, tokens, weights, proj_bias, gain2, shift2, fc2_bias, gain1, shift1, fc1_bias,
+    qv_bias, threshold, rows_t, cols_t,
+    att, qaug, bias_rows, kv_out, o_out, lse_out, peak_out, n1_out, tables, vectors,
+    n1, qkv, wide_t, rq, rkv, kaug_t, kaug, vaug, oacc, mrow, lpk, att_s, att_r,
     q_send, q_recv, k_send, k_recv, x_send, x_recv, r_send, r_recv, o_sem,
 ):
     heads, group, rows, block = shape.heads, shape.group, shape.rows, shape.block
+    local = heads * HEAD
     me = lax.axis_index("dp")
     z, g = me // group, lax.rem(me, group)
-    column = [lax.rem(z + k, heads) for k in range(1, heads)]
+    column = [paired(z, k, heads) for k in range(1, heads)]
     mates = [lax.rem(g + k, group) for k in range(1, group)]
     greet([h * group + g for h in column] + [z * group + o for o in mates])
+    width = tokens.shape[1]
+    vectors[...] = jnp.zeros_like(vectors)
+    for copy in copies[2:] + copies[:1]:
+        copy.wait()
+    listed = (proj_bias, gain2, shift2, fc2_bias, gain1, shift1, fc1_bias)
+    for n, each in enumerate(listed):
+        vectors[n : n + 1, : each.shape[0]] = each[...].reshape(1, each.shape[0])
+    vectors[7:9, :local] = qv_bias[...]
+    vectors[9:10] = jnp.broadcast_to(threshold[...].reshape(1, 1), (1, width))
+    scaled, _ = normed(tokens[...].astype(F32))
+    n1[...] = (scaled * vectors[4:5] + vectors[5:6]).astype(LOW)
+    biases = vectors[7:9].astype(F32)
+    biases = jnp.concatenate([biases, jnp.zeros((6, biases.shape[1]), F32)], axis=0).T
+
+    def project(t):
+        found = nt(weights[pl.ds(t * local, local), :], n1[...])
+        if t != 1:
+            found = found + biases[:local, t // 2 : t // 2 + 1]
+        qkv[t] = found.astype(LOW)
+
     sends = []
+    copies[1].wait()
+    project(0)
     for h in column:
-        sends.append(send_dp(qkv.at[h, 0], rq.at[z], q_send.at[h], q_recv.at[z], h * group + g))
+        mine = pl.ds(pl.multiple_of(h * HEAD, 16), HEAD)
+        copy = send_dp(qkv.at[0, mine], rq.at[z], q_send.at[h], q_recv.at[z], h * group + g)
+        copy.start()
+        sends.append(copy)
+    project(1)
+    project(2)
     for h in column:
-        sends.append(
-            send_dp(
-                qkv.at[h, pl.ds(1, 2)], rkv.at[z, g], k_send.at[h], k_recv.at[z], h * group + g
-            )
+        mine = pl.ds(pl.multiple_of(h * HEAD, 16), HEAD)
+        copy = send_dp(
+            qkv.at[pl.ds(1, 2), mine], rkv.at[z, g], k_send.at[h], k_recv.at[z], h * group + g
         )
-    for copy in sends:
         copy.start()
-    rq[z] = qkv[z, 0]
-    rkv[z, g] = qkv[z, pl.ds(1, 2)]
+        sends.append(copy)
+    mine = pl.ds(pl.multiple_of(z * HEAD, 16), HEAD)
+    rq[z] = qkv[0, mine]
+    rkv[z, g] = qkv[pl.ds(1, 2), mine]
+    for n, mate in enumerate(mates):
+        send_dp(
+            rkv.at[z, g], rkv.at[z, g], x_send.at[z, n], x_recv.at[z, g], z * group + mate
+        ).start()
+    n1_out[...] = n1[...].T
+    wide_t[...] = jnp.zeros_like(wide_t)
+    for n, held in enumerate((rows_t, cols_t)):
+        wide_t[n, :HEAD, : held.shape[1]] = held[...]
+        tables[n] = nn(wide_t[n], turned(2 * SIDE)).T[:, :HEAD].astype(LOW)
     qaug[pl.ds(LSE_AT, 16), :] = jnp.zeros((16, shape.queries), LOW)
     kaug_t[pl.ds(LSE_AT, 16), :] = jnp.zeros((16, rows), LOW)
     vaug[pl.ds(HEAD, 16), :] = jnp.where(
@@ -136,7 +208,7 @@
     lpk[...] = jnp.full_like(lpk, -jnp.inf)
 
     def prepare(k, carry):
-        source = lax.rem(z - k + heads, heads)
+        source = paired(z, k, heads)
         span = pl.ds(pl.multiple_of(source * rows, rows), rows)
 
         @pl.when(k > 0)
@@ -184,17 +256,17 @@
         lax.fori_loop(0, shape.queries // block, one, 0)
 
     def column_step(k, carry):
-        source = lax.rem(z - k + heads, heads)
+        source = paired(z, k, heads)
 
         @pl.when(k > 0)
         def _():
             send_dp(rkv.at[source, g], rkv.at[source, g], k_send.at[source], k_recv.at[source], me).wait_recv()
-
-        for n, mate in enumerate(mates):
-            send_dp(
-                rkv.at[source, g], rkv.at[source, g], x_send.at[source, n], x_recv.at[source, g],
-                z * group + mate,
-            ).start()
+            for n, mate in enumerate(mates):
+                send_dp(
+                    rkv.at[source, g], rkv.at[source, g], x_send.at[source, n], x_recv.at[source, g],
+                    z * group + mate,
+                ).start()
+
         chunk(source, g)
 
         def mate_step(n, inner):
@@ -212,7 +284,8 @@
     keep_kv = pltpu.make_async_copy(rkv, kv_out, o_sem)
     keep_kv.start()
 
-    def finish(source, carry):
+    def finish(k, carry):
+        source = paired(z, lax.rem(k, heads), heads)
         span = pl.ds(pl.multiple_of(source * rows, rows), rows)
         total = oacc[pl.ds(HEAD, 1), span]
         attended = oacc[pl.ds(0, HEAD), span] / total
@@ -228,7 +301,7 @@
 
         return carry
 
-    lax.fori_loop(0, heads, finish, 0)
+    lax.fori_loop(1, heads + 1, finish, 0)
     att[z] = att_s[z]
     peak_out[...] = jnp.full(peak_out.shape, jnp.max(lpk[...]) * SCALE, F32)
     for h in column:
@@ -245,13 +318,15 @@
     keep_kv.wait()
 
 
-def attend(shape, qkv, tables):
+def attend(shape, tokens, weights, listed, rows_t, cols_t):
     heads, group, rows, queries = shape.heads, shape.group, shape.rows, shape.queries
+    width, local = tokens.shape[1], heads * HEAD
+    args = (tokens, weights, *listed, rows_t, cols_t)
     vmem = pl.BlockSpec(memory_space=pltpu.VMEM)
     hbm = pl.BlockSpec(memory_space=pl.ANY)
     dma = pltpu.SemaphoreType.DMA
     return pl.pallas_call(
-        functools.partial(forward_kernel, shape),
+        functools.partial(forward_kernel, shape, len(args), 10),
         out_shape=(
             jax.ShapeDtypeStruct((heads, HEAD, rows), LOW),
             jax.ShapeDtypeStruct((AUG, queries), LOW),
@@ -260,10 +335,18 @@
             jax.ShapeDtypeStruct((HEAD, queries), F32),
             jax.ShapeDtypeStruct((1, queries), F32),
             jax.ShapeDtypeStruct((8, 128), F32),
+            jax.ShapeDtypeStruct((width, rows), LOW),
+            jax.ShapeDtypeStruct((2, 2 * SIDE, HEAD), LOW),
+            jax.ShapeDtypeStruct((16, width), F32),
         ),
-        in_specs=[vmem, vmem],
-        out_specs=(vmem, vmem, vmem, hbm, vmem, vmem, vmem),
+        in_specs=[pl.BlockSpec(memory_space=pltpu.HBM)] * len(args),
+        out_specs=(vmem, vmem, vmem, hbm, vmem, vmem, vmem, vmem, vmem, vmem),
         scratch_shapes=[
+            *[pltpu.VMEM(each.shape, each.dtype) for each in args],
+            dma((len(args),)),
+            pltpu.VMEM((rows, width), LOW),
+            pltpu.VMEM((3, local, rows), LOW),
+            pltpu.VMEM((2, 128, 2 * SIDE), LOW),
             pltpu.VMEM((heads, HEAD, rows), LOW),
             pltpu.VMEM((heads, group, 2, HEAD, rows), LOW),
             pltpu.VMEM((AUG, rows), LOW),
@@ -279,15 +362,15 @@
             dma,
         ],
         compiler_params=pltpu.CompilerParams(
-            collective_id=1, has_side_effects=True, vmem_limit_bytes=VMEM_LIMIT
+            collective_id=1, has_side_effects=True, vmem_limit_bytes=VMEM_LIMIT["attend"]
         ),
         name="attend",
-    )(qkv, tables)
+    )(*args)
 
 
 def backward_kernel(
-    shape, ga, tables, qaug_in, bias_rows, rkv, o_in, lse_in, fc2_state, fc1, fc2,
-    grads, table_grads, fc1_out, fc2_out,
+    shape, ga, tables, qaug_in, bias_rows, rkv, o_in, lse_in, fc2_state, fc2_more, fc1, proj,
+    grads, table_grads, fc1_out, fc2_out, fc1_state, proj_state,
     rdo, qaug, q_tok, do_aug, do_tok, kaug_t, kaug, vaug_t, vaug, kacc, vacc, dq, drow, dcol,
     part, xr, summed, gq_s, gq_r, gkv_r,
     d_send, d_recv, x_send, x_recv, kv_send, kv_recv, q_send, q_recv, *rest,
@@ -300,16 +383,19 @@
         return found
 
     whole_bufs = 2 + 3 * halve_bits()
-    moved2 = [Halve(near_first(), fc2_state, taken(3 * (halve_bits() - 1)), first=1)]
+    bits = halve_bits()
+    moved2 = [Halve(near_first(), fc2_state, taken(3 * (bits - 2)), first=2)]
+    if chunks > 1:
+        moved2 += [Halve(near_first(), fc2_more, taken(3 * (bits - 1)), first=1)]
+    moved0 = Halve(near_first(), proj, taken(3), last=0)
     moved1 = [Halve(near_first(), fc1.at[:, 0], taken(whole_bufs), own=True)]
     if chunks > 1:
-        moved2 += [Halve(near_first(), fc2.at[:, 1], taken(whole_bufs), own=True)]
-        moved1 += [Halve(far_first(shape.group), fc1.at[:, 1], taken(whole_bufs), own=True)]
+        moved1 += [Halve(near_first(), fc1.at[:, 1], taken(5), last=0, own=True)]
     heads, group, rows, block = shape.heads, shape.group, shape.rows, shape.block
     queries = shape.queries
     me = lax.axis_index("dp")
     z, g = me // group, lax.rem(me, group)
-    column = [lax.rem(z + k, heads) for k in range(1, heads)]
+    column = [paired(z, k, heads) for k in range(1, heads)]
     mates = [lax.rem(g + k, group) for k in range(1, group)]
     greet([h * group + g for h in column] + [z * group + o for o in mates])
     sends = []
@@ -317,11 +403,11 @@
         copy = send_dp(ga.at[h], rdo.at[z], d_send.at[h], d_recv.at[z], h * group + g)
         copy.start()
         sends.append(copy)
-    if chunks > 1:
-        moved2[1].start()
-        moved2[1].load()
-        moved1[1].load()
-    moved1[0].load()
+    moved1[0].start()
+    for each in moved2:
+        each.start()
+    for each in moved1:
+        each.load()
     rdo[z] = ga[z]
     qaug[...] = qaug_in[...]
     ones = jnp.where(lax.broadcasted_iota(jnp.int32, (16, rows), 0) < 3, 1.0, 0.0).astype(LOW)
@@ -337,7 +423,7 @@
     drow[...] = jnp.zeros_like(drow)
 
     def prepare(k, carry):
-        source = lax.rem(z - k + heads, heads)
+        source = paired(z, k, heads)
         span = pl.ds(pl.multiple_of(source * rows, rows), rows)
 
         @pl.when(k > 0)
@@ -357,9 +443,6 @@
         return carry
 
     lax.fori_loop(0, heads, prepare, 0)
-    moved2[0].start()
-    if chunks > 1:
-        moved1[1].start()
 
     def chunk(source, mate):
         dev = source * group + mate
@@ -409,7 +492,7 @@
         )
 
     def mates_step(k, carry):
-        source = lax.rem(z + k, heads)
+        source = paired(z, lax.rem(k, heads), heads)
 
         def mate_step(n, inner):
             mate = lax.rem(g + n, group)
@@ -420,20 +503,18 @@
 
         lax.fori_loop(1, group, mate_step, 0)
 
-        @pl.when(k == 2)
-        def _():
-            moved2[0].run(1)
-
         return carry
 
     lax.fori_loop(1, heads + 1, mates_step, 0)
-    moved1[0].start()
+    moved0.start()
     if chunks > 1:
-        moved2[1].loaded()
-        moved2[1].run(0)
+        moved1[1].start()
+        moved2[1].run(1)
+    moved1[0].loaded()
+    moved1[0].run(0)
 
     def own_step(k, carry):
-        source = lax.rem(z + k, heads)
+        source = paired(z, lax.rem(k, heads), heads)
         chunk(source, g)
         extra = []
         for mate in mates:
@@ -449,26 +530,13 @@
                 summed.at[source], gkv_r.at[z], kv_send.at[source], kv_recv.at[z], source * group + g
             ).start()
 
-        @pl.when(k == 1)
-        def _():
-            if chunks > 1:
-                moved1[1].loaded()
-                moved1[1].run(0)
-
-        @pl.when(k == 2)
-        def _():
-            if chunks > 1:
-                moved2[1].run(1)
-
         return carry
 
     lax.fori_loop(1, heads + 1, own_step, 0)
-    moved1[0].loaded()
-    moved1[0].run(0)
     table_grads[...] = jnp.zeros_like(table_grads)
 
     def finish(k, carry):
-        source = lax.rem(z + k, heads)
+        source = paired(z, lax.rem(k, heads), heads)
         span = pl.ds(pl.multiple_of(source * rows, rows), rows)
         by_row, by_col = shifts(rows, source * group + g)
         total = dq[:, span] * SCALE
@@ -489,20 +557,19 @@
         return carry
 
     lax.fori_loop(1, heads + 1, finish, 0)
+    moved1[0].run(1)
+    for stage in range(2, halve_bits() - 1):
+        for each in moved2 + moved1[:1]:
+            each.run(stage)
+    found = [each.total() for each in moved2]
+    fc2_out[...] = jnp.concatenate(found, axis=0) if chunks > 1 else found[0]
+    fc1_out[...] = moved1[0].total()
     if chunks > 1:
-        moved1[1].run(1)
-    for other in range(2, halve_bits() - 1):
-        for each in moved2:
-            each.run(other)
-    found = [each.total() for each in moved2]
-    fc2_out[...] = (jnp.concatenate(found, axis=0) if chunks > 1 else found[0]).T
-    for other in range(1, halve_bits() - 1):
-        moved1[0].run(other)
-        if chunks > 1 and other > 1:
-            moved1[1].run(other)
-    owned = fc1_out.shape[0] // chunks
-    for n, each in enumerate(moved1):
-        fc1_out[pl.ds(n * owned, owned), :] = each.total()
+        moved1[1].loaded()
+        moved1[1].run(0)
+        fc1_state[...] = moved1[1].stages[0][0][...]
+    moved0.run(0)
+    proj_state[...] = moved0.stages[0][0][...]
     grads[z, 0] = gq_s[z]
     grads[z, pl.ds(1, 2)] = summed[z]
     for h in column:
@@ -516,15 +583,21 @@
     for source in range(heads):
         for mate in mates:
             mate_copy(source, mate).wait_send()
-    for each in moved1 + moved2:
+    for each in moved1 + moved2 + [moved0]:
         each.finish()
 
 
-def attend_back(shape, ga, tables, qaug, bias_rows, kv, o_rows, lse, fc2_state, fc1, fc2):
+def attend_back(shape, ga, tables, qaug, bias_rows, kv, o_rows, lse, fc2_state, fc2_more, fc1, proj):
+    local = proj.shape[2]
     devices, chunks, owned, hidden = fc1.shape
     hbm = pl.BlockSpec(memory_space=pl.ANY)
-    moving = halve_bufs(owned, hidden, first=1)
-    moving += halve_bufs(owned, hidden, own=True) * (3 if chunks > 1 else 1)
+    moving = halve_bufs(owned, hidden, first=2)
+    if chunks > 1:
+        moving += halve_bufs(owned, hidden, first=1)
+    moving += halve_bufs(chunks * owned, local, last=0)
+    moving += halve_bufs(owned, hidden, own=True)
+    if chunks > 1:
+        moving += halve_bufs(owned, hidden, last=0, own=True)
     heads, group, rows, queries = shape.heads, shape.group, shape.rows, shape.queries
     vmem = pl.BlockSpec(memory_space=pltpu.VMEM)
     dma = pltpu.SemaphoreType.DMA
@@ -533,11 +606,13 @@
         out_shape=(
             jax.ShapeDtypeStruct((heads, 3, HEAD, rows), LOW),
             jax.ShapeDtypeStruct((2, 2 * SIDE, 128), F32),
+            jax.ShapeDtypeStruct((owned, hidden), F32),
             jax.ShapeDtypeStruct((chunks * owned, hidden), F32),
-            jax.ShapeDtypeStruct((hidden, chunks * owned), F32),
+            jax.ShapeDtypeStruct((devices // 2, owned, hidden), LOW),
+            jax.ShapeDtypeStruct((devices // 2, chunks * owned, local), LOW),
         ),
-        in_specs=[vmem] * 8 + [hbm] * 2,
-        out_specs=(vmem,) * 4,
+        in_specs=[vmem] * 9 + [hbm, vmem],
+        out_specs=(vmem,) * 6,
         scratch_shapes=[
             pltpu.VMEM((heads, HEAD, rows), LOW),
             pltpu.VMEM((AUG, queries), LOW),
@@ -563,10 +638,10 @@
             dma((heads,)), dma((heads,)), dma((heads,)), dma((heads,)),
         ] + moving,
         compiler_params=pltpu.CompilerParams(
-            collective_id=2, has_side_effects=True, vmem_limit_bytes=VMEM_LIMIT
+            collective_id=2, has_side_effects=True, vmem_limit_bytes=VMEM_LIMIT["attend_back"]
         ),
         name="attend_back",
-    )(ga, tables, qaug, bias_rows, kv, o_rows, lse, fc2_state, fc1, fc2)
+    )(ga, tables, qaug, bias_rows, kv, o_rows, lse, fc2_state, fc2_more, fc1, proj)
 
 
 def send_tensor(src, dst, send_sem, recv_sem, dev):
@@ -591,9 +666,9 @@
     return far + [line * 2 + 1 - core]
 
 
-def part_bufs(lines, share, width):
+def part_bufs(lines, share, width, dtype=LOW):
     dma = pltpu.SemaphoreType.DMA
-    return [pltpu.VMEM((lines, share, width), LOW)] * 3 + [dma((lines,))] * 4
+    return [pltpu.VMEM((lines, share, width), dtype)] * 3 + [dma((lines,))] * 4
 
 
 class Reduce:
@@ -622,7 +697,7 @@
     def pass_on(self, to):
         self.mate_copy(to).wait_recv()
         both = self.part[to * 2 + self.core].astype(F32) + self.mate_in[to].astype(F32)
-        self.passed[to] = both.astype(LOW)
+        self.passed[to] = both.astype(self.passed.dtype)
         self.line_copy(to, self.line).start()
 
     def others(self):
@@ -720,7 +795,7 @@
         self.z, self.g = me // self.group, lax.rem(me, self.group)
 
     def column(self):
-        return [lax.rem(self.z + k, self.heads) for k in range(1, self.heads)]
+        return [paired(self.z, k, self.heads) for k in range(1, self.heads)]
 
     def mates(self):
         return [lax.rem(self.g + k, self.group) for k in range(1, self.group)]
@@ -818,8 +893,8 @@
             self.source.at[pl.ds(0, self.count(0))], self.own[0], self.own[1]
         ).wait()
 
-    def start(self):
-        for at in self.spots(self.first):
+    def start(self, only=slice(None)):
+        for at in self.spots(self.first)[only]:
             self.copy(self.first, at).start()
 
     def kept(self, stage, at):
@@ -847,8 +922,8 @@
 
 
 def middle_kernel(
-    heads, att, proj_w, tokens, cot, fc1_hbm, fc2_hbm, fc1_bias, vectors,
-    output, middle_out, fc1_out, fc2_out, proj_out, ga_out, fc1_bias_out, sums_out, fc2_state,
+    heads, att, proj_w, tokens, cot, fc1_hbm, fc2_hbm, vectors,
+    output, middle_out, fc1_out, proj_out, ga_out, fc1_bias_out, sums_out, fc2_state, fc2_more,
     fc1, fc2, att_tok, branch, mlp, back, n2, act, gu, gb, outs, held, spread,
     wide, load1, load2, *rest,
 ):
@@ -869,9 +944,13 @@
     all_n2 = Gather(n2, *rest[21:24])
     all_gb = Gather(gb, *rest[24:27])
     all_out = Gather(outs, *rest[27:30])
-    devices, chunks, owned, _ = fc2_out.shape
-    blocks = rest[30]
-    moved = Halve(near_first(), blocks, rest[31:], last=0)
+    blocks2, blocks1, fc1_sem = rest[30:33]
+    devices, chunks, owned, _ = blocks2.shape
+    moved = [
+        Halve(near_first(), blocks2.at[:, n], rest[36 + 3 * n : 39 + 3 * n], last=0)
+        for n in range(1, chunks)
+    ]
+    moved = [Halve(near_first(), blocks2.at[:, 0], rest[33:39], last=1)] + moved
     att_tok[...] = att[...].T.reshape(att_tok.shape)
 
     def project(k, carry):
@@ -914,7 +993,7 @@
 
         def tile(n, inner):
             span = pl.ds(pl.multiple_of(n * step, step), step)
-            up = nn(inputs, fc1[:, span]) + fc1_bias[:, span]
+            up = nn(inputs, fc1[:, span]) + vectors[6:7, span]
             phi = 0.5 + 0.5 * lax.erf(up * math.sqrt(0.5))
             slope = phi + up * (jnp.exp(-0.5 * up * up) * (2 * math.pi) ** -0.5)
             act[pair, :, span] = (up * phi).astype(LOW).reshape(2, share, step)
@@ -934,6 +1013,30 @@
         lax.fori_loop(0, width // dstep, tile_back, 0)
         sum_back.give(at)
 
+        return carry
+
+    lax.fori_loop(0, lines, hidden_part, 0)
+
+    def weights2(n, carry):
+        span = pl.ds(pl.multiple_of(n * dstep, dstep), dstep)
+        found = tn(cot[:, :, span].reshape(rows, dstep), act[...].reshape(rows, hidden))
+        wide[span, :] = found.astype(LOW)
+        return carry
+
+    lax.fori_loop(0, width // dstep, weights2, 0)
+    for dev in range(devices):
+        for chunk in range(chunks):
+            at = (dev * chunks + chunk) * owned
+            blocks2[dev, chunk] = wide[pl.ds(at, owned), :]
+    for each in moved:
+        each.start()
+    for other in sum_back.others():
+        sum_back.pass_on(other)
+
+    def out_part(k, carry):
+        at = lax.rem(line + 1 + k, lines)
+        pair = pl.ds(at * 2, 2)
+
         def tile_out(n, inner):
             span = pl.ds(pl.multiple_of(n * dstep, dstep), dstep)
             found = nn(act[pair].reshape(2 * share, hidden), fc2[:, span])
@@ -944,25 +1047,21 @@
         sum_mlp.give(at)
         return carry
 
-    lax.fori_loop(0, lines, hidden_part, 0)
-    for other in sum_back.others():
-        sum_back.pass_on(other)
-
-    def weights2(n, carry):
+    lax.fori_loop(0, lines, out_part, 0)
+
+    def weights1(n, carry):
         span = pl.ds(pl.multiple_of(n * dstep, dstep), dstep)
-        found = tn(cot[:, :, span].reshape(rows, dstep), act[...].reshape(rows, hidden))
+        found = tn(n2[:, :, span].reshape(rows, dstep), gu[...].reshape(rows, hidden))
         wide[span, :] = found.astype(LOW)
         return carry
 
-    lax.fori_loop(0, width // dstep, weights2, 0)
+    lax.fori_loop(0, width // dstep, weights1, 0)
     for dev in range(devices):
         for chunk in range(chunks):
             at = (dev * chunks + chunk) * owned
-            fc2_out[dev, chunk] = wide[pl.ds(at, owned), :]
-        blocks[dev] = wide[pl.ds(dev * chunks * owned, owned), :]
-    moved.start()
-    for other in sum_mlp.others():
-        sum_mlp.pass_on(other)
+            blocks1[dev, chunk] = wide[pl.ds(at, owned), :]
+    keep_fc1 = pltpu.make_async_copy(blocks1, fc1_out, fc1_sem)
+    keep_fc1.start()
     upstream = sum_back.total()
     sums_out[0:1] = jnp.sum(upstream * held[1], axis=0, keepdims=True)
     sums_out[1:2] = jnp.sum(upstream, axis=0, keepdims=True)
@@ -972,25 +1071,14 @@
     middle_out[...] = grad_middle
     gb[me] = grad_middle.astype(LOW)
     all_gb.start()
+    for other in sum_mlp.others():
+        sum_mlp.pass_on(other)
     outs[me] = (held[0] + sum_mlp.total() + vectors[3:4]).astype(LOW)
     all_out.start()
 
-    def weights1(n, carry):
-        span = pl.ds(pl.multiple_of(n * dstep, dstep), dstep)
-        found = tn(n2[:, :, span].reshape(rows, dstep), gu[...].reshape(rows, hidden))
-        wide[span, :] = found.astype(LOW)
-        return carry
-
-    lax.fori_loop(0, width // dstep, weights1, 0)
-    for dev in range(devices):
-        for chunk in range(chunks):
-            at = (dev * chunks + chunk) * owned
-            fc1_out[dev, chunk] = wide[pl.ds(at, owned), :]
     sums_out[2:3] = jnp.sum(cot[...].astype(F32).reshape(rows, width), axis=0, keepdims=True)
     for other in all_gb.others():
         all_gb.forward(other)
-    for other in all_out.others():
-        all_out.forward(other)
     all_gb.take(line)
     for other in all_gb.others():
         all_gb.take(other)
@@ -1007,17 +1095,24 @@
     lax.fori_loop(0, width // dstep, weights0, 0)
     for dev in range(devices):
         proj_out[dev] = wide[pl.ds(dev * chunks * owned, chunks * owned), :local]
+    moved[0].run(0)
+    for other in all_out.others():
+        all_out.forward(other)
     all_out.take(line)
     for other in all_out.others():
         all_out.take(other)
     output[...] = outs[...]
-    moved.run(0)
-    fc2_state[...] = moved.stages[0][0][...]
-    for each in (sum_branch, sum_mlp, sum_back, all_n2, all_gb, all_out, moved):
+    moved[0].run(1)
+    fc2_state[...] = moved[0].stages[1][0][...]
+    for n, each in enumerate(moved[1:]):
+        each.run(0)
+        fc2_more[...] = each.stages[0][0][...]
+    keep_fc1.wait()
+    for each in (sum_branch, sum_mlp, sum_back, all_n2, all_gb, all_out, *moved):
         each.finish()
 
 
-def middle_block(heads, att, proj_w, tokens, cot, fc1, fc2, fc1_bias, vectors):
+def middle_block(heads, att, proj_w, tokens, cot, fc1, fc2, vectors):
     count = lax.axis_size("tensor")
     lines = count // 2
     local, width = proj_w.shape
@@ -1051,31 +1146,31 @@
         dma,
     ]
     scratch += part_bufs(lines, share, width) * 3 + gather_sems(lines) * 3
-    scratch += [pltpu.VMEM((devices, owned // chunks, hidden), LOW)]
-    scratch += halve_bufs(owned // chunks, hidden, last=0)
+    scratch += [pltpu.VMEM(weights, LOW), pltpu.VMEM(weights, LOW), dma]
+    scratch += halve_bufs(owned // chunks, hidden, last=1)
+    scratch += halve_bufs(owned // chunks, hidden, last=0) * (chunks - 1)
     return pl.pallas_call(
         functools.partial(middle_kernel, heads),
         out_shape=(
             jax.ShapeDtypeStruct(whole, LOW),
             jax.ShapeDtypeStruct((share, width), F32),
             jax.ShapeDtypeStruct(weights, LOW),
-            jax.ShapeDtypeStruct(weights, LOW),
             jax.ShapeDtypeStruct((devices, owned, local), LOW),
             jax.ShapeDtypeStruct((local, rows), LOW),
             jax.ShapeDtypeStruct((1, hidden), F32),
             jax.ShapeDtypeStruct((8, width), F32),
+            jax.ShapeDtypeStruct((devices // 4, owned // chunks, hidden), LOW),
             jax.ShapeDtypeStruct((devices // 2, owned // chunks, hidden), LOW),
         ),
-        in_specs=[vmem] * 4 + [hbm] * 2 + [vmem] * 2,
-        out_specs=(vmem,) * 9,
+        in_specs=[vmem] * 4 + [hbm] * 2 + [vmem],
+        out_specs=(vmem,) * 2 + (hbm,) + (vmem,) * 6,
         scratch_shapes=scratch,
         compiler_params=pltpu.CompilerParams(
-            collective_id=3, has_side_effects=True, vmem_limit_bytes=VMEM_LIMIT
+            collective_id=3, has_side_effects=True, vmem_limit_bytes=VMEM_LIMIT["middle"]
         ),
         name="middle",
     )(
-        att, proj_w, tokens.reshape(whole), cot.reshape(whole), fc1, fc2,
-        fc1_bias.reshape(1, hidden), vectors,
+        att, proj_w, tokens.reshape(whole), cot.reshape(whole), fc1, fc2, vectors,
     )
 
 
@@ -1148,8 +1243,9 @@
 
 
 def tail_kernel(
-    heads, grads, qkv_w, n1_t, tokens, grad_middle, vectors, tables, sums, fc1_bias, peak, proj,
-    tokens_out, proj_out, qkv_out, tables_out, sums_out, late_out, dp_out,
+    heads, grads, qkv_w, n1_t, tokens, grad_middle, vectors, tables, sums, fc1_bias, peak,
+    proj_state, fc1_half, fc1_state,
+    tokens_out, proj_out, fc1_out, qkv_out, tables_out, rows_out, clip_out,
     g_all, g_tok, part, gt, *rest,
 ):
     ring = Ring(heads)
@@ -1170,20 +1266,30 @@
     blocks = [taken(1)[0] for _ in range(chunks)]
     orders = [near_first(), far_first(ring.group)]
     moved3 = [Halve(orders[n], blocks[n], taken(3 * halve_bits())) for n in range(chunks)]
-    moved0 = Halve(near_first(), proj, taken(3 * halve_bits()))
+    moved0 = Halve(near_first(), proj_state, taken(3 * (halve_bits() - 1)), first=1)
+    moved1 = []
+    if chunks > 1:
+        moved1 = [Halve(near_first(), fc1_state, taken(3 * (halve_bits() - 1)), first=1)]
     sum_part = Reduce(part, *taken(7))
     all_gt = Gather(gt, *taken(3))
-    small_tables = Small(ring, EVERY, lax.add, *taken(16))
-    small_sums = Small(ring, EVERY, lax.add, *taken(16))
+    pool, pooled = taken(2)
+    sum_pool = Reduce(pool, *taken(7))
+    all_pool = Gather(pooled, *taken(3))
+    small_pool = Small(ring, OVER_DP, lax.add, *taken(8))
     small_late = Small(ring, EVERY, lax.add, *taken(16))
     small_dp = Small(ring, OVER_DP, add_peaks, *taken(8))
-    small_tables.start(0, tables[...].reshape(4 * SIDE, 128))
-    small_sums.start(0, sums[...])
+    pool[...] = tables[...].reshape(pool.shape)
+    for other in sum_pool.others() + [line]:
+        sum_pool.give(other)
+    for each in moved1:
+        each.start()
     moved0.start()
     for t in range(3):
         for h in range(heads):
             g_all[pl.ds(t * local + h * HEAD, HEAD), :] = grads[h, t]
     g_tok[...] = g_all[...].T.reshape(g_tok.shape)
+    for other in sum_pool.others():
+        sum_pool.pass_on(other)
     whole = g_tok[...].reshape(rows, 3 * local)
     lane = lax.broadcasted_iota(jnp.int32, (1, width), 1)
     peaks = jnp.where(lane == ring.z, peak[0:1, 0:1], -jnp.inf)
@@ -1191,24 +1297,6 @@
     dp_rows = [widen(fc1_bias[...], width), widen(bias_sums, width), peaks]
     small_dp.start(0, jnp.concatenate(dp_rows + [jnp.zeros((5, width), F32)], axis=0))
 
-    def norm_part(k, carry):
-        at = lax.rem(line + 1 + k, lines)
-        pair = pl.ds(at * 2, 2)
-
-        def tile(n, inner):
-            span = pl.ds(pl.multiple_of(n * dstep, dstep), dstep)
-            found = nt(g_tok[pair].reshape(2 * share, 3 * local), qkv_w[span, :])
-            part[pair, :, span] = found.astype(LOW).reshape(2, share, dstep)
-            return inner
-
-        lax.fori_loop(0, width // dstep, tile, 0)
-        sum_part.give(at)
-        return carry
-
-    lax.fori_loop(0, lines, norm_part, 0)
-    for other in sum_part.others():
-        sum_part.pass_on(other)
-
     for n in range(chunks):
 
         def weight_part(dev, carry):
@@ -1217,53 +1305,112 @@
             return carry
 
         lax.fori_loop(0, devices, weight_part, 0)
+        if n == 0:
+            small_pool.start(0, sum_pool.total())
+        if n == chunks - 1:
+            small_pool.step(0)
+            small_dp.step(0)
         moved3[n].start()
-    small_tables.step(0)
-    small_sums.step(0)
+
+    def norm_part(k, carry):
+        at = lax.rem(line + 1 + k, lines)
+        pair = pl.ds(at * 2, 2)
+
+        def tile(n, inner):
+            span = pl.ds(pl.multiple_of(n * dstep, dstep), dstep)
+            found = nn(g_tok[pair].reshape(2 * share, 3 * local), qkv_w[:, span])
+            part[pair, :, span] = found.astype(LOW).reshape(2, share, dstep)
+            return inner
+
+        lax.fori_loop(0, width // dstep, tile, 0)
+        sum_part.give(at)
+        return carry
+
+    lax.fori_loop(0, lines, norm_part, 0)
+    for other in sum_part.others():
+        sum_part.pass_on(other)
     scaled, inverse = normed(tokens[me].astype(F32))
+    moved0.run(1)
+    for each in moved1:
+        each.run(1)
     upstream = sum_part.total()
     late = [
+        sums[0:4],
         jnp.sum(upstream * scaled, axis=0, keepdims=True),
         jnp.sum(upstream, axis=0, keepdims=True),
-        jnp.zeros((6, width), F32),
+        jnp.zeros((2, width), F32),
     ]
     small_late.start(0, jnp.concatenate(late, axis=0))
-    found = grad_middle[...] + normed_back(upstream, scaled, inverse, vectors[0:1])
+    found = grad_middle[...] + normed_back(upstream, scaled, inverse, vectors[4:5])
     gt[me] = found.astype(LOW)
     all_gt.start()
-    small_tables.step(1)
-    small_sums.step(1)
+    pooled[me] = small_pool.take(1)
+    all_pool.start()
+    moved3[0].run(0)
     small_late.step(0)
-    small_dp.step(0)
-    moved0.run(0)
+    for each in moved3[1:]:
+        each.run(0)
     small_late.step(1)
     for other in all_gt.others():
         all_gt.forward(other)
-    for each in moved3:
-        each.run(0)
-    small_tables.step(2)
-    small_sums.step(2)
+    for other in all_pool.others():
+        all_pool.forward(other)
+    dp_sum = small_dp.take(1)
+    limit = vectors[9:10]
+    factors = jnp.sqrt(limit / jnp.maximum(dp_sum[2:3], limit))
+    lane = lax.broadcasted_iota(jnp.int32, (1, width), 1)
+    clipped_bias = vectors[7:8]
+    for h in range(heads):
+        factor = factors[:, h : h + 1]
+        own = (lane >= h * HEAD) & (lane < (h + 1) * HEAD)
+        clipped_bias = jnp.where(own, clipped_bias * factor, clipped_bias)
+        for t in range(2):
+            span = pl.ds(t * local + h * HEAD, HEAD)
+            clip_out[span, :] = (qkv_w[span, :].astype(F32) * factor).astype(LOW)
+    rows_out[8:11] = dp_sum[0:3]
+    rows_out[11:12] = factors
+    rows_out[12:13] = clipped_bias
+    rows_out[13:16] = jnp.zeros((3, width), F32)
+    moved3[0].run(1)
     small_late.step(2)
-    for stage in range(1, halve_bits() - 1):
-        moved0.run(stage)
-        for each in moved3:
+    for each in moved3[1:]:
+        each.run(1)
+    for stage in range(2, halve_bits() - 1):
+        for each in moved3 + [moved0] + moved1:
             each.run(stage)
-    all_gt.take(line)
-    for other in all_gt.others():
+    for other in all_gt.others() + [line]:
         all_gt.take(other)
+    for other in all_pool.others() + [line]:
+        all_pool.take(other)
     tokens_out[...] = gt[...]
-    dp_out[...] = small_dp.take(1)
-    tables_out[...] = small_tables.take(3)
-    sums_out[...] = small_sums.take(3)
-    late_out[...] = small_late.take(3)
-    proj_out[...] = moved0.total().T
+    for n in range(2):
+        turned_sums = pooled[...].reshape(2, 2 * SIDE, 128)[n].T[:HEAD]
+        found = jnp.zeros((HEAD, 2 * SIDE), F32)
+        for piece in parts_of(turned_sums, 3):
+            found = found + nn(piece.astype(LOW), turned(2 * SIDE))
+        tables_out[n] = found
+    late = small_late.take(3)
+    row = lax.broadcasted_iota(jnp.int32, late.shape, 0)
+    rows_out[0:8] = jnp.where((row == 2) | (row == 3), late * (1.0 / count), late)
+    owned = fc1_half.shape[0]
+    fc1_out[0:owned] = fc1_half[...]
+    for each in moved1:
+        fc1_out[pl.ds(owned, owned), :] = each.total()
+    proj_out[...] = moved0.total()
     for n, each in enumerate(moved3):
-        qkv_out[n] = each.total()
-    for each in [moved0, sum_part, all_gt, small_tables, small_sums, small_late, small_dp] + moved3:
+        total = each.total()
+        owned = total.shape[0]
+        for t in range(3):
+            qkv_out[t, pl.ds(n * owned, owned), :] = total[:, t * local : (t + 1) * local]
+    for each in [
+        moved0, sum_part, all_gt, sum_pool, all_pool, small_pool, small_late, small_dp,
+    ] + moved3 + moved1:
+
         each.finish()
 
 
-def tail(heads, grads, qkv_w, n1_t, tokens, grad_middle, vectors, tables, sums, fc1_bias, peak, proj):
+def tail(heads, grads, qkv_w, n1_t, tokens, grad_middle, vectors, tables, sums, fc1_bias, peak, proj_state, fc1_half, fc1_state):
+    hidden = fc1_half.shape[1]
     count = lax.axis_size("tensor")
     lines = count // 2
     local = heads * HEAD
@@ -1280,33 +1427,88 @@
     ]
     scratch += [pltpu.VMEM((devices, owned, 3 * local), LOW)] * chunks
     scratch += halve_bufs(owned, 3 * local) * chunks
-    scratch += halve_bufs(chunks * owned, local)
+    scratch += halve_bufs(chunks * owned, local, first=1)
+    if chunks > 1:
+        scratch += halve_bufs(owned, hidden, first=1)
     scratch += part_bufs(lines, share, width) + gather_sems(lines)
-    scratch += small_bufs(heads, EVERY, (4 * SIDE, 128))
-    scratch += small_bufs(heads, EVERY, (8, width)) * 2
+    pool = (count, 4 * SIDE // count, 128)
+    scratch += [pltpu.VMEM(pool, F32)] * 2
+    scratch += part_bufs(lines, *pool[1:], F32) + gather_sems(lines)
+    scratch += small_bufs(heads, OVER_DP, pool[1:])
+    scratch += small_bufs(heads, EVERY, (8, width))
     scratch += small_bufs(heads, OVER_DP, (8, width))
     return pl.pallas_call(
         functools.partial(tail_kernel, heads),
         out_shape=(
             jax.ShapeDtypeStruct(whole, LOW),
-            jax.ShapeDtypeStruct((local, chunks * owned), F32),
-            jax.ShapeDtypeStruct((chunks, owned, 3 * local), F32),
-            jax.ShapeDtypeStruct((4 * SIDE, 128), F32),
-            jax.ShapeDtypeStruct((8, width), F32),
-            jax.ShapeDtypeStruct((8, width), F32),
-            jax.ShapeDtypeStruct((8, width), F32),
+            jax.ShapeDtypeStruct((chunks * owned, local), F32),
+            jax.ShapeDtypeStruct((chunks * owned, hidden), F32),
+            jax.ShapeDtypeStruct((3, chunks * owned, local), F32),
+            jax.ShapeDtypeStruct((2, HEAD, 2 * SIDE), F32),
+            jax.ShapeDtypeStruct((16, width), F32),
+            jax.ShapeDtypeStruct((2 * local, width), LOW),
         ),
-        in_specs=[vmem] * 11,
+        in_specs=[vmem] * 13,
         out_specs=(vmem,) * 7,
         scratch_shapes=scratch,
         compiler_params=pltpu.CompilerParams(
-            collective_id=4, has_side_effects=True, vmem_limit_bytes=VMEM_LIMIT
+            collective_id=4, has_side_effects=True, vmem_limit_bytes=VMEM_LIMIT["tail"]
         ),
         name="tail",
     )(
         grads, qkv_w, n1_t, tokens.reshape(whole), grad_middle, vectors, tables, sums, fc1_bias,
-        peak, proj,
+        peak, proj_state, fc1_half, fc1_state,
     )
+
+
+def finish_kernel(count, *refs):
+    large, (rows, tables), refs = refs[:count], refs[count : count + 2], refs[count + 2 :]
+    outs, smalls, stage = refs[:count], refs[count : count + 13], refs[count + 13 :]
+    sems_in, sems_out = stage[count], stage[count + 1]
+    into = [pltpu.make_async_copy(a, b, sems_in.at[n]) for n, (a, b) in enumerate(zip(large, stage))]
+    out = [pltpu.make_async_copy(b, c, sems_out.at[n]) for n, (b, c) in enumerate(zip(stage, outs))]
+    for copy in into:
+        copy.start()
+    gain1, shift1, qv, proj, by_row, by_col, gain2, shift2, fc1, fc2, clip_bias, peaks, factors = smalls
+    picks = (
+        (gain2, 0), (shift2, 1), (fc2, 2), (proj, 3), (gain1, 4), (shift1, 5), (fc1, 8),
+        (peaks, 10), (factors, 11), (clip_bias, 12),
+    )
+    for ref, at in picks:
+        ref[...] = rows[at : at + 1, : ref.shape[0]].reshape(ref.shape)
+    local = qv.shape[1]
+    qv[0:1] = rows[9:10, :local]
+    qv[1:2] = rows[9:10, 2 * local : 3 * local]
+    by_row[...] = tables[0, :, : by_row.shape[1]]
+    by_col[...] = tables[1, :, : by_col.shape[1]]
+    for copy, after in zip(into, out):
+        copy.wait()
+        after.start()
+    for copy in out:
+        copy.wait()
+
+
+def finish(large, rows, tables, hidden, local):
+    width = rows.shape[1]
+    heads = local // HEAD
+    vmem = pl.BlockSpec(memory_space=pltpu.VMEM)
+    hbm = pl.BlockSpec(memory_space=pl.ANY)
+    count = len(large)
+    shapes = [
+        (width,), (width,), (2, local), (width,), (HEAD, 2 * SIDE - 1), (HEAD, 2 * SIDE - 1),
+        (width,), (width,), (hidden,), (width,), (local,), (heads,), (heads,),
+    ]
+    return pl.pallas_call(
+        functools.partial(finish_kernel, count),
+        out_shape=[jax.ShapeDtypeStruct(each.shape, each.dtype) for each in large]
+        + [jax.ShapeDtypeStruct(each, F32) for each in shapes],
+        in_specs=[hbm] * count + [vmem] * 2,
+        out_specs=[hbm] * count + [vmem] * len(shapes),
+        scratch_shapes=[pltpu.VMEM(each.shape, each.dtype) for each in large]
+        + [pltpu.SemaphoreType.DMA((count,))] * 2,
+        compiler_params=pltpu.CompilerParams(vmem_limit_bytes=VMEM_LIMIT["finish"]),
+        name="finish",
+    )(*large, rows, tables)
 
 
 def on_device(
@@ -1332,86 +1534,88 @@
     token_count = images * row_count
     local_width = qkv_weight.shape[2]
     local_heads = local_width // HEAD
-    groups = lax.axis_size("tensor")
-    residual_in = tokens.reshape(token_count, model_width).astype(jnp.float32)
-    scaled1, _ = normed(residual_in)
-    normed1_low = (scaled1 * norm1_gain + norm1_shift).astype(jnp.bfloat16)
     shape = Shape(local_heads, lax.axis_size("dp") // local_heads, row_count)
-    flipped = jnp.stack([table_rows, table_cols])[:, ::-1]
-    flipped = jnp.pad(flipped, ((0, 0), (0, 1), (0, 0)))
-    triple = jnp.einsum("dtc,nd->tcn", qkv_weight, normed1_low, preferred_element_type=jnp.float32)
-    bias = jnp.stack([qv_bias[0], jnp.zeros_like(qv_bias[0]), qv_bias[1]])
-    triple = (triple + bias[:, :, None]).astype(jnp.bfloat16)
-    qkv = triple.reshape(3, local_heads, HEAD, row_count).transpose(1, 0, 2, 3)
-    attended, qaug, bias_rows, kv, o_rows, lse, peak = attend(shape, qkv, flipped)
-    grad_out = cotangent.reshape(token_count, model_width)
-    vectors = jnp.stack([proj_bias, norm2_gain, norm2_shift, fc2_bias])
-    vectors = jnp.pad(vectors, ((0, 4), (0, 0)))
+    flat = tokens.reshape(token_count, model_width)
+
+    listed = (
+        proj_bias, norm2_gain, norm2_shift, fc2_bias, norm1_gain, norm1_shift, fc1_bias, qv_bias,
+        threshold,
+    )
+    weights = qkv_weight.transpose(1, 2, 0).reshape(3 * local_width, model_width)
+    attended, qaug, bias_rows, kv, o_rows, lse, peak, normed1, tables, vectors = attend(
+        shape, flat, weights, listed, table_rows.T, table_cols.T
+    )
     (
         output,
         grad_middle,
         grad_fc1,
-        grad_fc2,
         grad_proj,
         grad_attended,
         grad_fc1_bias,
         sums,
         fc2_state,
+        fc2_more,
     ) = middle_block(
         local_heads,
         attended.reshape(local_width, token_count),
         proj_weight,
-        tokens.reshape(token_count, model_width),
-        grad_out,
+        flat,
+        cotangent.reshape(token_count, model_width),
         fc1_weight,
         fc2_weight,
-        fc1_bias,
         vectors,
     )
     grad_heads = grad_attended.reshape(local_heads, HEAD, row_count)
     devices, chunks, owned, _ = grad_fc1.shape
-    grad_triple, table_terms, grad_fc1, grad_fc2 = attend_back(
-        shape, grad_heads, flipped, qaug, bias_rows, kv, o_rows, lse, fc2_state, grad_fc1, grad_fc2
+    grad_triple, table_terms, fc1_half, grad_fc2, fc1_state, proj_state = attend_back(
+        shape, grad_heads, tables, qaug, bias_rows, kv, o_rows, lse, fc2_state, fc2_more, grad_fc1,
+        grad_proj,
     )
-    tail_vectors = jnp.pad(norm1_gain[None], ((0, 7), (0, 0)))
-    (
-        grad_tokens,
-        grad_proj,
-        grad_qkv,
-        table_sums,
-        sums,
-        late,
-        dp_sums,
-    ) = tail(
+    grad_tokens, grad_proj, grad_fc1, grad_qkv, table_sums, rows, clipped = tail(
         local_heads,
         grad_triple,
-        qkv_weight.reshape(model_width, 3 * local_width),
-        normed1_low.T.reshape(devices, chunks, owned, token_count),
-        tokens.reshape(token_count, model_width),
+        weights,
+        normed1.reshape(devices, chunks, owned, token_count),
+        flat,
         grad_middle,
-        tail_vectors,
+        vectors,
         table_terms,
         sums,
         grad_fc1_bias,
         peak,
+        proj_state,
+        fc1_half,
+        fc1_state,
+    )
+    large = (output, grad_tokens, grad_fc1, grad_fc2, grad_qkv, clipped, grad_proj)
+    (
+        output,
+        grad_tokens,
+        grad_fc1,
+        grad_fc2,
+        grad_qkv,
+        clipped,
         grad_proj,
-    )
+        grad_norm1_gain,
+        grad_norm1_shift,
+        grad_qv_bias,
+        grad_proj_bias,
+        grad_rows_t,
+        grad_cols_t,
+        grad_norm2_gain,
+        grad_norm2_shift,
+        grad_fc1_bias,
+        grad_fc2_bias,
+        clipped_q_bias,
+        head_peaks,
+        clip_factors,
+    ) = finish(large, rows, table_sums, fc1_bias.shape[0], local_width)
+    output = output.reshape(images, row_count, model_width)
     grad_tokens = grad_tokens.reshape(images, row_count, model_width)
-    grad_qkv = grad_qkv.reshape(model_width // devices, 3, local_width)
-    table_sums = table_sums.reshape(2, 2 * SIDE, 128)[:, 2 * SIDE - 2 :: -1, :HEAD]
-    grad_table_rows, grad_table_cols = table_sums[0], table_sums[1]
-    grad_norm2_gain, grad_norm2_shift = sums[0], sums[1]
-    grad_fc2_bias, grad_proj_bias = sums[2] / groups, sums[3] / groups
-    grad_norm1_gain, grad_norm1_shift = late[0], late[1]
-    grad_fc1_bias = dp_sums[0, : fc1_bias.shape[0]]
-    grad_qv_bias = dp_sums[1, : 3 * local_width].reshape(3, local_width)[0::2]
-    head_peaks = dp_sums[2, :local_heads]
-    limit = threshold[0]
-    clip_factors = jnp.sqrt(limit / jnp.maximum(head_peaks, limit))
-    spread_factors = jnp.repeat(clip_factors, HEAD)
-    clipped_qk = (qkv_weight[:, :2, :].astype(jnp.float32) * spread_factors).astype(jnp.bfloat16)
-    clipped_q_bias = qv_bias[0] * spread_factors
-    output = output.reshape(images, row_count, model_width)
+    grad_qkv = grad_qkv.transpose(1, 0, 2)
+    grad_fc2, grad_proj = grad_fc2.T, grad_proj.T
+    grad_table_rows, grad_table_cols = grad_rows_t.T, grad_cols_t.T
+    clipped_qk = clipped.reshape(2, local_width, model_width).transpose(2, 0, 1)
     return (
         output,
         grad_tokens,

time: 345 us -> 268 us (0.78)
  Pallas kernels: 304 us -> 262 us
  local copies, waits for them, and re-layouts: 24.2 us -> 1.9 us
  other arithmetic: 10.6 us -> 0 us
    pallas_call x1, Pallas kernels: 97.4 us -> 65.7 us  [attend_back(): pl.pallas_call(functools.partial(backward_kernel, shape), out_shape=(jax....]
    pallas_call x1, Pallas kernels: 76.9 us -> 65.4 us  [tail(): pl.pallas_call(functools.partial(tail_kernel, heads), out_shape=(jax.Shap...]
    reshape x4 -> x0, local copies, waits for them, and re-layouts: 6.73 us -> none  [the longest x1 3.59 us: on_device(): qkv_weight.reshape(model_width, 3 * local_width)]
    unnamed x46 -> x28, local copies, waits for them, and re-layouts: 7.83 us -> 1.9 us
    slice x7 -> x0, local copies, waits for them, and re-layouts: 5.09 us -> none  [the longest x1 1.48 us: on_device(): grad_norm1_gain, grad_norm1_shift = (late[0], late[1])]
    pallas_call x1 -> x2, Pallas kernels: 57.2 us -> 57.3 us  [the longest x1 52.3 us: attend(): pl.pallas_call(functools.partial(forward_kernel, shape, len(args), 10), o...]
where the time goes in v4:
time: 268 us; the launch traced here: 266 us
  Pallas kernels  262 us (98%)
    pallas_call x1, Pallas kernels, middle_block(): pl.pallas_call(functools.partial(middle_kernel, heads), out_shape=(jax.Sh...  73.6 us
    pallas_call x1, Pallas kernels, attend_back(): pl.pallas_call(functools.partial(backward_kernel, shape), out_shape=(jax....  65.7 us
    pallas_call x1, Pallas kernels, tail(): pl.pallas_call(functools.partial(tail_kernel, heads), out_shape=(jax.Shap...  65.4 us
    pallas_call x1, Pallas kernels, attend(): pl.pallas_call(functools.partial(forward_kernel, shape, len(args), 10), o...  52.3 us

profile of v4, /device:TPU:0, one launch (start us, length us, event | category | flops | bytes accessed | tf_op | source)
XLA Modules:
  0.0 265.6 jit_solution(15672209627066589096)
XLA Ops:
  1.3 0.0 copy-start
  1.3 0.0 copy-start.2
  1.3 0.0 copy-start.6
  1.3 52.3 %attend.1 = (bf16[4,80,512]{2,1,0:T(8,128)(2,1)}, bf16[240,2048]{1,0:T(8,128)(2,1)}, bf16[8,16,2048]{2,1,0:T(8,128)(2,1)}, bf16[4,2,2,80,512]{4,3,2,1,0:T(8,128)...) custom-call(bf16[512,1280]{1,0:T(8,128)(2,1)} %bitcast.21, ...), custom_call_target="tpu_custom_call" | custom-call | tf_op jit(solution)/shard_map/attend/pallas_call | solution.py:328
  53.6 0.0 copy-done
  53.7 0.0 copy-done.2
  53.7 0.0 copy-done.6
  53.7 0.0 copy-start.9
  53.7 0.9 copy-done.9
  54.6 1.0 copy-done.10
  55.6 0.0 copy-start.11
  55.6 0.0 copy-start.12
  55.6 73.6 %middle.1 = (bf16[4,128,1280]{2,1,0:T(8,128)(2,1)S(1)}, f32[128,1280]{1,0:T(8,128)S(1)}, bf16[8,2,80,1280]{3,2,1,0:T(8,128)(2,1)S(1)}, bf16[8,160,320]{2,1,0:T(8...) custom-call(bf16[320,512]{1,0:T(8,128)(2,1)S(1)} %bitcast.28, ...), custom_call_target="tpu_custom_call" | custom-call | tf_op jit(solution)/shard_map/middle/pallas_call | solution.py:1152
  129.2 0.0 copy-done.4
  129.2 0.0 copy-done.5
  129.2 0.0 copy-done.7
  129.2 0.0 copy-done.8
  129.2 0.0 copy-done.11
  129.3 0.0 copy-done.12
  129.3 0.0 copy-start.1
  129.3 0.0 copy-start.3
  129.3 65.7 %attend_back.1 = (bf16[4,3,80,512]{3,2,1,0:T(8,128)(2,1)S(1)}, f32[2,128,128]{2,1,0:T(8,128)S(1)}, f32[80,1280]{1,0:T(8,128)S(1)}, f32[160,1280]{1,0:T(8,128)S(1...) custom-call(bf16[4,80,512]{2,1,0:T(8,128)(2,1)S(1)} %bitcast.29, ...), custom_call_target="tpu_custom_call" | custom-call | tf_op jit(solution)/shard_map/attend_back/pallas_call | solution.py:604
  195.0 65.4 %tail.1 = (bf16[4,128,1280]{2,1,0:T(8,128)(2,1)S(1)}, f32[160,320]{1,0:T(8,128)S(1)}, f32[160,1280]{1,0:T(8,128)S(1)}, f32[3,160,320]{2,1,0:T(8,128)S(1)}, f32[2...) custom-call(bf16[4,3,80,512]{3,2,1,0:T(8,128)(2,1)S(1)} %get-tuple-element.86.grads, ...), custom_call_target="tpu_custom_call" | custom-call | tf_op jit(solution)/shard_map/tail/pallas_call | solution.py:1440
  260.5 5.0 %finish.1 = (bf16[4,128,1280]{2,1,0:T(8,128)(2,1)}, bf16[4,128,1280]{2,1,0:T(8,128)(2,1)}, f32[160,1280]{1,0:T(8,128)}, f32[160,1280]{1,0:T(8,128)}, f32[3,160,3...) custom-call(bf16[4,128,1280]{2,1,0:T(8,128)(2,1)S(1)} %get-tuple-ele, ...), custom_call_target="tpu_custom_call" | custom-call | tf_op jit(solution)/shard_map/finish/pallas_call | solution.py:1501
  (9 shorter events, 0.0 us)
Async XLA Ops:
  1.3 52.3 %copy-start = (bf16[1,512,1280]{2,1,0:T(8,128)(2,1)S(1)}, bf16[1,512,1280]{2,1,0:T(8,128)(2,1)}, u32[]{:S(2)}) copy-start(bf16[1,512,1280]{2,1,0:T(8,128)(2,1)} %param.17) | copy-start | bytes 3932164
  1.3 52.3 %copy-start.2 = (bf16[1,512,1280]{2,1,0:T(8,128)(2,1)S(1)}, bf16[1,512,1280]{2,1,0:T(8,128)(2,1)}, u32[]{:S(2)}) copy-start(bf16[1,512,1280]{2,1,0:T(8,128)(2,1)} %param.18) | copy-start | bytes 3932164
  1.3 52.3 %copy-start.6 = (bf16[320,1280]{1,0:T(8,128)(2,1)S(1)}, bf16[320,1280]{1,0:T(8,128)(2,1)}, u32[]{:S(2)}) copy-start(bf16[320,1280]{1,0:T(8,128)(2,1)} %proj_w.1) | copy-start | bytes 2457604
  53.7 0.9 copy-start.9
  54.6 1.0 copy-start.10
  55.5 73.7 %copy-start.4 = (bf16[4,2,2,80,512]{4,3,2,1,0:T(8,128)(2,1)S(1)}, bf16[4,2,2,80,512]{4,3,2,1,0:T(8,128)(2,1)}, u32[]{:S(2)}) copy-start(bf16[4,2,2,80,512]{4,3,2,1,0:T(8,128)(2,1)} %get-tuple-element.79.rkv) | copy-start | bytes 3932164
  55.5 73.7 %copy-start.5 = (bf16[240,2048]{1,0:T(8,128)(2,1)S(1)}, bf16[240,2048]{1,0:T(8,128)(2,1)}, u32[]{:S(2)}) copy-start(bf16[240,2048]{1,0:T(8,128)(2,1)} %get-tuple-element.77.qaug_in) | copy-start | bytes 2949124
  55.5 73.7 %copy-start.7 = (f32[80,2048]{1,0:T(8,128)S(1)}, f32[80,2048]{1,0:T(8,128)}, u32[]{:S(2)}) copy-start(f32[80,2048]{1,0:T(8,128)} %get-tuple-element.80.o_in) | copy-start | bytes 1966084
  55.5 73.7 %copy-start.8 = (bf16[8,16,2048]{2,1,0:T(8,128)(2,1)S(1)}, bf16[8,16,2048]{2,1,0:T(8,128)(2,1)}, u32[]{:S(2)}) copy-start(bf16[8,16,2048]{2,1,0:T(8,128)(2,1)} %get-tuple-element.78.bias_rows) | copy-start | bytes 1572868
  55.6 73.7 %copy-start.11 = (bf16[2,128,80]{2,1,0:T(8,128)(2,1)S(1)}, bf16[2,128,80]{2,1,0:T(8,128)(2,1)}, u32[]{:S(2)}) copy-start(bf16[2,128,80]{2,1,0:T(8,128)(2,1)} %get-tuple-element.76.tables) | copy-start | bytes 122884
  55.6 73.7 %copy-start.12 = (f32[1,2048]{1,0:T(1,128)S(1)}, f32[1,2048]{1,0:T(1,128)}, u32[]{:S(2)}) copy-start(f32[1,2048]{1,0:T(1,128)} %get-tuple-element.81.lse_in) | copy-start | bytes 24580
  129.3 65.7 %copy-start.1 = (bf16[1280,3,320]{0,2,1:T(8,128)(2,1)S(1)}, bf16[1280,3,320]{0,2,1:T(8,128)(2,1)}, u32[]{:S(2)}) copy-start(bf16[1280,3,320]{0,2,1:T(8,128)(2,1)} %param.21) | copy-start | bytes 7372804
  129.3 65.7 %copy-start.3 = (bf16[1280,512]{1,0:T(8,128)(2,1)S(1)}, bf16[1280,512]{1,0:T(8,128)(2,1)}, u32[]{:S(2)}) copy-start(bf16[1280,512]{1,0:T(8,128)(2,1)} %get-tuple-element.87) | copy-start | bytes 3932164
  129.3 65.7 %copy-start.13 = (f32[8,128]{1,0:T(8,128)S(1)}, f32[8,128]{1,0:T(8,128)}, u32[]{:S(2)}) copy-start(f32[8,128]{1,0:T(8,128)} %get-tuple-element.92.peak) | copy-start | bytes 12292

commit v5 on v4

--- a/solution.py
+++ b/solution.py
@@ -193,7 +193,12 @@
         send_dp(
             rkv.at[z, g], rkv.at[z, g], x_send.at[z, n], x_recv.at[z, g], z * group + mate
         ).start()
-    n1_out[...] = n1[...].T
+    n1_t = n1[...].T
+    pieces, devices, piece, _ = n1_out.shape
+    for dev in range(devices):
+        for at in range(pieces):
+            start = (dev * pieces + at) * piece
+            n1_out[at, dev] = n1_t[start : start + piece]
     wide_t[...] = jnp.zeros_like(wide_t)
     for n, held in enumerate((rows_t, cols_t)):
         wide_t[n, :HEAD, : held.shape[1]] = held[...]
@@ -322,6 +327,9 @@
     heads, group, rows, queries = shape.heads, shape.group, shape.rows, shape.queries
     width, local = tokens.shape[1], heads * HEAD
     args = (tokens, weights, *listed, rows_t, cols_t)
+    devices = heads * group
+    owned = width // devices
+    piece = 32 if owned % 32 == 0 else owned
     vmem = pl.BlockSpec(memory_space=pltpu.VMEM)
     hbm = pl.BlockSpec(memory_space=pl.ANY)
     dma = pltpu.SemaphoreType.DMA
@@ -335,7 +343,7 @@
             jax.ShapeDtypeStruct((HEAD, queries), F32),
             jax.ShapeDtypeStruct((1, queries), F32),
             jax.ShapeDtypeStruct((8, 128), F32),
-            jax.ShapeDtypeStruct((width, rows), LOW),
+            jax.ShapeDtypeStruct((owned // piece, devices, piece, rows), LOW),
             jax.ShapeDtypeStruct((2, 2 * SIDE, HEAD), LOW),
             jax.ShapeDtypeStruct((16, width), F32),
         ),
@@ -369,8 +377,8 @@
 
 
 def backward_kernel(
-    shape, ga, tables, qaug_in, bias_rows, rkv, o_in, lse_in, fc2_state, fc2_more, fc1, proj,
-    grads, table_grads, fc1_out, fc2_out, fc1_state, proj_state,
+    shape, ga, tables, qaug_in, bias_rows, rkv, o_in, lse_in, fc2_state, fc1, mlp, values, vectors, proj,
+    grads, table_grads, fc1_out, fc2_out, fc1_state, output, proj_state,
     rdo, qaug, q_tok, do_aug, do_tok, kaug_t, kaug, vaug_t, vaug, kacc, vacc, dq, drow, dcol,
     part, xr, summed, gq_s, gq_r, gkv_r,
     d_send, d_recv, x_send, x_recv, kv_send, kv_recv, q_send, q_recv, *rest,
@@ -384,10 +392,16 @@
 
     whole_bufs = 2 + 3 * halve_bits()
     bits = halve_bits()
-    moved2 = [Halve(near_first(), fc2_state, taken(3 * (bits - 2)), first=2)]
-    if chunks > 1:
-        moved2 += [Halve(near_first(), fc2_more, taken(3 * (bits - 1)), first=1)]
-    moved0 = Halve(near_first(), proj, taken(3), last=0)
+    orders = [near_first(), far_first(shape.group)]
+    moved2 = [
+        Halve(orders[n], fc2_state.at[n], taken(3 * (bits - 2)), first=2) for n in range(chunks)
+    ]
+    moved0 = Halve(far_first(shape.group), proj, taken(3), last=0)
+    outs = taken(1)[0]
+    lines = lax.axis_size("tensor") // 2
+    sum_mlp = Reduce(mlp, *taken(7))
+    all_out = Gather(outs, *taken(3))
+    line = tensor_place()[1]
     moved1 = [Halve(near_first(), fc1.at[:, 0], taken(whole_bufs), own=True)]
     if chunks > 1:
         moved1 += [Halve(near_first(), fc1.at[:, 1], taken(5), last=0, own=True)]
@@ -397,7 +411,9 @@
     z, g = me // group, lax.rem(me, group)
     column = [paired(z, k, heads) for k in range(1, heads)]
     mates = [lax.rem(g + k, group) for k in range(1, group)]
-    greet([h * group + g for h in column] + [z * group + o for o in mates])
+    greet_all(Ring(heads))
+    for other in sum_mlp.others() + [line]:
+        sum_mlp.give(other)
     sends = []
     for h in column:
         copy = send_dp(ga.at[h], rdo.at[z], d_send.at[h], d_recv.at[z], h * group + g)
@@ -443,6 +459,9 @@
         return carry
 
     lax.fori_loop(0, heads, prepare, 0)
+    for other in sum_mlp.others():
+        sum_mlp.pass_on(other)
+    moved0.start()
 
     def chunk(source, mate):
         dev = source * group + mate
@@ -506,10 +525,11 @@
         return carry
 
     lax.fori_loop(1, heads + 1, mates_step, 0)
-    moved0.start()
     if chunks > 1:
         moved1[1].start()
-        moved2[1].run(1)
+    spot = lax.axis_index("tensor")
+    outs[spot] = (values[...] + sum_mlp.total() + vectors[3:4]).astype(LOW)
+    all_out.start()
     moved1[0].loaded()
     moved1[0].run(0)
 
@@ -533,6 +553,8 @@
         return carry
 
     lax.fori_loop(1, heads + 1, own_step, 0)
+    for other in all_out.others():
+        all_out.forward(other)
     table_grads[...] = jnp.zeros_like(table_grads)
 
     def finish(k, carry):
@@ -570,6 +592,9 @@
         fc1_state[...] = moved1[1].stages[0][0][...]
     moved0.run(0)
     proj_state[...] = moved0.stages[0][0][...]
+    for other in all_out.others() + [line]:
+        all_out.take(other)
+    output[...] = outs[...]
     grads[z, 0] = gq_s[z]
     grads[z, pl.ds(1, 2)] = summed[z]
     for h in column:
@@ -583,18 +608,18 @@
     for source in range(heads):
         for mate in mates:
             mate_copy(source, mate).wait_send()
-    for each in moved1 + moved2 + [moved0]:
+    for each in moved1 + moved2 + [sum_mlp, all_out, moved0]:
         each.finish()
 
 
-def attend_back(shape, ga, tables, qaug, bias_rows, kv, o_rows, lse, fc2_state, fc2_more, fc1, proj):
-    local = proj.shape[2]
+def attend_back(shape, ga, tables, qaug, bias_rows, kv, o_rows, lse, fc2_state, fc1, mlp, values, vectors, proj):
+    count, share, width = mlp.shape
     devices, chunks, owned, hidden = fc1.shape
     hbm = pl.BlockSpec(memory_space=pl.ANY)
-    moving = halve_bufs(owned, hidden, first=2)
-    if chunks > 1:
-        moving += halve_bufs(owned, hidden, first=1)
-    moving += halve_bufs(chunks * owned, local, last=0)
+    moving = halve_bufs(owned, hidden, first=2) * chunks
+    moving += halve_bufs(chunks * owned, proj.shape[2], last=0)
+    moving += [pltpu.VMEM((count, share, width), LOW)]
+    moving += part_bufs(count // 2, share, width) + gather_sems(count // 2)
     moving += halve_bufs(owned, hidden, own=True)
     if chunks > 1:
         moving += halve_bufs(owned, hidden, last=0, own=True)
@@ -609,10 +634,11 @@
             jax.ShapeDtypeStruct((owned, hidden), F32),
             jax.ShapeDtypeStruct((chunks * owned, hidden), F32),
             jax.ShapeDtypeStruct((devices // 2, owned, hidden), LOW),
-            jax.ShapeDtypeStruct((devices // 2, chunks * owned, local), LOW),
+            jax.ShapeDtypeStruct((count, share, width), LOW),
+            jax.ShapeDtypeStruct((devices // 2,) + proj.shape[1:], LOW),
         ),
-        in_specs=[vmem] * 9 + [hbm, vmem],
-        out_specs=(vmem,) * 6,
+        in_specs=[vmem] * 8 + [hbm] + [vmem] * 4,
+        out_specs=(vmem,) * 7,
         scratch_shapes=[
             pltpu.VMEM((heads, HEAD, rows), LOW),
             pltpu.VMEM((AUG, queries), LOW),
@@ -641,7 +667,7 @@
             collective_id=2, has_side_effects=True, vmem_limit_bytes=VMEM_LIMIT["attend_back"]
         ),
         name="attend_back",
-    )(ga, tables, qaug, bias_rows, kv, o_rows, lse, fc2_state, fc2_more, fc1, proj)
+    )(ga, tables, qaug, bias_rows, kv, o_rows, lse, fc2_state, fc1, mlp, values, vectors, proj)
 
 
 def send_tensor(src, dst, send_sem, recv_sem, dev):
@@ -923,8 +949,8 @@
 
 def middle_kernel(
     heads, att, proj_w, tokens, cot, fc1_hbm, fc2_hbm, vectors,
-    output, middle_out, fc1_out, proj_out, ga_out, fc1_bias_out, sums_out, fc2_state, fc2_more,
-    fc1, fc2, att_tok, branch, mlp, back, n2, act, gu, gb, outs, held, spread,
+    mlp, values_out, middle_out, fc1_out, proj_out, ga_out, fc1_bias_out, sums_out, fc2_state,
+    fc1, fc2, att_tok, branch, back, n2, act, gu, gb, held, spread,
     wide, load1, load2, *rest,
 ):
     core, line, lines = tensor_place()
@@ -939,18 +965,16 @@
     in_fc2.start()
     greet_all(Ring(heads))
     sum_branch = Reduce(branch, *rest[0:7])
-    sum_mlp = Reduce(mlp, *rest[7:14])
-    sum_back = Reduce(back, *rest[14:21])
-    all_n2 = Gather(n2, *rest[21:24])
-    all_gb = Gather(gb, *rest[24:27])
-    all_out = Gather(outs, *rest[27:30])
-    blocks2, blocks1, fc1_sem = rest[30:33]
+    sum_back = Reduce(back, *rest[7:14])
+    all_n2 = Gather(n2, *rest[14:17])
+    all_gb = Gather(gb, *rest[17:20])
+    blocks2, blocks1, fc1_sem = rest[20:23]
     devices, chunks, owned, _ = blocks2.shape
+    orders = [near_first(), far_first(lax.axis_size("dp") // heads)]
     moved = [
-        Halve(near_first(), blocks2.at[:, n], rest[36 + 3 * n : 39 + 3 * n], last=0)
-        for n in range(1, chunks)
+        Halve(orders[n], blocks2.at[:, n], rest[23 + 6 * n : 29 + 6 * n], last=1)
+        for n in range(chunks)
     ]
-    moved = [Halve(near_first(), blocks2.at[:, 0], rest[33:39], last=1)] + moved
     att_tok[...] = att[...].T.reshape(att_tok.shape)
 
     def project(k, carry):
@@ -972,8 +996,8 @@
     scaled, inverse = normed(middle)
     n2[me] = (scaled * vectors[1:2] + vectors[2:3]).astype(LOW)
     all_n2.start()
-    held[0] = middle
-    held[1] = scaled
+    values_out[...] = middle
+    held[...] = scaled
     spread[...] = jnp.broadcast_to(inverse, spread.shape)
     fc1_bias_out[...] = jnp.zeros_like(fc1_bias_out)
     in_fc1.wait()
@@ -1044,7 +1068,6 @@
             return inner
 
         lax.fori_loop(0, width // dstep, tile_out, 0)
-        sum_mlp.give(at)
         return carry
 
     lax.fori_loop(0, lines, out_part, 0)
@@ -1063,19 +1086,16 @@
     keep_fc1 = pltpu.make_async_copy(blocks1, fc1_out, fc1_sem)
     keep_fc1.start()
     upstream = sum_back.total()
-    sums_out[0:1] = jnp.sum(upstream * held[1], axis=0, keepdims=True)
+    sums_out[0:1] = jnp.sum(upstream * held[...], axis=0, keepdims=True)
     sums_out[1:2] = jnp.sum(upstream, axis=0, keepdims=True)
     grad_middle = cot[me].astype(F32) + normed_back(
-        upstream, held[1], spread[:, :1], vectors[1:2]
+        upstream, held[...], spread[:, :1], vectors[1:2]
     )
     middle_out[...] = grad_middle
     gb[me] = grad_middle.astype(LOW)
     all_gb.start()
-    for other in sum_mlp.others():
-        sum_mlp.pass_on(other)
-    outs[me] = (held[0] + sum_mlp.total() + vectors[3:4]).astype(LOW)
-    all_out.start()
-
+    for each in moved:
+        each.run(0)
     sums_out[2:3] = jnp.sum(cot[...].astype(F32).reshape(rows, width), axis=0, keepdims=True)
     for other in all_gb.others():
         all_gb.forward(other)
@@ -1095,20 +1115,11 @@
     lax.fori_loop(0, width // dstep, weights0, 0)
     for dev in range(devices):
         proj_out[dev] = wide[pl.ds(dev * chunks * owned, chunks * owned), :local]
-    moved[0].run(0)
-    for other in all_out.others():
-        all_out.forward(other)
-    all_out.take(line)
-    for other in all_out.others():
-        all_out.take(other)
-    output[...] = outs[...]
-    moved[0].run(1)
-    fc2_state[...] = moved[0].stages[1][0][...]
-    for n, each in enumerate(moved[1:]):
-        each.run(0)
-        fc2_more[...] = each.stages[0][0][...]
+    for n, each in enumerate(moved):
+        each.run(1)
+        fc2_state[n] = each.stages[1][0][...]
     keep_fc1.wait()
-    for each in (sum_branch, sum_mlp, sum_back, all_n2, all_gb, all_out, *moved):
+    for each in (sum_branch, sum_back, all_n2, all_gb, *moved):
         each.finish()
 
 
@@ -1134,36 +1145,33 @@
         pltpu.VMEM(whole, LOW),
         pltpu.VMEM(whole, LOW),
         pltpu.VMEM(whole, LOW),
-        pltpu.VMEM(whole, LOW),
         pltpu.VMEM((count, share, hidden), LOW),
         pltpu.VMEM((count, share, hidden), LOW),
         pltpu.VMEM(whole, LOW),
-        pltpu.VMEM(whole, LOW),
-        pltpu.VMEM((2, share, width), F32),
+        pltpu.VMEM((share, width), F32),
         pltpu.VMEM((share, 128), F32),
         pltpu.VMEM((width, hidden), LOW),
         dma,
         dma,
     ]
-    scratch += part_bufs(lines, share, width) * 3 + gather_sems(lines) * 3
+    scratch += part_bufs(lines, share, width) * 2 + gather_sems(lines) * 2
     scratch += [pltpu.VMEM(weights, LOW), pltpu.VMEM(weights, LOW), dma]
-    scratch += halve_bufs(owned // chunks, hidden, last=1)
-    scratch += halve_bufs(owned // chunks, hidden, last=0) * (chunks - 1)
+    scratch += halve_bufs(owned // chunks, hidden, last=1) * chunks
     return pl.pallas_call(
         functools.partial(middle_kernel, heads),
         out_shape=(
             jax.ShapeDtypeStruct(whole, LOW),
+            jax.ShapeDtypeStruct((share, width), F32),
             jax.ShapeDtypeStruct((share, width), F32),
             jax.ShapeDtypeStruct(weights, LOW),
             jax.ShapeDtypeStruct((devices, owned, local), LOW),
             jax.ShapeDtypeStruct((local, rows), LOW),
             jax.ShapeDtypeStruct((1, hidden), F32),
             jax.ShapeDtypeStruct((8, width), F32),
-            jax.ShapeDtypeStruct((devices // 4, owned // chunks, hidden), LOW),
-            jax.ShapeDtypeStruct((devices // 2, owned // chunks, hidden), LOW),
+            jax.ShapeDtypeStruct((chunks, devices // 4, owned // chunks, hidden), LOW),
         ),
         in_specs=[vmem] * 4 + [hbm] * 2 + [vmem],
-        out_specs=(vmem,) * 2 + (hbm,) + (vmem,) * 6,
+        out_specs=(vmem,) * 3 + (hbm,) + (vmem,) * 5,
         scratch_shapes=scratch,
         compiler_params=pltpu.CompilerParams(
             collective_id=3, has_side_effects=True, vmem_limit_bytes=VMEM_LIMIT["middle"]
@@ -1227,7 +1235,7 @@
                 self.copy(n, own, other, dev).wait_send()
 
 
-EVERY = ("core", "line", "mate", "far")
+EVERY = ("core", "line", "far", "mate")
 OVER_DP = ("mate", "far")
 
 
@@ -1244,7 +1252,7 @@
 
 def tail_kernel(
     heads, grads, qkv_w, n1_t, tokens, grad_middle, vectors, tables, sums, fc1_bias, peak,
-    proj_state, fc1_half, fc1_state,
+    proj, fc1_half, fc1_state,
     tokens_out, proj_out, fc1_out, qkv_out, tables_out, rows_out, clip_out,
     g_all, g_tok, part, gt, *rest,
 ):
@@ -1255,7 +1263,8 @@
     rows = count * share
     local = heads * HEAD
     dstep = tile_of(width)
-    devices, chunks, _, _ = n1_t.shape
+    pieces, devices, piece, _ = n1_t.shape
+    chunks = 1 if pieces == 1 else 2
     rest = list(rest)
 
     def taken(number):
@@ -1263,10 +1272,9 @@
         return found
 
     greet_all(ring)
-    blocks = [taken(1)[0] for _ in range(chunks)]
-    orders = [near_first(), far_first(ring.group)]
-    moved3 = [Halve(orders[n], blocks[n], taken(3 * halve_bits())) for n in range(chunks)]
-    moved0 = Halve(near_first(), proj_state, taken(3 * (halve_bits() - 1)), first=1)
+    blocks = [taken(1)[0] for _ in range(pieces)]
+    moved3 = [Halve(near_first(), each, taken(3 * halve_bits())) for each in blocks]
+    moved0 = Halve(far_first(ring.group), proj, taken(3 * (halve_bits() - 1)), first=1)
     moved1 = []
     if chunks > 1:
         moved1 = [Halve(near_first(), fc1_state, taken(3 * (halve_bits() - 1)), first=1)]
@@ -1293,23 +1301,17 @@
     whole = g_tok[...].reshape(rows, 3 * local)
     lane = lax.broadcasted_iota(jnp.int32, (1, width), 1)
     peaks = jnp.where(lane == ring.z, peak[0:1, 0:1], -jnp.inf)
-    bias_sums = jnp.sum(whole.astype(F32), axis=0, keepdims=True)
+    bias_sums = nn(jnp.ones((8, rows), LOW), whole)[0:1]
     dp_rows = [widen(fc1_bias[...], width), widen(bias_sums, width), peaks]
     small_dp.start(0, jnp.concatenate(dp_rows + [jnp.zeros((5, width), F32)], axis=0))
 
-    for n in range(chunks):
-
-        def weight_part(dev, carry):
-            found = nn(n1_t[dev, n], g_tok[...].reshape(rows, 3 * local))
-            blocks[n][dev] = found.astype(LOW)
-            return carry
-
-        lax.fori_loop(0, devices, weight_part, 0)
-        if n == 0:
+    for n in range(pieces):
+        found = nn(
+            n1_t[n].reshape(devices * piece, rows), g_tok[...].reshape(rows, 3 * local)
+        )
+        blocks[n][...] = found.astype(LOW).reshape(devices, piece, 3 * local)
+        if n == min(1, pieces - 1):
             small_pool.start(0, sum_pool.total())
-        if n == chunks - 1:
-            small_pool.step(0)
-            small_dp.step(0)
         moved3[n].start()
 
     def norm_part(k, carry):
@@ -1330,9 +1332,14 @@
     for other in sum_part.others():
         sum_part.pass_on(other)
     scaled, inverse = normed(tokens[me].astype(F32))
+    small_pool.step(0)
     moved0.run(1)
     for each in moved1:
         each.run(1)
+    moved3[0].run(0)
+    for each in moved3[1:2]:
+        each.run(0)
+    moved3[0].run(1)
     upstream = sum_part.total()
     late = [
         sums[0:4],
@@ -1346,15 +1353,26 @@
     all_gt.start()
     pooled[me] = small_pool.take(1)
     all_pool.start()
-    moved3[0].run(0)
-    small_late.step(0)
-    for each in moved3[1:]:
+    small_dp.step(0)
+    for n, each in enumerate(moved3[2:]):
         each.run(0)
-    small_late.step(1)
-    for other in all_gt.others():
-        all_gt.forward(other)
-    for other in all_pool.others():
-        all_pool.forward(other)
+        if n == 0:
+            small_late.step(0)
+        if n == 1:
+            small_late.step(1)
+            for other in all_gt.others():
+                all_gt.forward(other)
+            for other in all_pool.others():
+                all_pool.forward(other)
+        moved3[n + 1].run(1)
+    if pieces < 4:
+        for n in range(max(pieces - 2, 0), 2):
+            small_late.step(n)
+        for other in all_gt.others():
+            all_gt.forward(other)
+        for other in all_pool.others():
+            all_pool.forward(other)
+    small_late.step(2)
     dp_sum = small_dp.take(1)
     limit = vectors[9:10]
     factors = jnp.sqrt(limit / jnp.maximum(dp_sum[2:3], limit))
@@ -1371,10 +1389,8 @@
     rows_out[11:12] = factors
     rows_out[12:13] = clipped_bias
     rows_out[13:16] = jnp.zeros((3, width), F32)
-    moved3[0].run(1)
-    small_late.step(2)
-    for each in moved3[1:]:
-        each.run(1)
+    if pieces > 1:
+        moved3[-1].run(1)
     for stage in range(2, halve_bits() - 1):
         for each in moved3 + [moved0] + moved1:
             each.run(stage)
@@ -1405,17 +1421,18 @@
     for each in [
         moved0, sum_part, all_gt, sum_pool, all_pool, small_pool, small_late, small_dp,
     ] + moved3 + moved1:
-
         each.finish()
 
 
-def tail(heads, grads, qkv_w, n1_t, tokens, grad_middle, vectors, tables, sums, fc1_bias, peak, proj_state, fc1_half, fc1_state):
+def tail(heads, grads, qkv_w, n1_t, tokens, grad_middle, vectors, tables, sums, fc1_bias, peak, proj, fc1_half, fc1_state):
     hidden = fc1_half.shape[1]
     count = lax.axis_size("tensor")
     lines = count // 2
     local = heads * HEAD
-    devices, chunks, owned, rows = n1_t.shape
-    width = devices * chunks * owned
+    pieces, devices, piece, rows = n1_t.shape
+    width = devices * pieces * piece
+    owned = fc1_half.shape[0]
+    chunks = pieces * piece // owned
     share = rows // count
     vmem = pl.BlockSpec(memory_space=pltpu.VMEM)
     whole = (count, share, width)
@@ -1425,8 +1442,8 @@
         pltpu.VMEM(whole, LOW),
         pltpu.VMEM(whole, LOW),
     ]
-    scratch += [pltpu.VMEM((devices, owned, 3 * local), LOW)] * chunks
-    scratch += halve_bufs(owned, 3 * local) * chunks
+    scratch += [pltpu.VMEM((devices, piece, 3 * local), LOW)] * pieces
+    scratch += halve_bufs(piece, 3 * local) * pieces
     scratch += halve_bufs(chunks * owned, local, first=1)
     if chunks > 1:
         scratch += halve_bufs(owned, hidden, first=1)
@@ -1457,7 +1474,7 @@
         name="tail",
     )(
         grads, qkv_w, n1_t, tokens.reshape(whole), grad_middle, vectors, tables, sums, fc1_bias,
-        peak, proj_state, fc1_half, fc1_state,
+        peak, proj, fc1_half, fc1_state,
     )
 
 
@@ -1546,7 +1563,8 @@
         shape, flat, weights, listed, table_rows.T, table_cols.T
     )
     (
-        output,
+        mlp_part,
+        values,
         grad_middle,
         grad_fc1,
         grad_proj,
@@ -1554,7 +1572,6 @@
         grad_fc1_bias,
         sums,
         fc2_state,
-        fc2_more,
     ) = middle_block(
         local_heads,
         attended.reshape(local_width, token_count),
@@ -1566,16 +1583,15 @@
         vectors,
     )
     grad_heads = grad_attended.reshape(local_heads, HEAD, row_count)
-    devices, chunks, owned, _ = grad_fc1.shape
-    grad_triple, table_terms, fc1_half, grad_fc2, fc1_state, proj_state = attend_back(
-        shape, grad_heads, tables, qaug, bias_rows, kv, o_rows, lse, fc2_state, fc2_more, grad_fc1,
-        grad_proj,
+    grad_triple, table_terms, fc1_half, grad_fc2, fc1_state, output, proj_state = attend_back(
+        shape, grad_heads, tables, qaug, bias_rows, kv, o_rows, lse, fc2_state, grad_fc1,
+        mlp_part, values, vectors, grad_proj,
     )
     grad_tokens, grad_proj, grad_fc1, grad_qkv, table_sums, rows, clipped = tail(
         local_heads,
         grad_triple,
         weights,
-        normed1.reshape(devices, chunks, owned, token_count),
+        normed1,
         flat,
         grad_middle,
         vectors,

time: 268 us -> 243 us (0.907)
  Pallas kernels: 262 us -> 240 us
    pallas_call x1, Pallas kernels: 73.6 us -> 62.9 us  [middle_block(): pl.pallas_call(functools.partial(middle_kernel, heads), out_shape=(jax.Sh...]
    pallas_call x1, Pallas kernels: 65.4 us -> 55.5 us  [tail(): pl.pallas_call(functools.partial(tail_kernel, heads), out_shape=(jax.Shap...]
where the time goes in v5:
time: 243 us
  Pallas kernels  240 us (99%)
    pallas_call x1, Pallas kernels, attend_back(): pl.pallas_call(functools.partial(backward_kernel, shape), out_shape=(jax....  64 us
    pallas_call x1, Pallas kernels, middle_block(): pl.pallas_call(functools.partial(middle_kernel, heads), out_shape=(jax.Sh...  62.9 us
    pallas_call x1, Pallas kernels, tail(): pl.pallas_call(functools.partial(tail_kernel, heads), out_shape=(jax.Shap...  55.5 us
    pallas_call x1, Pallas kernels, attend(): pl.pallas_call(functools.partial(forward_kernel, shape, len(args), 10), o...  52.3 us
    pallas_call x1, Pallas kernels, finish(): pl.pallas_call(functools.partial(finish_kernel, count), out_shape=[jax.Sh...  4.97 us

profile of v5, /device:TPU:0, one launch (start us, length us, event | category | flops | bytes accessed | tf_op | source)
XLA Modules:
  0.0 243.3 jit_solution(4755740026181343622)
XLA Ops:
  1.3 0.0 copy-start
  1.3 0.0 copy-start.2
  1.3 0.0 copy-start.6
  1.3 52.3 %attend.1 = (bf16[4,80,512]{2,1,0:T(8,128)(2,1)}, bf16[240,2048]{1,0:T(8,128)(2,1)}, bf16[8,16,2048]{2,1,0:T(8,128)(2,1)}, bf16[4,2,2,80,512]{4,3,2,1,0:T(8,128)...) custom-call(bf16[512,1280]{1,0:T(8,128)(2,1)} %bitcast.20, ...), custom_call_target="tpu_custom_call" | custom-call | tf_op jit(solution)/shard_map/attend/pallas_call | solution.py:336
  53.6 0.0 copy-done
  53.7 0.0 copy-done.2
  53.7 0.0 copy-done.6
  53.7 0.0 copy-start.7
  53.7 0.9 copy-done.7
  54.6 1.0 copy-done.10
  55.6 0.0 copy-start.11
  55.6 0.0 copy-start.12
  55.6 62.9 %middle.1 = (bf16[4,128,1280]{2,1,0:T(8,128)(2,1)S(1)}, f32[128,1280]{1,0:T(8,128)S(1)}, f32[128,1280]{1,0:T(8,128)S(1)}, bf16[8,2,80,1280]{3,2,1,0:T(8,128)(2,1...) custom-call(bf16[320,512]{1,0:T(8,128)(2,1)S(1)} %bitcast.27, ...), custom_call_target="tpu_custom_call" | custom-call | tf_op jit(solution)/shard_map/middle/pallas_call | solution.py:1160
  118.5 0.0 copy-done.4
  118.5 0.0 copy-done.5
  118.5 0.0 copy-done.8
  118.5 0.0 copy-done.9
  118.5 0.0 copy-start.1
  118.6 64.0 %attend_back.1 = (bf16[4,3,80,512]{3,2,1,0:T(8,128)(2,1)S(1)}, f32[2,128,128]{2,1,0:T(8,128)S(1)}, f32[80,1280]{1,0:T(8,128)S(1)}, f32[160,1280]{1,0:T(8,128)S(1...) custom-call(bf16[4,80,512]{2,1,0:T(8,128)(2,1)S(1)} %bitcast.26, ...), custom_call_target="tpu_custom_call" | custom-call | tf_op jit(solution)/shard_map/attend_back/pallas_call | solution.py:629
  182.5 0.0 copy-done.1
  182.5 0.0 copy-done.3
  182.6 0.0 copy-done.13
  182.6 55.5 %tail.1 = (bf16[4,128,1280]{2,1,0:T(8,128)(2,1)S(1)}, f32[160,320]{1,0:T(8,128)S(1)}, f32[160,1280]{1,0:T(8,128)S(1)}, f32[3,160,320]{2,1,0:T(8,128)S(1)}, f32[2...) custom-call(bf16[4,3,80,512]{3,2,1,0:T(8,128)(2,1)S(1)} %get-tuple-element.88.grads, ...), custom_call_target="tpu_custom_call" | custom-call | tf_op jit(solution)/shard_map/tail/pallas_call | solution.py:1457
  238.1 5.0 %finish.1 = (bf16[4,128,1280]{2,1,0:T(8,128)(2,1)}, bf16[4,128,1280]{2,1,0:T(8,128)(2,1)}, f32[160,1280]{1,0:T(8,128)}, f32[160,1280]{1,0:T(8,128)}, f32[3,160,3...) custom-call(bf16[4,128,1280]{2,1,0:T(8,128)(2,1)S(1)} %get-tuple-ele, ...), custom_call_target="tpu_custom_call" | custom-call | tf_op jit(solution)/shard_map/finish/pallas_call | solution.py:1518
  (9 shorter events, 0.0 us)
Async XLA Ops:
  1.3 52.3 %copy-start = (bf16[1,512,1280]{2,1,0:T(8,128)(2,1)S(1)}, bf16[1,512,1280]{2,1,0:T(8,128)(2,1)}, u32[]{:S(2)}) copy-start(bf16[1,512,1280]{2,1,0:T(8,128)(2,1)} %param.17) | copy-start | bytes 3932164
  1.3 52.3 %copy-start.2 = (bf16[1,512,1280]{2,1,0:T(8,128)(2,1)S(1)}, bf16[1,512,1280]{2,1,0:T(8,128)(2,1)}, u32[]{:S(2)}) copy-start(bf16[1,512,1280]{2,1,0:T(8,128)(2,1)} %param.18) | copy-start | bytes 3932164
  1.3 52.3 %copy-start.6 = (bf16[320,1280]{1,0:T(8,128)(2,1)S(1)}, bf16[320,1280]{1,0:T(8,128)(2,1)}, u32[]{:S(2)}) copy-start(bf16[320,1280]{1,0:T(8,128)(2,1)} %proj_w.1) | copy-start | bytes 2457604
  53.7 0.9 copy-start.7
  54.6 1.0 copy-start.10
  55.5 62.9 %copy-start.4 = (bf16[4,2,2,80,512]{4,3,2,1,0:T(8,128)(2,1)S(1)}, bf16[4,2,2,80,512]{4,3,2,1,0:T(8,128)(2,1)}, u32[]{:S(2)}) copy-start(bf16[4,2,2,80,512]{4,3,2,1,0:T(8,128)(2,1)} %get-tuple-element.79.rkv) | copy-start | bytes 3932164
  55.5 62.9 %copy-start.5 = (bf16[240,2048]{1,0:T(8,128)(2,1)S(1)}, bf16[240,2048]{1,0:T(8,128)(2,1)}, u32[]{:S(2)}) copy-start(bf16[240,2048]{1,0:T(8,128)(2,1)} %get-tuple-element.77.qaug_in) | copy-start | bytes 2949124
  55.5 63.0 %copy-start.8 = (f32[80,2048]{1,0:T(8,128)S(1)}, f32[80,2048]{1,0:T(8,128)}, u32[]{:S(2)}) copy-start(f32[80,2048]{1,0:T(8,128)} %get-tuple-element.80.o_in) | copy-start | bytes 1966084
  55.5 63.0 %copy-start.9 = (bf16[8,16,2048]{2,1,0:T(8,128)(2,1)S(1)}, bf16[8,16,2048]{2,1,0:T(8,128)(2,1)}, u32[]{:S(2)}) copy-start(bf16[8,16,2048]{2,1,0:T(8,128)(2,1)} %get-tuple-element.78.bias_rows) | copy-start | bytes 1572868
  55.6 63.0 %copy-start.11 = (bf16[2,128,80]{2,1,0:T(8,128)(2,1)S(1)}, bf16[2,128,80]{2,1,0:T(8,128)(2,1)}, u32[]{:S(2)}) copy-start(bf16[2,128,80]{2,1,0:T(8,128)(2,1)} %get-tuple-element.76.tables) | copy-start | bytes 122884
  55.6 63.0 %copy-start.12 = (f32[1,2048]{1,0:T(1,128)S(1)}, f32[1,2048]{1,0:T(1,128)}, u32[]{:S(2)}) copy-start(f32[1,2048]{1,0:T(1,128)} %get-tuple-element.81.lse_in) | copy-start | bytes 24580
  118.5 64.0 %copy-start.1 = (bf16[1280,3,320]{0,2,1:T(8,128)(2,1)S(1)}, bf16[1280,3,320]{0,2,1:T(8,128)(2,1)}, u32[]{:S(2)}) copy-start(bf16[1280,3,320]{0,2,1:T(8,128)(2,1)} %param.21) | copy-start | bytes 7372804
  118.5 64.0 %copy-start.3 = (bf16[5,8,32,512]{3,2,1,0:T(8,128)(2,1)S(1)}, bf16[5,8,32,512]{3,2,1,0:T(8,128)(2,1)}, u32[]{:S(2)}) copy-start(bf16[5,8,32,512]{3,2,1,0:T(8,128)(2,1)} %get-tuple-element.89.n1_t) | copy-start | bytes 3932164
  118.6 64.0 %copy-start.13 = (f32[8,128]{1,0:T(8,128)S(1)}, f32[8,128]{1,0:T(8,128)}, u32[]{:S(2)}) copy-start(f32[8,128]{1,0:T(8,128)} %get-tuple-element.94.peak) | copy-start | bytes 12292

commit v6 on v5

--- a/solution.py
+++ b/solution.py
@@ -24,7 +24,7 @@
 VMEM_LIMIT = {
     "attend": 60 * 2**20,
     "middle": 40 * 2**20,
-    "attend_back": 24 * 2**20,
+    "attend_back": 32 * 2**20,
     "tail": 24 * 2**20,
     "finish": 12 * 2**20,
 }
@@ -119,24 +119,31 @@
     def __init__(self, heads, group, rows):
         self.heads, self.group, self.rows = heads, group, rows
         self.queries = heads * rows
-        self.block = min(1024, self.queries)
+        self.block = min(2048, self.queries)
 
 
 def forward_kernel(shape, count, outs, *refs):
-    held = refs[count + outs : 2 * count + outs]
-    load = refs[2 * count + outs]
+    results = refs[count : count + outs]
+    held, refs_left = refs[count + outs : 2 * count + outs], refs[2 * count + outs :]
+    load, save, inner, refs_left = refs_left[0], refs_left[1], refs_left[2 : 1 + outs], refs_left[1 + outs :]
+    inner = list(inner[:3]) + [results[3]] + list(inner[3:])
+    saves = [
+        None if n == 3 else pltpu.make_async_copy(a, b, save.at[n])
+        for n, (a, b) in enumerate(zip(inner, results))
+    ]
     copies = [
         pltpu.make_async_copy(a, b, load.at[n]) for n, (a, b) in enumerate(zip(refs[:count], held))
     ]
     for copy in copies[2:] + copies[:2]:
         copy.start()
-    forward_body(
-        shape, copies, *held, *refs[count : count + outs], *refs[2 * count + outs + 1 :]
-    )
+    forward_body(shape, copies, saves, *held, *inner, *refs_left)
+    for copy in saves:
+        if copy is not None:
+            copy.wait()
 
 
 def forward_body(
-    shape, copies, tokens, weights, proj_bias, gain2, shift2, fc2_bias, gain1, shift1, fc1_bias,
+    shape, copies, saves, tokens, weights, proj_bias, gain2, shift2, fc2_bias, gain1, shift1, fc1_bias,
     qv_bias, threshold, rows_t, cols_t,
     att, qaug, bias_rows, kv_out, o_out, lse_out, peak_out, n1_out, tables, vectors,
     n1, qkv, wide_t, rq, rkv, kaug_t, kaug, vaug, oacc, mrow, lpk, att_s, att_r,
@@ -199,10 +206,13 @@
         for at in range(pieces):
             start = (dev * pieces + at) * piece
             n1_out[at, dev] = n1_t[start : start + piece]
+    saves[7].start()
     wide_t[...] = jnp.zeros_like(wide_t)
     for n, held in enumerate((rows_t, cols_t)):
         wide_t[n, :HEAD, : held.shape[1]] = held[...]
         tables[n] = nn(wide_t[n], turned(2 * SIDE)).T[:, :HEAD].astype(LOW)
+    saves[8].start()
+    saves[9].start()
     qaug[pl.ds(LSE_AT, 16), :] = jnp.zeros((16, shape.queries), LOW)
     kaug_t[pl.ds(LSE_AT, 16), :] = jnp.zeros((16, rows), LOW)
     vaug[pl.ds(HEAD, 16), :] = jnp.where(
@@ -234,6 +244,7 @@
         return carry
 
     lax.fori_loop(0, heads, prepare, 0)
+    saves[2].start()
 
     def chunk(source, mate):
         dev = source * group + mate
@@ -274,6 +285,15 @@
 
         chunk(source, g)
 
+        @pl.when(k != 1)
+        def _():
+            mates_of(jnp.maximum(k - 1, 0))
+
+        return carry
+
+    def mates_of(k):
+        source = paired(z, k, heads)
+
         def mate_step(n, inner):
             mate = lax.rem(g + n, group)
             send_dp(
@@ -283,9 +303,10 @@
             return inner
 
         lax.fori_loop(1, group, mate_step, 0)
-        return carry
 
     lax.fori_loop(0, heads, column_step, 0)
+    if heads > 1:
+        mates_of(heads - 1)
     keep_kv = pltpu.make_async_copy(rkv, kv_out, o_sem)
     keep_kv.start()
 
@@ -306,12 +327,17 @@
 
         return carry
 
+    saves[1].start()
     lax.fori_loop(1, heads + 1, finish, 0)
+    saves[4].start()
+    saves[5].start()
     att[z] = att_s[z]
     peak_out[...] = jnp.full(peak_out.shape, jnp.max(lpk[...]) * SCALE, F32)
+    saves[6].start()
     for h in column:
         send_dp(att_s.at[h], att_r.at[h], r_send.at[h], r_recv.at[h], h * group + g).wait()
         att[h] = att_r[h]
+    saves[0].start()
     for copy in sends:
         copy.wait_send()
     for source in range(heads):
@@ -333,25 +359,28 @@
     vmem = pl.BlockSpec(memory_space=pltpu.VMEM)
     hbm = pl.BlockSpec(memory_space=pl.ANY)
     dma = pltpu.SemaphoreType.DMA
+    outs = (
+        jax.ShapeDtypeStruct((heads, HEAD, rows), LOW),
+        jax.ShapeDtypeStruct((AUG, queries), LOW),
+        jax.ShapeDtypeStruct((SIDE // 8, 16, queries), LOW),
+        jax.ShapeDtypeStruct((heads, group, 2, HEAD, rows), LOW),
+        jax.ShapeDtypeStruct((HEAD, queries), F32),
+        jax.ShapeDtypeStruct((1, queries), F32),
+        jax.ShapeDtypeStruct((8, 128), F32),
+        jax.ShapeDtypeStruct((owned // piece, devices, piece, rows), LOW),
+        jax.ShapeDtypeStruct((2, 2 * SIDE, HEAD), LOW),
+        jax.ShapeDtypeStruct((16, width), F32),
+    )
     return pl.pallas_call(
-        functools.partial(forward_kernel, shape, len(args), 10),
-        out_shape=(
-            jax.ShapeDtypeStruct((heads, HEAD, rows), LOW),
-            jax.ShapeDtypeStruct((AUG, queries), LOW),
-            jax.ShapeDtypeStruct((SIDE // 8, 16, queries), LOW),
-            jax.ShapeDtypeStruct((heads, group, 2, HEAD, rows), LOW),
-            jax.ShapeDtypeStruct((HEAD, queries), F32),
-            jax.ShapeDtypeStruct((1, queries), F32),
-            jax.ShapeDtypeStruct((8, 128), F32),
-            jax.ShapeDtypeStruct((owned // piece, devices, piece, rows), LOW),
-            jax.ShapeDtypeStruct((2, 2 * SIDE, HEAD), LOW),
-            jax.ShapeDtypeStruct((16, width), F32),
-        ),
+        functools.partial(forward_kernel, shape, len(args), len(outs)),
+        out_shape=outs,
         in_specs=[pl.BlockSpec(memory_space=pltpu.HBM)] * len(args),
-        out_specs=(vmem, vmem, vmem, hbm, vmem, vmem, vmem, vmem, vmem, vmem),
+        out_specs=(hbm,) * len(outs),
         scratch_shapes=[
             *[pltpu.VMEM(each.shape, each.dtype) for each in args],
             dma((len(args),)),
+            dma((len(outs),)),
+            *[pltpu.VMEM(each.shape, each.dtype) for n, each in enumerate(outs) if n != 3],
             pltpu.VMEM((rows, width), LOW),
             pltpu.VMEM((3, local, rows), LOW),
             pltpu.VMEM((2, 128, 2 * SIDE), LOW),
@@ -378,7 +407,7 @@
 
 def backward_kernel(
     shape, ga, tables, qaug_in, bias_rows, rkv, o_in, lse_in, fc2_state, fc1, mlp, values, vectors, proj,
-    grads, table_grads, fc1_out, fc2_out, fc1_state, output, proj_state,
+    grads, table_grads, first_state, fc2_out, fc1_state, output, proj_state,
     rdo, qaug, q_tok, do_aug, do_tok, kaug_t, kaug, vaug_t, vaug, kacc, vacc, dq, drow, dcol,
     part, xr, summed, gq_s, gq_r, gkv_r,
     d_send, d_recv, x_send, x_recv, kv_send, kv_recv, q_send, q_recv, *rest,
@@ -390,7 +419,6 @@
         found, rest[:] = rest[:number], rest[number:]
         return found
 
-    whole_bufs = 2 + 3 * halve_bits()
     bits = halve_bits()
     orders = [near_first(), far_first(shape.group)]
     moved2 = [
@@ -402,7 +430,7 @@
     sum_mlp = Reduce(mlp, *taken(7))
     all_out = Gather(outs, *taken(3))
     line = tensor_place()[1]
-    moved1 = [Halve(near_first(), fc1.at[:, 0], taken(whole_bufs), own=True)]
+    moved1 = [Halve(near_first(), fc1.at[:, 0], taken(8), last=1, own=True)]
     if chunks > 1:
         moved1 += [Halve(near_first(), fc1.at[:, 1], taken(5), last=0, own=True)]
     heads, group, rows, block = shape.heads, shape.group, shape.rows, shape.block
@@ -420,8 +448,6 @@
         copy.start()
         sends.append(copy)
     moved1[0].start()
-    for each in moved2:
-        each.start()
     for each in moved1:
         each.load()
     rdo[z] = ga[z]
@@ -462,6 +488,8 @@
     for other in sum_mlp.others():
         sum_mlp.pass_on(other)
     moved0.start()
+    for each in moved2:
+        each.start()
 
     def chunk(source, mate):
         dev = source * group + mate
@@ -581,11 +609,11 @@
     lax.fori_loop(1, heads + 1, finish, 0)
     moved1[0].run(1)
     for stage in range(2, halve_bits() - 1):
-        for each in moved2 + moved1[:1]:
+        for each in moved2:
             each.run(stage)
     found = [each.total() for each in moved2]
     fc2_out[...] = jnp.concatenate(found, axis=0) if chunks > 1 else found[0]
-    fc1_out[...] = moved1[0].total()
+    first_state[...] = moved1[0].stages[1][0][...]
     if chunks > 1:
         moved1[1].loaded()
         moved1[1].run(0)
@@ -620,7 +648,7 @@
     moving += halve_bufs(chunks * owned, proj.shape[2], last=0)
     moving += [pltpu.VMEM((count, share, width), LOW)]
     moving += part_bufs(count // 2, share, width) + gather_sems(count // 2)
-    moving += halve_bufs(owned, hidden, own=True)
+    moving += halve_bufs(owned, hidden, last=1, own=True)
     if chunks > 1:
         moving += halve_bufs(owned, hidden, last=0, own=True)
     heads, group, rows, queries = shape.heads, shape.group, shape.rows, shape.queries
@@ -631,7 +659,7 @@
         out_shape=(
             jax.ShapeDtypeStruct((heads, 3, HEAD, rows), LOW),
             jax.ShapeDtypeStruct((2, 2 * SIDE, 128), F32),
-            jax.ShapeDtypeStruct((owned, hidden), F32),
+            jax.ShapeDtypeStruct((devices // 4, owned, hidden), LOW),
             jax.ShapeDtypeStruct((chunks * owned, hidden), F32),
             jax.ShapeDtypeStruct((devices // 2, owned, hidden), LOW),
             jax.ShapeDtypeStruct((count, share, width), LOW),
@@ -1252,7 +1280,7 @@
 
 def tail_kernel(
     heads, grads, qkv_w, n1_t, tokens, grad_middle, vectors, tables, sums, fc1_bias, peak,
-    proj, fc1_half, fc1_state,
+    proj, first_state, fc1_state,
     tokens_out, proj_out, fc1_out, qkv_out, tables_out, rows_out, clip_out,
     g_all, g_tok, part, gt, *rest,
 ):
@@ -1275,9 +1303,9 @@
     blocks = [taken(1)[0] for _ in range(pieces)]
     moved3 = [Halve(near_first(), each, taken(3 * halve_bits())) for each in blocks]
     moved0 = Halve(far_first(ring.group), proj, taken(3 * (halve_bits() - 1)), first=1)
-    moved1 = []
+    moved1 = [Halve(near_first(), first_state, taken(3 * (halve_bits() - 2)), first=2)]
     if chunks > 1:
-        moved1 = [Halve(near_first(), fc1_state, taken(3 * (halve_bits() - 1)), first=1)]
+        moved1 += [Halve(near_first(), fc1_state, taken(3 * (halve_bits() - 1)), first=1)]
     sum_part = Reduce(part, *taken(7))
     all_gt = Gather(gt, *taken(3))
     pool, pooled = taken(2)
@@ -1334,7 +1362,7 @@
     scaled, inverse = normed(tokens[me].astype(F32))
     small_pool.step(0)
     moved0.run(1)
-    for each in moved1:
+    for each in moved1[1:]:
         each.run(1)
     moved3[0].run(0)
     for each in moved3[1:2]:
@@ -1408,10 +1436,9 @@
     late = small_late.take(3)
     row = lax.broadcasted_iota(jnp.int32, late.shape, 0)
     rows_out[0:8] = jnp.where((row == 2) | (row == 3), late * (1.0 / count), late)
-    owned = fc1_half.shape[0]
-    fc1_out[0:owned] = fc1_half[...]
-    for each in moved1:
-        fc1_out[pl.ds(owned, owned), :] = each.total()
+    owned = first_state.shape[1]
+    for n, each in enumerate(moved1):
+        fc1_out[pl.ds(n * owned, owned), :] = each.total()
     proj_out[...] = moved0.total()
     for n, each in enumerate(moved3):
         total = each.total()
@@ -1424,14 +1451,14 @@
         each.finish()
 
 
-def tail(heads, grads, qkv_w, n1_t, tokens, grad_middle, vectors, tables, sums, fc1_bias, peak, proj, fc1_half, fc1_state):
-    hidden = fc1_half.shape[1]
+def tail(heads, grads, qkv_w, n1_t, tokens, grad_middle, vectors, tables, sums, fc1_bias, peak, proj, first_state, fc1_state):
+    hidden = first_state.shape[2]
     count = lax.axis_size("tensor")
     lines = count // 2
     local = heads * HEAD
     pieces, devices, piece, rows = n1_t.shape
     width = devices * pieces * piece
-    owned = fc1_half.shape[0]
+    owned = first_state.shape[1]
     chunks = pieces * piece // owned
     share = rows // count
     vmem = pl.BlockSpec(memory_space=pltpu.VMEM)
@@ -1445,6 +1472,7 @@
     scratch += [pltpu.VMEM((devices, piece, 3 * local), LOW)] * pieces
     scratch += halve_bufs(piece, 3 * local) * pieces
     scratch += halve_bufs(chunks * owned, local, first=1)
+    scratch += halve_bufs(owned, hidden, first=2)
     if chunks > 1:
         scratch += halve_bufs(owned, hidden, first=1)
     scratch += part_bufs(lines, share, width) + gather_sems(lines)
@@ -1474,14 +1502,14 @@
         name="tail",
     )(
         grads, qkv_w, n1_t, tokens.reshape(whole), grad_middle, vectors, tables, sums, fc1_bias,
-        peak, proj, fc1_half, fc1_state,
+        peak, proj, first_state, fc1_state,
     )
 
 
 def finish_kernel(count, *refs):
     large, (rows, tables), refs = refs[:count], refs[count : count + 2], refs[count + 2 :]
-    outs, smalls, stage = refs[:count], refs[count : count + 13], refs[count + 13 :]
-    sems_in, sems_out = stage[count], stage[count + 1]
+    outs, smalls_out, refs = refs[:count], refs[count : count + 13], refs[count + 13 :]
+    stage, smalls, (sems_in, sems_out, sems_small) = refs[:count], refs[count : count + 13], refs[count + 13 :]
     into = [pltpu.make_async_copy(a, b, sems_in.at[n]) for n, (a, b) in enumerate(zip(large, stage))]
     out = [pltpu.make_async_copy(b, c, sems_out.at[n]) for n, (b, c) in enumerate(zip(stage, outs))]
     for copy in into:
@@ -1498,10 +1526,15 @@
     qv[1:2] = rows[9:10, 2 * local : 3 * local]
     by_row[...] = tables[0, :, : by_row.shape[1]]
     by_col[...] = tables[1, :, : by_col.shape[1]]
+    small = [
+        pltpu.make_async_copy(a, b, sems_small.at[n]) for n, (a, b) in enumerate(zip(smalls, smalls_out))
+    ]
     for copy, after in zip(into, out):
         copy.wait()
         after.start()
-    for copy in out:
+    for copy in small:
+        copy.start()
+    for copy in out + small:
         copy.wait()
 
 
@@ -1520,9 +1553,11 @@
         out_shape=[jax.ShapeDtypeStruct(each.shape, each.dtype) for each in large]
         + [jax.ShapeDtypeStruct(each, F32) for each in shapes],
         in_specs=[hbm] * count + [vmem] * 2,
-        out_specs=[hbm] * count + [vmem] * len(shapes),
+        out_specs=[hbm] * (count + len(shapes)),
         scratch_shapes=[pltpu.VMEM(each.shape, each.dtype) for each in large]
-        + [pltpu.SemaphoreType.DMA((count,))] * 2,
+        + [pltpu.VMEM(each, F32) for each in shapes]
+        + [pltpu.SemaphoreType.DMA((count,))] * 2
+        + [pltpu.SemaphoreType.DMA((len(shapes),))],
         compiler_params=pltpu.CompilerParams(vmem_limit_bytes=VMEM_LIMIT["finish"]),
         name="finish",
     )(*large, rows, tables)
@@ -1583,7 +1618,7 @@
         vectors,
     )
     grad_heads = grad_attended.reshape(local_heads, HEAD, row_count)
-    grad_triple, table_terms, fc1_half, grad_fc2, fc1_state, output, proj_state = attend_back(
+    grad_triple, table_terms, first_state, grad_fc2, fc1_state, output, proj_state = attend_back(
         shape, grad_heads, tables, qaug, bias_rows, kv, o_rows, lse, fc2_state, grad_fc1,
         mlp_part, values, vectors, grad_proj,
     )
@@ -1600,7 +1635,7 @@
         grad_fc1_bias,
         peak,
         proj_state,
-        fc1_half,
+        first_state,
         fc1_state,
     )
     large = (output, grad_tokens, grad_fc1, grad_fc2, grad_qkv, clipped, grad_proj)

time: 243 us -> 229 us (0.942)
  Pallas kernels: 240 us -> 225 us
    pallas_call x1, Pallas kernels: 64 us -> 56.4 us  [attend_back(): pl.pallas_call(functools.partial(backward_kernel, shape), out_shape=(jax....]
    pallas_call x1, Pallas kernels: 52.3 us -> 45.7 us  [attend(): pl.pallas_call(functools.partial(forward_kernel, shape, len(args), len(ou...]
where the time goes in v6:
time: 229 us; the launch traced here: 228 us
  Pallas kernels  225 us (98%)
    pallas_call x1, Pallas kernels, middle_block(): pl.pallas_call(functools.partial(middle_kernel, heads), out_shape=(jax.Sh...  62.3 us
    pallas_call x1, Pallas kernels, attend_back(): pl.pallas_call(functools.partial(backward_kernel, shape), out_shape=(jax....  56.4 us
    pallas_call x1, Pallas kernels, tail(): pl.pallas_call(functools.partial(tail_kernel, heads), out_shape=(jax.Shap...  55.8 us
    pallas_call x1, Pallas kernels, attend(): pl.pallas_call(functools.partial(forward_kernel, shape, len(args), len(ou...  45.7 us

profile of v6, /device:TPU:0, one launch (start us, length us, event | category | flops | bytes accessed | tf_op | source)
XLA Modules:
  0.0 228.3 jit_solution(14834240232362701808)
XLA Ops:
  1.3 0.0 copy-start
  1.3 0.0 copy-start.2
  1.3 0.0 copy-start.6
  1.3 45.7 %attend.1 = (bf16[4,80,512]{2,1,0:T(8,128)(2,1)}, bf16[240,2048]{1,0:T(8,128)(2,1)}, bf16[8,16,2048]{2,1,0:T(8,128)(2,1)}, bf16[4,2,2,80,512]{4,3,2,1,0:T(8,128)...) custom-call(bf16[512,1280]{1,0:T(8,128)(2,1)} %bitcast.20, ...), custom_call_target="tpu_custom_call" | custom-call | tf_op jit(solution)/shard_map/attend/pallas_call | solution.py:374
  47.0 0.0 copy-done
  47.0 0.0 copy-done.2
  47.0 0.0 copy-done.6
  47.1 0.0 copy-start.7
  47.1 0.9 copy-done.7
  47.9 1.0 copy-done.11
  48.9 0.0 copy-start.10
  48.9 0.0 copy-start.12
  48.9 0.0 copy-start.13
  49.0 62.3 %middle.1 = (bf16[4,128,1280]{2,1,0:T(8,128)(2,1)S(1)}, f32[128,1280]{1,0:T(8,128)S(1)}, f32[128,1280]{1,0:T(8,128)S(1)}, bf16[8,2,80,1280]{3,2,1,0:T(8,128)(2,1...) custom-call(bf16[320,512]{1,0:T(8,128)(2,1)S(1)} %bitcast.27, ...), custom_call_target="tpu_custom_call" | custom-call | tf_op jit(solution)/shard_map/middle/pallas_call | solution.py:1188
  111.3 0.0 copy-done.4
  111.3 0.0 copy-done.5
  111.3 0.0 copy-done.8
  111.4 0.0 copy-start.1
  111.4 56.4 %attend_back.1 = (bf16[4,3,80,512]{3,2,1,0:T(8,128)(2,1)S(1)}, f32[2,128,128]{2,1,0:T(8,128)S(1)}, bf16[2,80,1280]{2,1,0:T(8,128)(2,1)S(1)}, f32[160,1280]{1,0:T...) custom-call(bf16[4,80,512]{2,1,0:T(8,128)(2,1)S(1)} %bitcast.26, ...), custom_call_target="tpu_custom_call" | custom-call | tf_op jit(solution)/shard_map/attend_back/pallas_call | solution.py:657
  167.8 0.0 copy-done.1
  167.8 0.0 copy-done.3
  167.8 0.0 copy-done.14
  167.8 55.8 %tail.1 = (bf16[4,128,1280]{2,1,0:T(8,128)(2,1)S(1)}, f32[160,320]{1,0:T(8,128)S(1)}, f32[160,1280]{1,0:T(8,128)S(1)}, f32[3,160,320]{2,1,0:T(8,128)S(1)}, f32[2...) custom-call(bf16[4,3,80,512]{3,2,1,0:T(8,128)(2,1)S(1)} %get-tuple-element.88.grads, ...), custom_call_target="tpu_custom_call" | custom-call | tf_op jit(solution)/shard_map/tail/pallas_call | solution.py:1485
  223.6 4.5 %finish.1 = (bf16[4,128,1280]{2,1,0:T(8,128)(2,1)}, bf16[4,128,1280]{2,1,0:T(8,128)(2,1)}, f32[160,1280]{1,0:T(8,128)}, f32[160,1280]{1,0:T(8,128)}, f32[3,160,3...) custom-call(bf16[4,128,1280]{2,1,0:T(8,128)(2,1)S(1)} %get-tuple-ele, ...), custom_call_target="tpu_custom_call" | custom-call | tf_op jit(solution)/shard_map/finish/pallas_call | solution.py:1551
  (11 shorter events, 0.0 us)
Async XLA Ops:
  1.3 45.7 %copy-start = (bf16[1,512,1280]{2,1,0:T(8,128)(2,1)S(1)}, bf16[1,512,1280]{2,1,0:T(8,128)(2,1)}, u32[]{:S(2)}) copy-start(bf16[1,512,1280]{2,1,0:T(8,128)(2,1)} %param.17) | copy-start | bytes 3932164
  1.3 45.7 %copy-start.2 = (bf16[1,512,1280]{2,1,0:T(8,128)(2,1)S(1)}, bf16[1,512,1280]{2,1,0:T(8,128)(2,1)}, u32[]{:S(2)}) copy-start(bf16[1,512,1280]{2,1,0:T(8,128)(2,1)} %param.18) | copy-start | bytes 3932164
  1.3 45.7 %copy-start.6 = (bf16[320,1280]{1,0:T(8,128)(2,1)S(1)}, bf16[320,1280]{1,0:T(8,128)(2,1)}, u32[]{:S(2)}) copy-start(bf16[320,1280]{1,0:T(8,128)(2,1)} %proj_w.1) | copy-start | bytes 2457604
  47.1 0.9 copy-start.7
  47.9 1.0 copy-start.11
  48.9 62.4 %copy-start.4 = (bf16[4,2,2,80,512]{4,3,2,1,0:T(8,128)(2,1)S(1)}, bf16[4,2,2,80,512]{4,3,2,1,0:T(8,128)(2,1)}, u32[]{:S(2)}) copy-start(bf16[4,2,2,80,512]{4,3,2,1,0:T(8,128)(2,1)} %get-tuple-element.79.rkv) | copy-start | bytes 3932164
  48.9 62.4 %copy-start.5 = (bf16[240,2048]{1,0:T(8,128)(2,1)S(1)}, bf16[240,2048]{1,0:T(8,128)(2,1)}, u32[]{:S(2)}) copy-start(bf16[240,2048]{1,0:T(8,128)(2,1)} %get-tuple-element.77.qaug_in) | copy-start | bytes 2949124
  48.9 62.4 %copy-start.8 = (f32[16,1280]{1,0:T(8,128)S(1)}, f32[16,1280]{1,0:T(8,128)}, u32[]{:S(2)}) copy-start(f32[16,1280]{1,0:T(8,128)} %get-tuple-element.74.vectors) | copy-start | bytes 245764
  48.9 62.4 %copy-start.9 = (f32[80,2048]{1,0:T(8,128)S(1)}, f32[80,2048]{1,0:T(8,128)}, u32[]{:S(2)}) copy-start(f32[80,2048]{1,0:T(8,128)} %get-tuple-element.80.o_in) | copy-start | bytes 1966084
  48.9 62.4 %copy-start.10 = (bf16[8,16,2048]{2,1,0:T(8,128)(2,1)S(1)}, bf16[8,16,2048]{2,1,0:T(8,128)(2,1)}, u32[]{:S(2)}) copy-start(bf16[8,16,2048]{2,1,0:T(8,128)(2,1)} %get-tuple-element.78.bias_rows) | copy-start | bytes 1572868
  48.9 62.4 %copy-start.12 = (bf16[2,128,80]{2,1,0:T(8,128)(2,1)S(1)}, bf16[2,128,80]{2,1,0:T(8,128)(2,1)}, u32[]{:S(2)}) copy-start(bf16[2,128,80]{2,1,0:T(8,128)(2,1)} %get-tuple-element.76.tables) | copy-start | bytes 122884
  48.9 62.4 %copy-start.13 = (f32[1,2048]{1,0:T(1,128)S(1)}, f32[1,2048]{1,0:T(1,128)}, u32[]{:S(2)}) copy-start(f32[1,2048]{1,0:T(1,128)} %get-tuple-element.81.lse_in) | copy-start | bytes 24580
  111.4 56.4 %copy-start.1 = (bf16[1280,3,320]{0,2,1:T(8,128)(2,1)S(1)}, bf16[1280,3,320]{0,2,1:T(8,128)(2,1)}, u32[]{:S(2)}) copy-start(bf16[1280,3,320]{0,2,1:T(8,128)(2,1)} %param.21) | copy-start | bytes 7372804
  111.4 56.4 %copy-start.3 = (bf16[5,8,32,512]{3,2,1,0:T(8,128)(2,1)S(1)}, bf16[5,8,32,512]{3,2,1,0:T(8,128)(2,1)}, u32[]{:S(2)}) copy-start(bf16[5,8,32,512]{3,2,1,0:T(8,128)(2,1)} %get-tuple-element.89.n1_t) | copy-start | bytes 3932164
  111.4 56.4 %copy-start.14 = (f32[8,128]{1,0:T(8,128)S(1)}, f32[8,128]{1,0:T(8,128)}, u32[]{:S(2)}) copy-start(f32[8,128]{1,0:T(8,128)} %get-tuple-element.94.peak) | copy-start | bytes 12292

commit v7 on v6

--- a/solution.py
+++ b/solution.py
@@ -1360,11 +1360,11 @@
     for other in sum_part.others():
         sum_part.pass_on(other)
     scaled, inverse = normed(tokens[me].astype(F32))
-    small_pool.step(0)
-    moved0.run(1)
     for each in moved1[1:]:
         each.run(1)
     moved3[0].run(0)
+    small_pool.step(0)
+    moved0.run(1)
     for each in moved3[1:2]:
         each.run(0)
     moved3[0].run(1)
@@ -1401,6 +1401,8 @@
         for other in all_pool.others():
             all_pool.forward(other)
     small_late.step(2)
+    if pieces > 1:
+        moved3[-1].run(1)
     dp_sum = small_dp.take(1)
     limit = vectors[9:10]
     factors = jnp.sqrt(limit / jnp.maximum(dp_sum[2:3], limit))
@@ -1417,8 +1419,6 @@
     rows_out[11:12] = factors
     rows_out[12:13] = clipped_bias
     rows_out[13:16] = jnp.zeros((3, width), F32)
-    if pieces > 1:
-        moved3[-1].run(1)
     for stage in range(2, halve_bits() - 1):
         for each in moved3 + [moved0] + moved1:
             each.run(stage)

time: 229 us -> 227 us (level)
  no operation moved by 1% of the time
where the time goes in v7:
time: 227 us
  Pallas kernels  223 us (98%)
    pallas_call x1, Pallas kernels, middle_block(): pl.pallas_call(functools.partial(middle_kernel, heads), out_shape=(jax.Sh...  62.3 us
    pallas_call x1, Pallas kernels, attend_back(): pl.pallas_call(functools.partial(backward_kernel, shape), out_shape=(jax....  56.4 us
    pallas_call x1, Pallas kernels, tail(): pl.pallas_call(functools.partial(tail_kernel, heads), out_shape=(jax.Shap...  54.1 us
    pallas_call x1, Pallas kernels, attend(): pl.pallas_call(functools.partial(forward_kernel, shape, len(args), len(ou...  45.7 us

profile of v7, /device:TPU:0, one launch (start us, length us, event | category | flops | bytes accessed | tf_op | source)
XLA Modules:
  0.0 226.6 jit_solution(9529583447873104020)
XLA Ops:
  1.3 0.0 copy-start
  1.3 0.0 copy-start.2
  1.3 0.0 copy-start.6
  1.3 45.7 %attend.1 = (bf16[4,80,512]{2,1,0:T(8,128)(2,1)}, bf16[240,2048]{1,0:T(8,128)(2,1)}, bf16[8,16,2048]{2,1,0:T(8,128)(2,1)}, bf16[4,2,2,80,512]{4,3,2,1,0:T(8,128)...) custom-call(bf16[512,1280]{1,0:T(8,128)(2,1)} %bitcast.20, ...), custom_call_target="tpu_custom_call" | custom-call | tf_op jit(solution)/shard_map/attend/pallas_call | solution.py:374
  47.0 0.0 copy-done
  47.0 0.0 copy-done.2
  47.0 0.0 copy-done.6
  47.1 0.0 copy-start.7
  47.1 0.9 copy-done.7
  47.9 1.0 copy-done.11
  48.9 0.0 copy-start.10
  48.9 0.0 copy-start.12
  48.9 0.0 copy-start.13
  49.0 62.3 %middle.1 = (bf16[4,128,1280]{2,1,0:T(8,128)(2,1)S(1)}, f32[128,1280]{1,0:T(8,128)S(1)}, f32[128,1280]{1,0:T(8,128)S(1)}, bf16[8,2,80,1280]{3,2,1,0:T(8,128)(2,1...) custom-call(bf16[320,512]{1,0:T(8,128)(2,1)S(1)} %bitcast.27, ...), custom_call_target="tpu_custom_call" | custom-call | tf_op jit(solution)/shard_map/middle/pallas_call | solution.py:1188
  111.3 0.0 copy-done.4
  111.3 0.0 copy-done.5
  111.3 0.0 copy-done.8
  111.4 0.0 copy-start.1
  111.4 56.4 %attend_back.1 = (bf16[4,3,80,512]{3,2,1,0:T(8,128)(2,1)S(1)}, f32[2,128,128]{2,1,0:T(8,128)S(1)}, bf16[2,80,1280]{2,1,0:T(8,128)(2,1)S(1)}, f32[160,1280]{1,0:T...) custom-call(bf16[4,80,512]{2,1,0:T(8,128)(2,1)S(1)} %bitcast.26, ...), custom_call_target="tpu_custom_call" | custom-call | tf_op jit(solution)/shard_map/attend_back/pallas_call | solution.py:657
  167.8 0.0 copy-done.1
  167.8 0.0 copy-done.3
  167.8 0.0 copy-done.14
  167.8 54.1 %tail.1 = (bf16[4,128,1280]{2,1,0:T(8,128)(2,1)S(1)}, f32[160,320]{1,0:T(8,128)S(1)}, f32[160,1280]{1,0:T(8,128)S(1)}, f32[3,160,320]{2,1,0:T(8,128)S(1)}, f32[2...) custom-call(bf16[4,3,80,512]{3,2,1,0:T(8,128)(2,1)S(1)} %get-tuple-element.88.grads, ...), custom_call_target="tpu_custom_call" | custom-call | tf_op jit(solution)/shard_map/tail/pallas_call | solution.py:1485
  221.9 4.5 %finish.1 = (bf16[4,128,1280]{2,1,0:T(8,128)(2,1)}, bf16[4,128,1280]{2,1,0:T(8,128)(2,1)}, f32[160,1280]{1,0:T(8,128)}, f32[160,1280]{1,0:T(8,128)}, f32[3,160,3...) custom-call(bf16[4,128,1280]{2,1,0:T(8,128)(2,1)S(1)} %get-tuple-ele, ...), custom_call_target="tpu_custom_call" | custom-call | tf_op jit(solution)/shard_map/finish/pallas_call | solution.py:1551
  (11 shorter events, 0.0 us)
Async XLA Ops:
  1.3 45.7 %copy-start = (bf16[1,512,1280]{2,1,0:T(8,128)(2,1)S(1)}, bf16[1,512,1280]{2,1,0:T(8,128)(2,1)}, u32[]{:S(2)}) copy-start(bf16[1,512,1280]{2,1,0:T(8,128)(2,1)} %param.17) | copy-start | bytes 3932164
  1.3 45.7 %copy-start.2 = (bf16[1,512,1280]{2,1,0:T(8,128)(2,1)S(1)}, bf16[1,512,1280]{2,1,0:T(8,128)(2,1)}, u32[]{:S(2)}) copy-start(bf16[1,512,1280]{2,1,0:T(8,128)(2,1)} %param.18) | copy-start | bytes 3932164
  1.3 45.7 %copy-start.6 = (bf16[320,1280]{1,0:T(8,128)(2,1)S(1)}, bf16[320,1280]{1,0:T(8,128)(2,1)}, u32[]{:S(2)}) copy-start(bf16[320,1280]{1,0:T(8,128)(2,1)} %proj_w.1) | copy-start | bytes 2457604
  47.1 0.9 copy-start.7
  47.9 1.0 copy-start.11
  48.9 62.4 %copy-start.4 = (bf16[4,2,2,80,512]{4,3,2,1,0:T(8,128)(2,1)S(1)}, bf16[4,2,2,80,512]{4,3,2,1,0:T(8,128)(2,1)}, u32[]{:S(2)}) copy-start(bf16[4,2,2,80,512]{4,3,2,1,0:T(8,128)(2,1)} %get-tuple-element.79.rkv) | copy-start | bytes 3932164
  48.9 62.4 %copy-start.5 = (bf16[240,2048]{1,0:T(8,128)(2,1)S(1)}, bf16[240,2048]{1,0:T(8,128)(2,1)}, u32[]{:S(2)}) copy-start(bf16[240,2048]{1,0:T(8,128)(2,1)} %get-tuple-element.77.qaug_in) | copy-start | bytes 2949124
  48.9 62.4 %copy-start.8 = (f32[16,1280]{1,0:T(8,128)S(1)}, f32[16,1280]{1,0:T(8,128)}, u32[]{:S(2)}) copy-start(f32[16,1280]{1,0:T(8,128)} %get-tuple-element.74.vectors) | copy-start | bytes 245764
  48.9 62.4 %copy-start.9 = (f32[80,2048]{1,0:T(8,128)S(1)}, f32[80,2048]{1,0:T(8,128)}, u32[]{:S(2)}) copy-start(f32[80,2048]{1,0:T(8,128)} %get-tuple-element.80.o_in) | copy-start | bytes 1966084
  48.9 62.4 %copy-start.10 = (bf16[8,16,2048]{2,1,0:T(8,128)(2,1)S(1)}, bf16[8,16,2048]{2,1,0:T(8,128)(2,1)}, u32[]{:S(2)}) copy-start(bf16[8,16,2048]{2,1,0:T(8,128)(2,1)} %get-tuple-element.78.bias_rows) | copy-start | bytes 1572868
  48.9 62.4 %copy-start.12 = (bf16[2,128,80]{2,1,0:T(8,128)(2,1)S(1)}, bf16[2,128,80]{2,1,0:T(8,128)(2,1)}, u32[]{:S(2)}) copy-start(bf16[2,128,80]{2,1,0:T(8,128)(2,1)} %get-tuple-element.76.tables) | copy-start | bytes 122884
  48.9 62.4 %copy-start.13 = (f32[1,2048]{1,0:T(1,128)S(1)}, f32[1,2048]{1,0:T(1,128)}, u32[]{:S(2)}) copy-start(f32[1,2048]{1,0:T(1,128)} %get-tuple-element.81.lse_in) | copy-start | bytes 24580
  111.4 56.4 %copy-start.1 = (bf16[1280,3,320]{0,2,1:T(8,128)(2,1)S(1)}, bf16[1280,3,320]{0,2,1:T(8,128)(2,1)}, u32[]{:S(2)}) copy-start(bf16[1280,3,320]{0,2,1:T(8,128)(2,1)} %param.21) | copy-start | bytes 7372804
  111.4 56.4 %copy-start.3 = (bf16[5,8,32,512]{3,2,1,0:T(8,128)(2,1)S(1)}, bf16[5,8,32,512]{3,2,1,0:T(8,128)(2,1)}, u32[]{:S(2)}) copy-start(bf16[5,8,32,512]{3,2,1,0:T(8,128)(2,1)} %get-tuple-element.89.n1_t) | copy-start | bytes 3932164
  111.4 56.4 %copy-start.14 = (f32[8,128]{1,0:T(8,128)S(1)}, f32[8,128]{1,0:T(8,128)}, u32[]{:S(2)}) copy-start(f32[8,128]{1,0:T(8,128)} %get-tuple-element.94.peak) | copy-start | bytes 12292

commit v8 on v7

--- a/solution.py
+++ b/solution.py
@@ -1319,7 +1319,6 @@
         sum_pool.give(other)
     for each in moved1:
         each.start()
-    moved0.start()
     for t in range(3):
         for h in range(heads):
             g_all[pl.ds(t * local + h * HEAD, HEAD), :] = grads[h, t]
@@ -1341,6 +1340,8 @@
         if n == min(1, pieces - 1):
             small_pool.start(0, sum_pool.total())
         moved3[n].start()
+        if n == min(1, pieces - 1):
+            moved0.start()
 
     def norm_part(k, carry):
         at = lax.rem(line + 1 + k, lines)
@@ -1364,7 +1365,6 @@
         each.run(1)
     moved3[0].run(0)
     small_pool.step(0)
-    moved0.run(1)
     for each in moved3[1:2]:
         each.run(0)
     moved3[0].run(1)
@@ -1386,6 +1386,7 @@
         each.run(0)
         if n == 0:
             small_late.step(0)
+            moved0.run(1)
         if n == 1:
             small_late.step(1)
             for other in all_gt.others():
@@ -1393,6 +1394,8 @@
             for other in all_pool.others():
                 all_pool.forward(other)
         moved3[n + 1].run(1)
+    if pieces < 3:
+        moved0.run(1)
     if pieces < 4:
         for n in range(max(pieces - 2, 0), 2):
             small_late.step(n)

time: 227 us -> 227 us (level)
  no operation moved by 1% of the time
where the time goes in v8:
time: 227 us
  Pallas kernels  223 us (98%)
    pallas_call x1, Pallas kernels, middle_block(): pl.pallas_call(functools.partial(middle_kernel, heads), out_shape=(jax.Sh...  62.3 us
    pallas_call x1, Pallas kernels, attend_back(): pl.pallas_call(functools.partial(backward_kernel, shape), out_shape=(jax....  56.4 us
    pallas_call x1, Pallas kernels, tail(): pl.pallas_call(functools.partial(tail_kernel, heads), out_shape=(jax.Shap...  54.1 us
    pallas_call x1, Pallas kernels, attend(): pl.pallas_call(functools.partial(forward_kernel, shape, len(args), len(ou...  45.7 us

profile of v8, /device:TPU:0, one launch (start us, length us, event | category | flops | bytes accessed | tf_op | source)
XLA Modules:
  0.0 226.6 jit_solution(17771464525798969505)
XLA Ops:
  1.3 0.0 copy-start
  1.3 0.0 copy-start.2
  1.3 0.0 copy-start.6
  1.3 45.7 %attend.1 = (bf16[4,80,512]{2,1,0:T(8,128)(2,1)}, bf16[240,2048]{1,0:T(8,128)(2,1)}, bf16[8,16,2048]{2,1,0:T(8,128)(2,1)}, bf16[4,2,2,80,512]{4,3,2,1,0:T(8,128)...) custom-call(bf16[512,1280]{1,0:T(8,128)(2,1)} %bitcast.20, ...), custom_call_target="tpu_custom_call" | custom-call | tf_op jit(solution)/shard_map/attend/pallas_call | solution.py:374
  47.0 0.0 copy-done
  47.0 0.0 copy-done.2
  47.0 0.0 copy-done.6
  47.1 0.0 copy-start.7
  47.1 0.9 copy-done.7
  47.9 1.0 copy-done.11
  48.9 0.0 copy-start.10
  48.9 0.0 copy-start.12
  48.9 0.0 copy-start.13
  49.0 62.3 %middle.1 = (bf16[4,128,1280]{2,1,0:T(8,128)(2,1)S(1)}, f32[128,1280]{1,0:T(8,128)S(1)}, f32[128,1280]{1,0:T(8,128)S(1)}, bf16[8,2,80,1280]{3,2,1,0:T(8,128)(2,1...) custom-call(bf16[320,512]{1,0:T(8,128)(2,1)S(1)} %bitcast.27, ...), custom_call_target="tpu_custom_call" | custom-call | tf_op jit(solution)/shard_map/middle/pallas_call | solution.py:1188
  111.3 0.0 copy-done.4
  111.3 0.0 copy-done.5
  111.3 0.0 copy-done.8
  111.4 0.0 copy-start.1
  111.4 56.4 %attend_back.1 = (bf16[4,3,80,512]{3,2,1,0:T(8,128)(2,1)S(1)}, f32[2,128,128]{2,1,0:T(8,128)S(1)}, bf16[2,80,1280]{2,1,0:T(8,128)(2,1)S(1)}, f32[160,1280]{1,0:T...) custom-call(bf16[4,80,512]{2,1,0:T(8,128)(2,1)S(1)} %bitcast.26, ...), custom_call_target="tpu_custom_call" | custom-call | tf_op jit(solution)/shard_map/attend_back/pallas_call | solution.py:657
  167.8 0.0 copy-done.1
  167.8 0.0 copy-done.3
  167.8 0.0 copy-done.14
  167.8 54.1 %tail.1 = (bf16[4,128,1280]{2,1,0:T(8,128)(2,1)S(1)}, f32[160,320]{1,0:T(8,128)S(1)}, f32[160,1280]{1,0:T(8,128)S(1)}, f32[3,160,320]{2,1,0:T(8,128)S(1)}, f32[2...) custom-call(bf16[4,3,80,512]{3,2,1,0:T(8,128)(2,1)S(1)} %get-tuple-element.88.grads, ...), custom_call_target="tpu_custom_call" | custom-call | tf_op jit(solution)/shard_map/tail/pallas_call | solution.py:1488
  221.9 4.5 %finish.1 = (bf16[4,128,1280]{2,1,0:T(8,128)(2,1)}, bf16[4,128,1280]{2,1,0:T(8,128)(2,1)}, f32[160,1280]{1,0:T(8,128)}, f32[160,1280]{1,0:T(8,128)}, f32[3,160,3...) custom-call(bf16[4,128,1280]{2,1,0:T(8,128)(2,1)S(1)} %get-tuple-ele, ...), custom_call_target="tpu_custom_call" | custom-call | tf_op jit(solution)/shard_map/finish/pallas_call | solution.py:1554
  (11 shorter events, 0.0 us)
Async XLA Ops:
  1.3 45.7 %copy-start = (bf16[1,512,1280]{2,1,0:T(8,128)(2,1)S(1)}, bf16[1,512,1280]{2,1,0:T(8,128)(2,1)}, u32[]{:S(2)}) copy-start(bf16[1,512,1280]{2,1,0:T(8,128)(2,1)} %param.17) | copy-start | bytes 3932164
  1.3 45.7 %copy-start.2 = (bf16[1,512,1280]{2,1,0:T(8,128)(2,1)S(1)}, bf16[1,512,1280]{2,1,0:T(8,128)(2,1)}, u32[]{:S(2)}) copy-start(bf16[1,512,1280]{2,1,0:T(8,128)(2,1)} %param.18) | copy-start | bytes 3932164
  1.3 45.7 %copy-start.6 = (bf16[320,1280]{1,0:T(8,128)(2,1)S(1)}, bf16[320,1280]{1,0:T(8,128)(2,1)}, u32[]{:S(2)}) copy-start(bf16[320,1280]{1,0:T(8,128)(2,1)} %proj_w.1) | copy-start | bytes 2457604
  47.1 0.9 copy-start.7
  47.9 1.0 copy-start.11
  48.9 62.4 %copy-start.4 = (bf16[4,2,2,80,512]{4,3,2,1,0:T(8,128)(2,1)S(1)}, bf16[4,2,2,80,512]{4,3,2,1,0:T(8,128)(2,1)}, u32[]{:S(2)}) copy-start(bf16[4,2,2,80,512]{4,3,2,1,0:T(8,128)(2,1)} %get-tuple-element.79.rkv) | copy-start | bytes 3932164
  48.9 62.4 %copy-start.5 = (bf16[240,2048]{1,0:T(8,128)(2,1)S(1)}, bf16[240,2048]{1,0:T(8,128)(2,1)}, u32[]{:S(2)}) copy-start(bf16[240,2048]{1,0:T(8,128)(2,1)} %get-tuple-element.77.qaug_in) | copy-start | bytes 2949124
  48.9 62.4 %copy-start.8 = (f32[16,1280]{1,0:T(8,128)S(1)}, f32[16,1280]{1,0:T(8,128)}, u32[]{:S(2)}) copy-start(f32[16,1280]{1,0:T(8,128)} %get-tuple-element.74.vectors) | copy-start | bytes 245764
  48.9 62.4 %copy-start.9 = (f32[80,2048]{1,0:T(8,128)S(1)}, f32[80,2048]{1,0:T(8,128)}, u32[]{:S(2)}) copy-start(f32[80,2048]{1,0:T(8,128)} %get-tuple-element.80.o_in) | copy-start | bytes 1966084
  48.9 62.4 %copy-start.10 = (bf16[8,16,2048]{2,1,0:T(8,128)(2,1)S(1)}, bf16[8,16,2048]{2,1,0:T(8,128)(2,1)}, u32[]{:S(2)}) copy-start(bf16[8,16,2048]{2,1,0:T(8,128)(2,1)} %get-tuple-element.78.bias_rows) | copy-start | bytes 1572868
  48.9 62.4 %copy-start.12 = (bf16[2,128,80]{2,1,0:T(8,128)(2,1)S(1)}, bf16[2,128,80]{2,1,0:T(8,128)(2,1)}, u32[]{:S(2)}) copy-start(bf16[2,128,80]{2,1,0:T(8,128)(2,1)} %get-tuple-element.76.tables) | copy-start | bytes 122884
  48.9 62.4 %copy-start.13 = (f32[1,2048]{1,0:T(1,128)S(1)}, f32[1,2048]{1,0:T(1,128)}, u32[]{:S(2)}) copy-start(f32[1,2048]{1,0:T(1,128)} %get-tuple-element.81.lse_in) | copy-start | bytes 24580
  111.4 56.4 %copy-start.1 = (bf16[1280,3,320]{0,2,1:T(8,128)(2,1)S(1)}, bf16[1280,3,320]{0,2,1:T(8,128)(2,1)}, u32[]{:S(2)}) copy-start(bf16[1280,3,320]{0,2,1:T(8,128)(2,1)} %param.21) | copy-start | bytes 7372804
  111.4 56.4 %copy-start.3 = (bf16[5,8,32,512]{3,2,1,0:T(8,128)(2,1)S(1)}, bf16[5,8,32,512]{3,2,1,0:T(8,128)(2,1)}, u32[]{:S(2)}) copy-start(bf16[5,8,32,512]{3,2,1,0:T(8,128)(2,1)} %get-tuple-element.89.n1_t) | copy-start | bytes 3932164
  111.4 56.4 %copy-start.14 = (f32[8,128]{1,0:T(8,128)S(1)}, f32[8,128]{1,0:T(8,128)}, u32[]{:S(2)}) copy-start(f32[8,128]{1,0:T(8,128)} %get-tuple-element.94.peak) | copy-start | bytes 12292
